TPU v7x, 512 devices: a whole 4x8x8 slice. The times are simulated.
512 devices in a mesh: tm: 16 (over z, core), space: 32 (over x, y).
Axes of the slice: x: 4, y: 8, z: 8, core: 2. Of those that a mesh axis runs over, the one named last changes fastest.
Arguments:
- queries: bfloat16 [16, 4096, 1120], P('tm', 'space'), may hold values from -6 to 6
- keys_in: bfloat16 [16, 4096, 1120], P('tm', 'space'), may hold values from -30 to 30
- values_in: bfloat16 [16, 4096, 1120], P('tm', 'space'), may hold values from -10 to 10
- grad_attn: bfloat16 [16, 4096, 1120], P('tm', 'space'), may hold values from -6 to 6
Outputs:
- mixed: bfloat16 [16, 4096, 1120], P('tm', 'space')
- grad_queries: bfloat16 [16, 4096, 1120], P('tm', 'space')
- grad_keys: bfloat16 [16, 4096, 1120], P('tm', 'space')
- values_gradient: bfloat16 [16, 4096, 1120], P('tm', 'space')
All inputs are finite; a program needn't handle non-finite values.
Results may differ from a plain program's by a relative error of at most 0.001.
Values sent between devices are 32-bit elements; how exact they have to be, the bound alone decides.
No kernel may reach another device: no remote copies, remote signals or barrier semaphores. Data moves between devices by JAX's collectives and lax.ppermute only.
A program may use at most 64 MiB of HBM per device.

v0:
```python
import math

import jax
import jax.numpy as jnp
from jax import lax
from jax.sharding import PartitionSpec as P

HEAD_DIM = 112


HIGH_PRECISION = lax.Precision.HIGHEST


def split_up(shard, dim, size):
    lengths = shard.shape
    pieces = shard.reshape(*lengths[:dim], size, lengths[dim] // size, *lengths[dim + 1 :])
    return jnp.moveaxis(pieces, dim, 0)


def sent_and_summed(shard, axis, dim):
    size = lax.axis_size(axis)
    pieces = lax.all_to_all(split_up(shard, dim, size), axis, 0, 0, tiled=True)
    return jnp.sum(pieces, axis=0)


def in_one_piece(arrays, axis, dim, along):
    widths = [math.prod(a.shape[along:]) for a in arrays]
    both = jnp.concatenate(
        [a.reshape(*a.shape[:along], w) for a, w in zip(arrays, widths)], axis=along
    )
    filled = sent_and_summed(both, axis, dim)
    pieces = jnp.split(filled, [sum(widths[:k]) for k in range(1, len(widths))], axis=along)
    return tuple(
        (b.reshape(*filled.shape[:along], *a.shape[along:]) for a, b in zip(arrays, pieces))
    )


def sent_to_all(shard, axis):
    size = lax.axis_size(axis)
    return lax.all_to_all(
        jnp.broadcast_to(shard[None], (size, *shard.shape)), axis, 0, 0, tiled=True
    )


def collected_together(shard, axis):
    leaves = jax.tree.leaves(shard)
    order = sorted(range(len(leaves)), key=lambda k: -leaves[k].size)
    width = (1, *leaves[order[0]].shape)[-1]
    lines = [
        jnp.pad(leaves[k].reshape(-1), (0, -leaves[k].size % width)).reshape(-1, width)
        for k in order
    ]
    both, at, found = (sent_to_all(jnp.concatenate(lines), axis), 0, {})
    for k, line in zip(order, lines):
        share = both[:, at : at + len(line)].reshape(len(both), -1)
        found[k] = share[:, : leaves[k].size].reshape(-1, *leaves[k].shape)
        at += len(line)
    numbers = iter(range(len(leaves)))
    return jax.tree.map(lambda _: found[next(numbers)], shard)


def folded_in_pairs(pieces, combine):
    while len(jax.tree.leaves(pieces)[0]) > 1:
        pieces = jax.vmap(combine)(
            *(jax.tree.map(lambda part: part[side::2], pieces) for side in (0, 1))
        )
    return jax.tree.map(lambda part: part[0], pieces)


def carried_in(shard, axis, combine, identity):
    size, mine = (lax.axis_size(axis), lax.axis_index(axis))
    passed = jnp.arange(size) < mine

    def kept(part, zero, own):
        part = jnp.where(
            passed.reshape(-1, *(1 for _ in own.shape)), part, jnp.asarray(zero, own.dtype)
        )
        return part

    pieces = collected_together(shard, axis)
    return folded_in_pairs(jax.tree.map(kept, pieces, identity, shard), combine)


def gather_turned(arrays, axis, dims):
    turned = [jnp.moveaxis(a, dim, 0) for a, dim in zip(arrays, dims)]
    both = jnp.concatenate([t.reshape(len(t), -1) for t in turned], axis=1)
    filled, at, finished = (lax.all_gather(both, axis, axis=0, tiled=True), 0, [])
    for t, dim in zip(turned, dims):
        share = filled[:, at : at + t[0].size].reshape(-1, *t.shape[1:])
        finished.append(jnp.moveaxis(share, 0, dim))
        at += t[0].size
    return tuple(finished)


def collected_together_2(shard, axis):
    leaves = jax.tree.leaves(shard)
    order = sorted(range(len(leaves)), key=lambda k: -leaves[k].size)
    width = (1, *leaves[order[0]].shape)[-1]
    lines = [
        jnp.pad(leaves[k].reshape(-1), (0, -leaves[k].size % width)).reshape(-1, width)
        for k in order
    ]
    both, at, found = (lax.all_gather(jnp.concatenate(lines), axis), 0, {})
    for k, line in zip(order, lines):
        share = both[:, at : at + len(line)].reshape(len(both), -1)
        found[k] = share[:, : leaves[k].size].reshape(-1, *leaves[k].shape)
        at += len(line)
    numbers = iter(range(len(leaves)))
    return jax.tree.map(lambda _: found[next(numbers)], shard)


def gathered_by_type(shard, axis):
    leaves, found = (jax.tree.leaves(shard), {})
    for leading, a in enumerate(leaves):
        if leading not in found:
            alike = [k for k, b in enumerate(leaves) if b.dtype == a.dtype]
            got = (
                collected_together_2([leaves[k] for k in alike], axis)
                if len(alike) > 1
                else [lax.all_gather(a, axis)]
            )
            for k, b in zip(alike, got):
                found[k] = b
    numbers = iter(range(len(leaves)))
    return jax.tree.map(lambda _: found[next(numbers)], shard)


def carried_in_2(shard, axis, combine, identity):
    size, mine = (lax.axis_size(axis), lax.axis_index(axis))
    everything = gathered_by_type(shard, axis)
    start = jax.tree.map(
        lambda part, zero: jnp.broadcast_to(jnp.asarray(zero, part.dtype), part.shape),
        shard,
        identity,
    )

    def hop(k, before):
        at = size - 1 - k
        reached = at > mine
        new = combine(before, jax.tree.map(lambda part: part[at], everything))
        return jax.tree.map(lambda a, b: jnp.where(reached, a, b), new, before)

    return lax.fori_loop(0, size, hop, start)


def add_pair(earlier, later):
    return (earlier[0] + later[0], earlier[1] + later[1])


def running_states(local_state, local_total):
    shares = in_one_piece((local_state, local_total), "space", 0, 1)
    before = carried_in(
        (shares[0], shares[1]),
        "tm",
        add_pair,
        (jnp.zeros_like(shares[0]), jnp.zeros_like(shares[1])),
    )
    running = add_pair(before, shares)
    return gather_turned((running[0], running[1]), "space", (0, 0))


def later_states(local_state, local_total):
    shares = (sent_and_summed(local_state, "space", 0), sent_and_summed(local_total, "space", 0))
    after = carried_in_2(
        (shares[0], shares[1]),
        "tm",
        add_pair,
        (jnp.zeros_like(shares[0]), jnp.zeros_like(shares[1])),
    )
    running = add_pair(after, shares)
    return gather_turned((running[0], running[1]), "space", (0, 0))


def body(queries, keys_in, values_in, grad_attn):
    row_count = queries.shape[1]
    channels = queries.shape[2]
    heads = channels // HEAD_DIM
    query_rows = queries[0]
    key_rows = keys_in[0]
    value_rows = values_in[0]
    key_pos = jax.nn.relu(key_rows)
    state_part = jnp.einsum(
        "isp,isz->spz",
        key_pos.reshape(row_count, heads, HEAD_DIM),
        value_rows.reshape(row_count, heads, HEAD_DIM),
        preferred_element_type=jnp.float32,
    )
    total_part = jnp.sum(key_pos, axis=0, dtype=jnp.float32)
    state_flat, total_flat = running_states(state_part.reshape(channels, HEAD_DIM), total_part)
    running_state = state_flat.reshape(heads, HEAD_DIM, HEAD_DIM)
    running_total = total_flat.reshape(heads, HEAD_DIM)
    query_position = jax.nn.relu(query_rows).astype(jnp.float32).reshape(row_count, heads, HEAD_DIM)
    numerator = jnp.einsum("igx,gxb->igb", query_position, running_state, precision=HIGH_PRECISION)
    denom = jnp.einsum("rhk,hk->rh", query_position, running_total, precision=HIGH_PRECISION) + 1.0
    attn_f = numerator / denom[..., None]
    mixed = attn_f.reshape(row_count, channels).astype(jnp.bfloat16)
    g_out = grad_attn[0].astype(jnp.float32).reshape(row_count, heads, HEAD_DIM)
    numerator_gradient = g_out / denom[..., None]
    denominator_gradient = -jnp.sum(g_out * attn_f, axis=-1) / denom
    feature_gradient = (
        jnp.einsum("tqd,qwd->tqw", numerator_gradient, running_state, precision=HIGH_PRECISION)
        + denominator_gradient[..., None] * running_total[None]
    )
    grad_queries = jnp.where(
        query_rows.reshape(row_count, heads, HEAD_DIM) > 0, feature_gradient, 0.0
    )
    partial_state_gradient = jnp.einsum(
        "isp,isz->spz", query_position, numerator_gradient, precision=HIGH_PRECISION
    )
    gtotal_part = jnp.einsum(
        "rhk,rh->hk", query_position, denominator_gradient, precision=HIGH_PRECISION
    )
    gstate_flat, gtotal_flat = later_states(
        partial_state_gradient.reshape(channels, HEAD_DIM), gtotal_part.reshape(channels)
    )
    state_gradient = gstate_flat.reshape(heads, HEAD_DIM, HEAD_DIM)
    total_gradient = gtotal_flat.reshape(heads, HEAD_DIM)
    key_wide_float = key_pos.astype(jnp.float32).reshape(row_count, heads, HEAD_DIM)
    value_wide_float = value_rows.astype(jnp.float32).reshape(row_count, heads, HEAD_DIM)
    values_gradient = jnp.einsum(
        "igx,gxb->igb", key_wide_float, state_gradient, precision=HIGH_PRECISION
    )
    key_gradient = (
        jnp.einsum("tqd,qwd->tqw", value_wide_float, state_gradient, precision=HIGH_PRECISION)
        + total_gradient[None]
    )
    grad_keys = jnp.where(key_rows.reshape(row_count, heads, HEAD_DIM) > 0, key_gradient, 0.0)
    return (
        mixed[None],
        grad_queries.reshape(row_count, channels).astype(jnp.bfloat16)[None],
        grad_keys.reshape(row_count, channels).astype(jnp.bfloat16)[None],
        values_gradient.reshape(row_count, channels).astype(jnp.bfloat16)[None],
    )


def solution(mesh):
    placed = (
        P("tm", "space", None),
        P("tm", "space", None),
        P("tm", "space", None),
        P("tm", "space", None),
    )
    return jax.shard_map(
        body,
        mesh=mesh,
        in_specs=placed,
        out_specs=(
            P("tm", "space", None),
            P("tm", "space", None),
            P("tm", "space", None),
            P("tm", "space", None),
        ),
        check_vma=False,
    )
```

profile of v0, /device:TPU:2, one launch (start us, length us, event | category | flops | bytes accessed | tf_op | source)
XLA Modules:
  0.0 212.7 jit_solution(13621507825996979436)
XLA Ops:
  0.6 0.0 copy-start
  0.6 0.0 copy-start.1
  0.7 1.2 convert_reduce_fusion
  1.9 0.3 concatenate.27
  2.2 0.3 fusion.16
  2.6 1.1 pad_maximum_fusion
  3.6 10.2 %all-to-all-start = ((f32[32,35,113]{2,1,0:T(8,128)}), f32[32,35,113]{2,1,0:T(8,128)S(1)}, u32[]{:S(2)}, u32[]{:S(2)}) async-start(f32[32,35,113]{2,1,0:T(8,128)} %pad_maximum_fusion), calls=%async_computation | async-start | bytes 1310720 | tf_op jit(solution)/shard_map/all_to_all | solution.py:22
  13.9 18.0 %all-to-all-done = f32[32,35,113]{2,1,0:T(8,128)S(1)} async-done(((f32[32,35,113]{2,1,0:T(8,128)}), f32[32,35,113]{2,1,0:T(8,128)S(1)}, u32[]{:S(2)}, u32[]{:S(2)}) %all-to-all-start) | async-done | bytes 506272 | tf_op jit(solution)/shard_map/all_to_all | solution.py:22
  31.9 0.1 reduce_sum.46
  32.0 0.2 slice_reduce_fusion.2
  32.2 0.7 broadcast_in_dim.43
  32.9 10.6 %all-to-all-start.1 = ((f32[16,36,112]{2,1,0:T(8,128)}), f32[16,36,112]{2,1,0:T(8,128)S(1)}, u32[]{:S(2)}, u32[]{:S(2)}) async-start(f32[16,36,112]{2,1,0:T(8,128)} %broadcast_in_dim.43), calls=%async_computation.1 | async-start | bytes 655360 | tf_op jit(solution)/shard_map/all_to_all | solution.py:40
  43.5 12.3 %all-to-all-done.1 = f32[16,36,112]{2,1,0:T(8,128)S(1)} async-done(((f32[16,36,112]{2,1,0:T(8,128)}), f32[16,36,112]{2,1,0:T(8,128)S(1)}, u32[]{:S(2)}, u32[]{:S(2)}) %all-to-all-start.1) | async-done | bytes 258080 | tf_op jit(solution)/shard_map/all_to_all | solution.py:40
  55.9 0.1 slice_select_fusion.1
  56.1 0.1 copy.33
  56.2 0.1 slice_add_fusion.4
  56.3 0.1 slice_select_fusion
  56.5 0.1 maximum_bitcast_fusion
  56.6 49.1 %all-gather.1 = f32[32,35,113]{2,1,0:T(8,128)S(1)} all-gather(f32[1,35,113]{2,1,0:T(8,128)S(1)} %maximum_bitcast_fusion), channel_id=1, replica_groups=mesh['tm'=16,'space'=32] {'space'}, dimensions={0}, use_global_device_ids=true | all-gather | bytes 522060 | tf_op jit(solution)/shard_map/all_gather | solution.py:87
  105.7 0.4 slice_reduce_fusion.1
  106.1 0.0 copy-start.3
  106.1 0.1 reshape.155
  106.2 0.3 fusion.17
  106.5 0.5 copy-done.3
  107.0 1.3 fusion.7
  108.4 0.5 fusion.14
  109.0 0.7 all_to_all.18
  109.7 7.1 %all-to-all-start.3 = ((f32[32,1,35]{2,1,0:T(1,128)}), f32[32,1,35]{2,1,0:T(1,128)S(1)}, u32[]{:S(2)}, u32[]{:S(2)}) async-start(f32[32,1,35]{2,1,0:T(1,128)} %all_to_all.18), calls=%async_computation.3 | async-start | bytes 32768 | tf_op jit(solution)/shard_map/all_to_all | solution.py:22
  116.8 0.7 fusion.8
  117.5 0.9 reshape_reshape.8
  118.4 7.2 %all-to-all-done.3 = f32[32,1,35]{2,1,0:T(1,128)S(1)} async-done(((f32[32,1,35]{2,1,0:T(1,128)}), f32[32,1,35]{2,1,0:T(1,128)S(1)}, u32[]{:S(2)}, u32[]{:S(2)}) %all-to-all-start.3) | async-done | bytes 4512 | tf_op jit(solution)/shard_map/all_to_all | solution.py:22
  125.6 5.0 %all-to-all-start.2 = ((f32[32,35,112]{2,1,0:T(8,128)}), f32[32,35,112]{2,1,0:T(8,128)S(1)}, u32[]{:S(2)}, u32[]{:S(2)}) async-start(f32[32,35,112]{2,1,0:T(8,128)} %reshape_reshape.8), calls=%async_computation.2 | async-start | bytes 1310720 | tf_op jit(solution)/shard_map/all_to_all | solution.py:22
  130.5 0.1 broadcast_compare_fusion.1
  130.6 0.1 broadcast_compare_fusion
  130.7 0.1 reshape_reshape.7
  130.8 1.5 fusion.6
  132.3 0.1 reduce_sum.49
  132.4 10.7 %all-to-all-done.2 = f32[32,35,112]{2,1,0:T(8,128)S(1)} async-done(((f32[32,35,112]{2,1,0:T(8,128)}), f32[32,35,112]{2,1,0:T(8,128)S(1)}, u32[]{:S(2)}, u32[]{:S(2)}) %all-to-all-start.2) | async-done | bytes 501792 | tf_op jit(solution)/shard_map/all_to_all | solution.py:22
  143.1 0.1 reduce_sum.48
  143.1 16.0 %all-gather.2 = f32[16,36,112]{2,1,0:T(8,128)S(1)} all-gather(f32[1,36,112]{2,1,0:T(8,128)S(1)} %maximum_bitcast_fusion.1), channel_id=2, replica_groups=mesh['tm'=16,'space'=32] {'tm'}, dimensions={0}, use_global_device_ids=true | all-gather | bytes 274176 | tf_op jit(solution)/shard_map/all_gather | solution.py:103
  159.2 1.1 while.18
  160.3 0.1 copy.35
  160.4 0.1 maximum_bitcast_fusion.2
  160.5 49.2 %all-gather.3 = f32[32,35,113]{2,1,0:T(8,128)S(1)} all-gather(f32[1,35,113]{2,1,0:T(8,128)S(1)} %maximum_bitcast_fusion.2), channel_id=1, replica_groups=mesh['tm'=16,'space'=32] {'space'}, dimensions={0}, use_global_device_ids=true | all-gather | bytes 522060 | tf_op jit(solution)/shard_map/all_gather | solution.py:87
  209.7 0.4 slice_reduce_fusion
  210.1 0.1 add.133
  210.2 1.3 convolution_convert_fusion
  211.6 1.2 fusion.5
  (69 shorter events, 1.0 us)
Async XLA Ops:
  0.6 1.6 copy-start
  0.6 1.2 copy-start.1
  3.6 28.3 %all-to-all-start = ((f32[32,35,113]{2,1,0:T(8,128)}), f32[32,35,113]{2,1,0:T(8,128)S(1)}, u32[]{:S(2)}, u32[]{:S(2)}) async-start(f32[32,35,113]{2,1,0:T(8,128)} %pad_maximum_fusion), calls=%async_computation | async-start | bytes 1310720 | tf_op jit(solution)/shard_map/all_to_all | solution.py:22
  32.9 10.6 %copy-start.2 = (bf16[1,128,1120]{1,2,0:T(8,128)(2,1)S(1)}, bf16[1,128,1120]{1,2,0:T(8,128)(2,1)}, u32[]{:S(2)}) copy-start(bf16[1,128,1120]{1,2,0:T(8,128)(2,1)} %param.6) | copy-start | bytes 860164
  32.9 23.0 %all-to-all-start.1 = ((f32[16,36,112]{2,1,0:T(8,128)}), f32[16,36,112]{2,1,0:T(8,128)S(1)}, u32[]{:S(2)}, u32[]{:S(2)}) async-start(f32[16,36,112]{2,1,0:T(8,128)} %broadcast_in_dim.43), calls=%async_computation.1 | async-start | bytes 655360 | tf_op jit(solution)/shard_map/all_to_all | solution.py:40
  106.1 1.0 copy-start.3
  109.7 15.9 %all-to-all-start.3 = ((f32[32,1,35]{2,1,0:T(1,128)}), f32[32,1,35]{2,1,0:T(1,128)S(1)}, u32[]{:S(2)}, u32[]{:S(2)}) async-start(f32[32,1,35]{2,1,0:T(1,128)} %all_to_all.18), calls=%async_computation.3 | async-start | bytes 32768 | tf_op jit(solution)/shard_map/all_to_all | solution.py:22
  125.6 17.5 %all-to-all-start.2 = ((f32[32,35,112]{2,1,0:T(8,128)}), f32[32,35,112]{2,1,0:T(8,128)S(1)}, u32[]{:S(2)}, u32[]{:S(2)}) async-start(f32[32,35,112]{2,1,0:T(8,128)} %reshape_reshape.8), calls=%async_computation.2 | async-start | bytes 1310720 | tf_op jit(solution)/shard_map/all_to_all | solution.py:22
where the time goes:
time: 213 us
  blocking collectives  114 us (54%)
  waiting for transfers between devices  48.2 us (23%)
  starting transfers between devices  32.8 us (15%)
  matrix products  7.28 us (3%)
  local copies, waits for them, and re-layouts  4.91 us (2%)
  other arithmetic  3.66 us (2%)
    all_gather x2, blocking collectives, gather_turned(): lax.all_gather(both, axis, axis=0, tiled=True)  98.3 us
    all_to_all x3, waiting for transfers between devices, sent_and_summed(): pieces = lax.all_to_all(split_up(shard, dim, size), axis, 0, 0, tiled=True)  35.9 us
    all_to_all x3, starting transfers between devices, sent_and_summed(): pieces = lax.all_to_all(split_up(shard, dim, size), axis, 0, 0, tiled=True)  22.3 us
    all_gather x1, blocking collectives, collected_together_2(): both, at, found = (lax.all_gather(jnp.concatenate(lines), axis), 0, {})  16 us
    all_to_all x1, waiting for transfers between devices, sent_to_all(): lax.all_to_all(jnp.broadcast_to(shard[None], (size, *shard.shape)), axis,...  12.3 us
    all_to_all x1, starting transfers between devices, sent_to_all(): lax.all_to_all(jnp.broadcast_to(shard[None], (size, *shard.shape)), axis,...  10.6 us
  transfers between devices with their start and end apart: 4, of which 4 were waited for; matrix products, arithmetic and copies ran while one was open for 2% of the time, Pallas kernels for 0%

commit v1 on v0

v1 whole, which is shorter than its diff:
```python
import jax
import jax.numpy as jnp
from jax import lax
from jax.sharding import PartitionSpec as P

HEAD_DIM = 112
HIGH = lax.Precision.HIGHEST


def exchanged(pieces, axis):
    return lax.all_to_all(pieces, axis, 0, 0, tiled=True)


def to_all(piece, axis):
    size = lax.axis_size(axis)
    return exchanged(jnp.broadcast_to(piece[None], (size, *piece.shape)), axis)


def body(queries, keys_in, values_in, grad_attn):
    row_count, channels = queries.shape[1:]
    heads = channels // HEAD_DIM
    spaces, groups = lax.axis_size("space"), lax.axis_size("tm")
    mine = lax.axis_index("tm")
    by_head = (row_count, heads, HEAD_DIM)
    share = channels * HEAD_DIM // spaces
    query_rows, key_rows, value_rows, g_rows = (
        a[0].reshape(by_head) for a in (queries, keys_in, values_in, grad_attn)
    )
    key_pos = jax.nn.relu(key_rows)
    query_pos = jax.nn.relu(query_rows).astype(jnp.float32)
    g_out = g_rows.astype(jnp.float32)

    state_part = jnp.einsum("rhk,rhv->hkv", key_pos, value_rows, preferred_element_type=jnp.float32)
    total_part = jnp.sum(key_pos, axis=0, dtype=jnp.float32).reshape(channels)
    sent = jnp.concatenate(
        [state_part.reshape(spaces, share), jnp.broadcast_to(total_part[None], (spaces, channels))],
        axis=1,
    )
    own = jnp.sum(exchanged(sent, "space"), axis=0)

    earlier = (jnp.arange(groups) <= mine)[:, None]
    prefix = jnp.sum(jnp.where(earlier, to_all(own, "tm"), 0.0), axis=0)
    state_share, total = prefix[:share], prefix[share:].reshape(heads, HEAD_DIM)

    denom = jnp.einsum("rhk,hk->rh", query_pos, total, precision=HIGH) + 1.0
    g_num = g_out / denom[..., None]
    gstate_part = jnp.einsum("rhk,rhv->hkv", query_pos, g_num, precision=HIGH)

    sent = jnp.concatenate(
        [jnp.broadcast_to(state_share[None], (spaces, share)), gstate_part.reshape(spaces, share)],
        axis=1,
    )
    got = exchanged(sent, "space")
    state = got[:, :share].reshape(heads, HEAD_DIM, HEAD_DIM)
    gshare = jnp.sum(got[:, share:], axis=0)

    attn_f = jnp.einsum("rhk,hkv->rhv", query_pos, state, precision=HIGH) / denom[..., None]
    g_den = -jnp.sum(g_out * attn_f, axis=-1) / denom
    gtotal_part = jnp.einsum("rhk,rh->hk", query_pos, g_den, precision=HIGH).reshape(channels)

    later = (jnp.arange(groups) >= mine)[:, None]
    suffix = jnp.sum(
        jnp.where(later, to_all(jnp.concatenate([gshare, gtotal_part]), "tm"), 0.0), axis=0
    )

    got = to_all(suffix, "space")
    gstate = got[:, :share].reshape(heads, HEAD_DIM, HEAD_DIM)
    gtotal = jnp.sum(got[:, share:], axis=0).reshape(heads, HEAD_DIM)

    feature = (
        jnp.einsum("rhv,hkv->rhk", g_num, state, precision=HIGH) + g_den[..., None] * total[None]
    )
    grad_queries = jnp.where(query_rows > 0, feature, 0.0)
    key_wide = key_pos.astype(jnp.float32)
    values_gradient = jnp.einsum("rhk,hkv->rhv", key_wide, gstate, precision=HIGH)
    key_gradient = (
        jnp.einsum("rhv,hkv->rhk", value_rows.astype(jnp.float32), gstate, precision=HIGH)
        + gtotal[None]
    )
    grad_keys = jnp.where(key_rows > 0, key_gradient, 0.0)
    return tuple(
        a.reshape(1, row_count, channels).astype(jnp.bfloat16)
        for a in (attn_f, grad_queries, grad_keys, values_gradient)
    )


def solution(mesh):
    placed = P("tm", "space", None)
    return jax.shard_map(
        body, mesh=mesh, in_specs=(placed,) * 4, out_specs=(placed,) * 4, check_vma=False
    )
```

time: 213 us -> 146 us (0.69)
  the two profiles are of different devices: /device:TPU:2 before, /device:TPU:1 now
where the time goes in v1:
time: 146 us; the launch traced here: 145 us
  blocking collectives  58.4 us (40%)
  waiting for transfers between devices  43.5 us (30%)
  starting transfers between devices  25.1 us (17%)
  matrix products  7.29 us (5%)
  local copies, waits for them, and re-layouts  7.21 us (5%)
  other arithmetic  2.78 us (2%)
    all_to_all x2, blocking collectives, exchanged(): return lax.all_to_all(pieces, axis, 0, 0, tiled=True)  58.4 us
    all_to_all x3, waiting for transfers between devices, exchanged(): return lax.all_to_all(pieces, axis, 0, 0, tiled=True)  43.5 us
    all_to_all x3, starting transfers between devices, exchanged(): return lax.all_to_all(pieces, axis, 0, 0, tiled=True)  25.1 us
    broadcast_in_dim x3, local copies, waits for them, and re-layouts, to_all(): return exchanged(jnp.broadcast_to(piece[None], (size, *piece.shape)), axis)  2.94 us
  transfers between devices with their start and end apart: 3, of which 3 were waited for; matrix products, arithmetic and copies ran while one was open for 1% of the time, Pallas kernels for 0%

profile of v1, /device:TPU:1, one launch (start us, length us, event | category | flops | bytes accessed | tf_op | source)
XLA Modules:
  0.0 145.1 jit_solution(14973259767843295937)
XLA Ops:
  0.6 0.0 copy-start
  0.7 1.0 broadcast_maximum_fusion.1
  1.7 0.0 copy-done.1
  1.7 0.2 convert_reduce_fusion
  1.9 0.3 fusion.16
  2.2 0.2 reshape.138
  2.4 0.1 pad.5.clone
  2.6 0.5 all_to_all.32
  3.0 26.7 %all_to_all.48 = f32[32,1,5040]{2,1,0:T(1,128)S(1)} all-to-all(f32[32,1,5040]{2,1,0:T(1,128)S(1)} %all_to_all.32), channel_id=1, replica_groups=mesh['tm'=16,'space'=32] {'space'}, dimensions={0} | all-to-all | bytes 1290240 | tf_op jit(solution)/shard_map/all_to_all | solution.py:11
  29.7 0.4 reduce_sum.64
  30.1 0.9 broadcast_in_dim.59
  31.0 15.5 %all-to-all-start.1 = ((f32[16,1,5040]{2,1,0:T(1,128)}), f32[16,1,5040]{2,1,0:T(1,128)S(1)}, u32[]{:S(2)}, u32[]{:S(2)}) async-start(f32[16,1,5040]{2,1,0:T(1,128)} %broadcast_in_dim.59), calls=%async_computation.1 | async-start | bytes 655360 | tf_op jit(solution)/shard_map/all_to_all | solution.py:11
  46.5 13.0 %all-to-all-done.1 = f32[16,1,5040]{2,1,0:T(1,128)S(1)} async-done(((f32[16,1,5040]{2,1,0:T(1,128)}), f32[16,1,5040]{2,1,0:T(1,128)S(1)}, u32[]{:S(2)}, u32[]{:S(2)}) %all-to-all-start.1) | async-done | bytes 322592 | tf_op jit(solution)/shard_map/all_to_all | solution.py:11
  59.5 0.2 fusion.10
  59.7 0.1 slice.33
  59.8 0.5 copy-done.3
  60.3 0.1 reshape.150
  60.4 0.3 fusion.17
  60.7 0.7 fusion.8
  61.5 0.2 reshape.140
  61.7 0.5 slice-done
  62.2 0.2 pad_maximum_fusion
  62.4 0.7 all_to_all.36
  63.1 31.7 %all_to_all.49 = f32[32,1,7840]{2,1,0:T(1,128)S(1)} all-to-all(f32[32,1,7840]{2,1,0:T(1,128)S(1)} %all_to_all.36), channel_id=1, replica_groups=mesh['tm'=16,'space'=32] {'space'}, dimensions={0} | all-to-all | bytes 2007040 | tf_op jit(solution)/shard_map/all_to_all | solution.py:11
  94.8 0.1 copy.34
  94.8 0.2 slice_reduce_fusion
  95.1 0.5 reshape.141
  95.5 1.4 fusion.7
  96.9 0.5 fusion.14
  97.5 0.1 reshape.142
  97.5 0.1 pad_maximum_fusion.2
  97.6 0.9 broadcast_in_dim.64
  98.5 4.1 %all-to-all-start.3 = ((f32[16,1,5040]{2,1,0:T(1,128)}), f32[16,1,5040]{2,1,0:T(1,128)S(1)}, u32[]{:S(2)}, u32[]{:S(2)}) async-start(f32[16,1,5040]{2,1,0:T(1,128)} %broadcast_in_dim.64), calls=%async_computation.3 | async-start | bytes 655360 | tf_op jit(solution)/shard_map/all_to_all | solution.py:11
  102.6 13.1 %all-to-all-done.3 = f32[16,1,5040]{2,1,0:T(1,128)S(1)} async-done(((f32[16,1,5040]{2,1,0:T(1,128)}), f32[16,1,5040]{2,1,0:T(1,128)S(1)}, u32[]{:S(2)}, u32[]{:S(2)}) %all-to-all-start.3) | async-done | bytes 322592 | tf_op jit(solution)/shard_map/all_to_all | solution.py:11
  115.7 0.2 fusion.9
  115.9 1.2 broadcast_in_dim.65
  117.0 5.5 %all-to-all-start.4 = ((f32[32,1,5040]{2,1,0:T(1,128)}), f32[32,1,5040]{2,1,0:T(1,128)S(1)}, u32[]{:S(2)}, u32[]{:S(2)}) async-start(f32[32,1,5040]{2,1,0:T(1,128)} %broadcast_in_dim.65), calls=%async_computation.4 | async-start | bytes 1310720 | tf_op jit(solution)/shard_map/all_to_all | solution.py:11
  122.6 0.1 broadcast_compare_fusion.1
  122.7 0.1 broadcast_compare_fusion
  122.7 0.1 reshape.139
  122.8 1.5 %fusion.6 = bf16[128,10,112]{0,2,1:T(8,128)(2,1)} fusion(pred[128,10,112]{0,2,1:T(8,128)(4,1)S(1)} %bitcast.86, f32[10,112,112]{2,1,0:T(8,128)S(1)} %reshape.141, bf16[128,10,112]{0,2,1:T(8,128)(2,1)S(1)} %bitcast.91, f32[10,112]{1,0:T(8,128)S(1)} %reshape.139, f32[128,10]{0,1:T(8,128)S(1)} %negate_divide_fusion, f32[128,10]{0,1:T(8,128)S(1)} %fusion.13), kind=kOutput, calls=%fused_computation.9 | convolution fusion | flops 193536000 | bytes 1233280 | tf_op jit(solution)/shard_map/rhv,hkv->rhk/dot_general | solution.py:71
  124.3 17.4 %all-to-all-done.4 = f32[32,1,5040]{2,1,0:T(1,128)S(1)} async-done(((f32[32,1,5040]{2,1,0:T(1,128)}), f32[32,1,5040]{2,1,0:T(1,128)S(1)}, u32[]{:S(2)}, u32[]{:S(2)}) %all-to-all-start.4) | async-done | bytes 645152 | tf_op jit(solution)/shard_map/all_to_all | solution.py:11
  141.7 0.1 copy.35
  141.9 0.1 slice_reduce_fusion.1
  142.0 0.5 reshape.143
  142.5 0.1 add.29
  142.6 1.3 convolution_convert_fusion
  143.9 1.2 fusion.5
  (17 shorter events, 0.2 us)
Async XLA Ops:
  0.6 1.3 copy-start
  0.6 1.1 copy-start.1
  31.0 15.5 %copy-start.2 = (bf16[1,128,1120]{1,2,0:T(8,128)(2,1)S(1)}, bf16[1,128,1120]{1,2,0:T(8,128)(2,1)}, u32[]{:S(2)}) copy-start(bf16[1,128,1120]{1,2,0:T(8,128)(2,1)} %param.4) | copy-start | bytes 860164
  31.0 28.5 %all-to-all-start.1 = ((f32[16,1,5040]{2,1,0:T(1,128)}), f32[16,1,5040]{2,1,0:T(1,128)S(1)}, u32[]{:S(2)}, u32[]{:S(2)}) async-start(f32[16,1,5040]{2,1,0:T(1,128)} %broadcast_in_dim.59), calls=%async_computation.1 | async-start | bytes 655360 | tf_op jit(solution)/shard_map/all_to_all | solution.py:11
  46.5 14.2 %copy-start.4 = (bf16[1,128,1120]{1,2,0:T(8,128)(2,1)S(1)}, bf16[1,128,1120]{1,2,0:T(8,128)(2,1)}, u32[]{:S(2)}) copy-start(bf16[1,128,1120]{1,2,0:T(8,128)(2,1)} %param.7) | copy-start | bytes 860164
  59.7 0.6 copy-start.3
  61.4 0.7 slice-start
  98.5 17.2 %all-to-all-start.3 = ((f32[16,1,5040]{2,1,0:T(1,128)}), f32[16,1,5040]{2,1,0:T(1,128)S(1)}, u32[]{:S(2)}, u32[]{:S(2)}) async-start(f32[16,1,5040]{2,1,0:T(1,128)} %broadcast_in_dim.64), calls=%async_computation.3 | async-start | bytes 655360 | tf_op jit(solution)/shard_map/all_to_all | solution.py:11
  117.0 24.7 %all-to-all-start.4 = ((f32[32,1,5040]{2,1,0:T(1,128)}), f32[32,1,5040]{2,1,0:T(1,128)S(1)}, u32[]{:S(2)}, u32[]{:S(2)}) async-start(f32[32,1,5040]{2,1,0:T(1,128)} %broadcast_in_dim.65), calls=%async_computation.4 | async-start | bytes 1310720 | tf_op jit(solution)/shard_map/all_to_all | solution.py:11

commit v2 on v1

v2 whole, which is shorter than its diff:
```python
import functools

import jax
import jax.numpy as jnp
from jax import lax
from jax.experimental import pallas as pl
from jax.experimental.pallas import tpu as pltpu
from jax.sharding import PartitionSpec as P

HEAD_DIM = 112
LANES = 128
SLAB = 8
F32, BF16 = jnp.float32, jnp.bfloat16
VMEM = pl.BlockSpec(memory_space=pltpu.VMEM)
SMEM = pl.BlockSpec(memory_space=pltpu.SMEM)
NT = (((1,), (1,)), ((), ()))


class Tile:
    def __init__(self, j, channels):
        self.j, self.at = j, LANES * j
        self.width = min(LANES, channels - self.at)
        self.first = self.at // HEAD_DIM
        self.last = (self.at + self.width - 1) // HEAD_DIM
        self.here = slice(self.at, self.at + self.width)
        self.cut = min(self.width, HEAD_DIM * (self.first + 1) - self.at)
        self.pair = slice(HEAD_DIM * self.first, HEAD_DIM * (self.last + 1))


def tiles(channels):
    return [Tile(j, channels) for j in range(-(-channels // LANES))]


def dot(a, b):
    return jnp.dot(a, b, preferred_element_type=F32)


def dot_rows(a, b):
    return lax.dot_general(a, b, (((1,), (1,)), ((), ())), preferred_element_type=F32)


def halves(x):
    hi = x.astype(BF16)
    return hi, (x - hi.astype(F32)).astype(BF16)


def thirds(x):
    hi = x.astype(BF16)
    rest = x - hi.astype(F32)
    mid = rest.astype(BF16)
    return hi, mid, (rest - mid.astype(F32)).astype(BF16)


def relu(x):
    return jnp.maximum(x, jnp.zeros_like(x))


def lane(shape):
    return lax.broadcasted_iota(jnp.int32, shape, 1)


def row(shape):
    return lax.broadcasted_iota(jnp.int32, shape, 0)


def of_head(h):
    return slice(HEAD_DIM * h, HEAD_DIM * (h + 1))


def on_own_head(tile, x):
    heads = jnp.where(lane(x.shape) < tile.cut, tile.first, tile.last)
    return jnp.where(row(x.shape) == heads, x, 0.0)


def heads_apart(tile, both):
    if tile.first == tile.last:
        return both
    top, bottom = both[:HEAD_DIM], both[HEAD_DIM:]
    return jnp.where(lane(top.shape) < tile.cut, top, bottom)


class Slabs:
    def __init__(self, pitch, each, base=0):
        self.pitch, self.each, self.base = pitch, each, base

    def rows(self, tile):
        for i in range(HEAD_DIM // SLAB):
            number = HEAD_DIM // SLAB * tile.j + i
            at = self.pitch * (number // self.each) + self.base + SLAB * (number % self.each)
            yield slice(SLAB * i, SLAB * (i + 1)), slice(at, at + SLAB)

    def put(self, ref, tile, value):
        for here, there in self.rows(tile):
            ref[there, : tile.width] = value[here]

    def get(self, ref, tile):
        parts = [ref[there, : tile.width] for _, there in self.rows(tile)]
        return jnp.concatenate(parts, axis=0)


def by_state(flat_ref, rows_ref, h):
    channels = flat_ref.shape[1]
    start = HEAD_DIM * h // LANES * LANES
    stop = min(channels, -(-HEAD_DIM * (h + 1) // LANES) * LANES)
    s = flat_ref[:, start:stop]
    c = lane(s.shape) + start
    hi, lo = halves(jnp.where((c >= HEAD_DIM * h) & (c < HEAD_DIM * (h + 1)), s, 0.0))
    rhs = relu(rows_ref[start:stop, :])
    return dot(hi, rhs) + dot(lo, rhs)


def turn(tile, state, extra, hi_ref, lo_ref):
    hi, lo = halves(jnp.concatenate([state, extra], axis=0).T)
    hi_ref[tile.here, :], lo_ref[tile.here, :] = hi, lo


def with_rows(x, rest):
    return jnp.concatenate([x, rest.astype(BF16)], axis=0)


def states_kernel(slabs, pieces, k_ref, v_ref, out_ref, total_ref):
    channels, rows = k_ref.shape
    out_ref[...] = jnp.zeros_like(out_ref)
    total_ref[...] = jnp.zeros_like(total_ref)
    ones = jnp.ones((16, rows), BF16)
    for t in tiles(channels):
        keys = relu(k_ref[t.here, :])
        slabs.put(out_ref, t, heads_apart(t, dot_rows(v_ref[t.pair, :], keys)))
        total_ref[t.j : t.j + 1, : t.width] = dot_rows(ones, keys)[:1]
    total = total_ref[...]
    for s in range(pieces):
        at = slabs.pitch * s + SLAB * slabs.each
        out_ref[at : at + len(total), :] = total


def sum_kernel(sources, targets, pitch, in_ref, out_ref):
    own = in_ref[0:pitch, :]
    for s in range(1, sources):
        own = own + in_ref[pitch * s : pitch * (s + 1), :]
    for s in range(targets):
        out_ref[pitch * s : pitch * (s + 1), :] = own


def kept(in_ref, groups, pitch, keep):
    total = None
    for g in range(groups):
        part = jnp.where(keep(g), in_ref[pitch * g : pitch * (g + 1), :], 0.0)
        total = part if total is None else total + part
    return total


def suffix_kernel(groups, targets, pitch, mine_ref, in_ref, out_ref):
    mine = mine_ref[0]
    own = kept(in_ref, groups, pitch, lambda g: g >= mine)
    for s in range(targets):
        out_ref[pitch * s : pitch * (s + 1), :] = own


def denominators(q_ref, total, padded):
    den = None
    for t in tiles(q_ref.shape[0]):
        spot = on_own_head(t, jnp.broadcast_to(total[t.j : t.j + 1, : t.width], (padded, t.width)))
        term = dot(jnp.concatenate(thirds(spot), axis=0), relu(q_ref[t.here, :]))
        den = term if den is None else den + term
    return den[:padded] + den[padded : 2 * padded] + den[2 * padded :] + 1.0


def gradient_states(slabs, q_ref, g_ref, rec, out_ref, hi_ref, lo_ref):
    channels = q_ref.shape[0]
    for h in range(channels // HEAD_DIM):
        hi, lo = halves(g_ref[of_head(h), :].astype(F32) * rec[h : h + 1])
        hi_ref[of_head(h), :], lo_ref[of_head(h), :] = hi, lo
    for t in tiles(channels):
        rhs = relu(q_ref[t.here, :])
        both = dot_rows(hi_ref[t.pair, :], rhs) + dot_rows(lo_ref[t.pair, :], rhs)
        slabs.put(out_ref, t, heads_apart(t, both))


def denominator_kernel(groups, spaces, pitch, slabs, mine_ref, in_ref, q_ref, g_ref, out_ref, rec_ref, total_ref, hi_ref, lo_ref):
    mine = mine_ref[0]
    out_ref[...] = jnp.zeros_like(out_ref)
    own = kept(in_ref, groups, pitch, lambda g: g <= mine)
    share, total = own[: slabs.base], own[slabs.base :]
    total_ref[...] = total
    rec = 1.0 / denominators(q_ref, total, rec_ref.shape[0])
    rec_ref[...] = rec
    gradient_states(slabs, q_ref, g_ref, rec, out_ref, hi_ref, lo_ref)
    for s in range(spaces):
        out_ref[slabs.pitch * s : slabs.pitch * s + slabs.base, :] = share


def attention(slabs, in_ref, q_ref, g_ref, rec, mixed_ref, sums_ref, gt_ref, flat_ref):
    channels = q_ref.shape[0]
    padded = rec.shape[0]
    for t in tiles(channels):
        flat_ref[:, t.here] = slabs.get(in_ref, t)
    sums_ref[...] = jnp.zeros_like(sums_ref)
    gt_ref[...] = jnp.zeros_like(gt_ref)
    for h in range(channels // HEAD_DIM):
        attn = by_state(flat_ref, q_ref, h) * rec[h : h + 1]
        mixed_ref[of_head(h), :] = attn.astype(BF16)
        sums_ref[h : h + 1, :] = jnp.sum(g_ref[of_head(h), :].astype(F32) * attn, axis=0, keepdims=True)
    pair = jnp.concatenate(halves(-sums_ref[...] * rec), axis=0)
    for t in tiles(channels):
        term = dot_rows(pair, relu(q_ref[t.here, :]))
        term = on_own_head(t, term[:padded] + term[padded:])
        gt_ref[t.j : t.j + 1, : t.width] = jnp.sum(term, axis=0, keepdims=True)


def attention_kernel(spaces, groups, pitch, slabs, in_ref, q_ref, g_ref, rec_ref, out_ref, mixed_ref, sums_ref, flat_ref, gt_ref):
    attention(slabs, in_ref, q_ref, g_ref, rec_ref[...], mixed_ref, sums_ref, gt_ref, flat_ref)
    size = SLAB * slabs.each
    share = in_ref[size : 2 * size, :]
    for s in range(1, spaces):
        at = slabs.pitch * s + size
        share = share + in_ref[at : at + size, :]
    own = jnp.concatenate([share, gt_ref[...]], axis=0)
    for g in range(groups):
        out_ref[pitch * g : pitch * (g + 1), :] = own


def queries_kernel(slabs, in_ref, q_ref, g_ref, rec_ref, sums_ref, total_ref, out_ref, hi_ref, lo_ref):
    channels, rows = q_ref.shape
    for t in tiles(channels):
        shape = (LANES - HEAD_DIM, t.width)
        extra = jnp.where(row(shape) < 2, jnp.broadcast_to(total_ref[t.j : t.j + 1, : t.width], shape), 0.0)
        turn(t, slabs.get(in_ref, t), extra, hi_ref, lo_ref)
    for h in range(channels // HEAD_DIM):
        hi, lo = halves(-sums_ref[h : h + 1, :])
        shape = (LANES - HEAD_DIM, rows)
        rest = jnp.where(row(shape) == 0, jnp.broadcast_to(hi.astype(F32), shape), 0.0)
        rest = jnp.where(row(shape) == 1, jnp.broadcast_to(lo.astype(F32), shape), rest)
        rhs = with_rows(g_ref[of_head(h), :], rest)
        feature = (dot(hi_ref[of_head(h), :], rhs) + dot(lo_ref[of_head(h), :], rhs)) * rec_ref[h : h + 1, :]
        q = q_ref[of_head(h), :].astype(F32)
        out_ref[of_head(h), :] = jnp.where(q > 0, feature, 0.0).astype(BF16)


def keys(slabs, in_ref, total, k_ref, v_ref, gk_ref, gv_ref, flat_ref, hi_ref, lo_ref):
    channels, rows = k_ref.shape
    for t in tiles(channels):
        shape = (LANES - HEAD_DIM, t.width)
        extra = jnp.where(row(shape) < 1, jnp.broadcast_to(total[t.j : t.j + 1, : t.width], shape), 0.0)
        state = slabs.get(in_ref, t)
        flat_ref[:, t.here] = state
        turn(t, state, extra, hi_ref, lo_ref)
    ones = jnp.ones((LANES - HEAD_DIM, rows), BF16)
    for h in range(channels // HEAD_DIM):
        gv_ref[of_head(h), :] = by_state(flat_ref, k_ref, h).astype(BF16)
        rhs = with_rows(v_ref[of_head(h), :], ones)
        grad = dot(hi_ref[of_head(h), :], rhs) + dot(lo_ref[of_head(h), :], rhs)
        k = k_ref[of_head(h), :].astype(F32)
        gk_ref[of_head(h), :] = jnp.where(k > 0, grad, 0.0).astype(BF16)


def keys_kernel(spaces, slabs, in_ref, k_ref, v_ref, gk_ref, gv_ref, flat_ref, hi_ref, lo_ref):
    base = SLAB * slabs.each
    total = in_ref[base : slabs.pitch, :]
    for s in range(1, spaces):
        total = total + in_ref[slabs.pitch * s + base : slabs.pitch * (s + 1), :]
    keys(slabs, in_ref, total, k_ref, v_ref, gk_ref, gv_ref, flat_ref, hi_ref, lo_ref)


def call(kernel, out, in_specs, scratch=(), flops=10**7, moved=10**6):
    shapes = [jax.ShapeDtypeStruct(s, d) for s, d in out]
    several = len(shapes) > 1
    return pl.pallas_call(
        kernel,
        out_shape=shapes if several else shapes[0],
        in_specs=in_specs,
        out_specs=[VMEM] * len(shapes) if several else VMEM,
        scratch_shapes=[pltpu.VMEM(s, d) for s, d in scratch],
        cost_estimate=pl.CostEstimate(flops=flops, bytes_accessed=moved, transcendentals=0),
        compiler_params=pltpu.CompilerParams(vmem_limit_bytes=24 * 2**20),
    )


def exchanged(message, axis):
    pieces = message.reshape(lax.axis_size(axis), -1)
    return lax.all_to_all(pieces, axis, 0, 0, tiled=True).reshape(message.shape)


def body(queries, keys_in, values_in, grad_attn):
    q, k, v, g = (a[0].T for a in (queries, keys_in, values_in, grad_attn))
    channels, rows = q.shape
    spaces, groups = lax.axis_size("space"), lax.axis_size("tm")
    mine = lax.axis_index("tm").astype(jnp.int32).reshape(1)
    count = len(tiles(channels))
    each = -(-count * (HEAD_DIM // SLAB) // spaces)
    base = SLAB * each
    pitch = base + count
    first, second = Slabs(pitch, each), Slabs(2 * base, each, base)
    flat, line = ((HEAD_DIM, channels), F32), ((count, LANES), F32)
    whole, small = ((channels, rows), BF16), ((16, rows), F32)

    sent = call(
        functools.partial(states_kernel, first, spaces),
        [((spaces * pitch, LANES), F32)], [VMEM] * 2, [line],
    )(k, v)
    sent = call(
        functools.partial(sum_kernel, spaces, groups, pitch),
        [((groups * pitch, LANES), F32)], [VMEM],
    )(exchanged(sent, "space"))
    sent, rec, total = call(
        functools.partial(denominator_kernel, groups, spaces, pitch, second),
        [((spaces * 2 * base, LANES), F32), small, line], [SMEM] + [VMEM] * 3, [whole, whole],
    )(mine, exchanged(sent, "tm"), q, g)
    states = exchanged(sent, "space")
    got = Slabs(2 * base, each)
    sent, mixed, sums = call(
        functools.partial(attention_kernel, spaces, groups, pitch, got),
        [((groups * pitch, LANES), F32), whole, small], [VMEM] * 4, [flat, line],
    )(states, q, g, rec)
    sent = call(
        functools.partial(suffix_kernel, groups, spaces, pitch),
        [((spaces * pitch, LANES), F32)], [SMEM, VMEM],
    )(mine, exchanged(sent, "tm"))
    grad_queries = call(
        functools.partial(queries_kernel, got), [whole], [VMEM] * 6, [whole, whole],
    )(states, q, g, rec, sums, total)
    grad_keys, values_gradient = call(
        functools.partial(keys_kernel, spaces, first), [whole] * 2, [VMEM] * 3, [flat, whole, whole],
    )(exchanged(sent, "space"), k, v)
    return tuple(a.T[None] for a in (mixed, grad_queries, grad_keys, values_gradient))


def solution(mesh):
    placed = P("tm", "space", None)
    return jax.shard_map(
        body, mesh=mesh, in_specs=(placed,) * 4, out_specs=(placed,) * 4, check_vma=False
    )
```

time: 146 us -> 139 us (0.952)
  blocking collectives: 58.4 us -> 76.6 us
  waiting for transfers between devices: 43.5 us -> 32 us
  matrix products: 7.29 us -> 0 us
  Pallas kernels: 0 us -> 7.04 us
  local copies, waits for them, and re-layouts: 7.21 us -> 1.93 us
  starting transfers between devices: 25.1 us -> 20.5 us
  other arithmetic: 2.78 us -> 0 us
    all_to_all x2 -> x3, blocking collectives: 58.4 us -> 76.6 us  [exchanged(): return lax.all_to_all(pieces, axis, 0, 0, tiled=True).reshape(message.shape)]
    all_to_all x3 -> x2, waiting for transfers between devices: 43.5 us -> 32 us  [exchanged(): return lax.all_to_all(pieces, axis, 0, 0, tiled=True).reshape(message.shape)]
    dot_general x8 -> x0, matrix products: 7.29 us -> none  [the longest x1 1.52 us: body(): jnp.einsum('rhv,hkv->rhk', g_num, state, precision=HIGH)]
    pallas_call x0 -> x7, Pallas kernels: none -> 7.04 us  [the longest x1 1.62 us: body(): call(functools.partial(keys_kernel, spaces, first), [whole] * 2, [VMEM] *...]
    all_to_all x3 -> x2, starting transfers between devices: 25.1 us -> 20.5 us  [exchanged(): return lax.all_to_all(pieces, axis, 0, 0, tiled=True).reshape(message.shape)]
    broadcast_in_dim x3 -> x0, local copies, waits for them, and re-layouts: 2.94 us -> none  [to_all(): return exchanged(jnp.broadcast_to(piece[None], (size, *piece.shape)), axis)]
    reshape x7 -> x0, local copies, waits for them, and re-layouts: 1.58 us -> none  [the longest x1 0.47 us: body(): state = got[:, :share].reshape(heads, HEAD_DIM, HEAD_DIM)]
  transfers between devices with their start and end apart: 3 -> 2, of which waited for: 3 -> 2; matrix products, arithmetic and copies ran while one was open for 1% -> 0% of each run, Pallas kernels for 0% -> 1%
where the time goes in v2:
time: 139 us
  blocking collectives  76.6 us (55%)
  waiting for transfers between devices  32 us (23%)
  starting transfers between devices  20.5 us (15%)
  Pallas kernels  7.04 us (5%)
  local copies, waits for them, and re-layouts  1.93 us (1%)
    all_to_all x3, blocking collectives, exchanged(): return lax.all_to_all(pieces, axis, 0, 0, tiled=True).reshape(message.shape)  76.6 us
    all_to_all x2, waiting for transfers between devices, exchanged(): return lax.all_to_all(pieces, axis, 0, 0, tiled=True).reshape(message.shape)  32 us
    all_to_all x2, starting transfers between devices, exchanged(): return lax.all_to_all(pieces, axis, 0, 0, tiled=True).reshape(message.shape)  20.5 us
  transfers between devices with their start and end apart: 2, of which 2 were waited for; matrix products, arithmetic and copies ran while one was open for 0% of the time, Pallas kernels for 1%

profile of v2, /device:TPU:1, one launch (start us, length us, event | category | flops | bytes accessed | tf_op | source)
XLA Modules:
  0.0 138.8 jit_solution(1639139699039970991)
XLA Ops:
  0.6 0.0 copy-start.2
  0.6 0.9 copy-done.2
  1.6 0.0 copy-start.4
  1.6 1.0 copy-done.4
  2.6 0.4 shard_map.75
  3.0 27.0 %all_to_all.45 = f32[32,1,5248]{2,1,0:T(1,128)S(1)} all-to-all(f32[32,1,5248]{2,1,0:T(1,128)S(1)} %bitcast.39), channel_id=1, replica_groups=mesh['tm'=16,'space'=32] {'space'}, dimensions={0} | all-to-all | bytes 1343488 | tf_op jit(solution)/shard_map/all_to_all | solution.py:280
  30.0 0.8 shard_map.76
  30.8 0.0 copy-start
  30.8 0.0 copy-start.1
  30.8 15.4 %all-to-all-start.1 = ((f32[16,1,5248]{2,1,0:T(1,128)}), f32[16,1,5248]{2,1,0:T(1,128)S(1)}, u32[]{:S(2)}, u32[]{:S(2)}) async-start(f32[16,1,5248]{2,1,0:T(1,128)} %bitcast.7), calls=%async_computation.1 | async-start | bytes 671744 | tf_op jit(solution)/shard_map/all_to_all | solution.py:280
  46.2 13.2 %all-to-all-done.1 = f32[16,1,5248]{2,1,0:T(1,128)S(1)} async-done(((f32[16,1,5248]{2,1,0:T(1,128)}), f32[16,1,5248]{2,1,0:T(1,128)S(1)}, u32[]{:S(2)}, u32[]{:S(2)}) %all-to-all-start.1) | async-done | bytes 335904 | tf_op jit(solution)/shard_map/all_to_all | solution.py:280
  59.5 0.0 copy-done
  59.5 0.0 copy-done.1
  59.5 0.8 shard_map.77
  60.2 32.3 %all_to_all.46 = f32[32,1,8192]{2,1,0:T(1,128)S(1)} all-to-all(f32[32,1,8192]{2,1,0:T(1,128)S(1)} %bitcast.52), channel_id=1, replica_groups=mesh['tm'=16,'space'=32] {'space'}, dimensions={0} | all-to-all | bytes 2097152 | tf_op jit(solution)/shard_map/all_to_all | solution.py:280
  92.5 1.2 shard_map.78
  93.7 17.3 %all_to_all.47 = f32[16,1,5248]{2,1,0:T(1,128)S(1)} all-to-all(f32[16,1,5248]{2,1,0:T(1,128)S(1)} %bitcast.53), channel_id=1, replica_groups=mesh['tm'=16,'space'=32] {'tm'}, dimensions={0} | all-to-all | bytes 671744 | tf_op jit(solution)/shard_map/all_to_all | solution.py:280
  111.0 0.9 shard_map.80
  111.9 5.1 %all-to-all-start.4 = ((f32[32,1,5248]{2,1,0:T(1,128)}), f32[32,1,5248]{2,1,0:T(1,128)S(1)}, u32[]{:S(2)}, u32[]{:S(2)}) async-start(f32[32,1,5248]{2,1,0:T(1,128)} %bitcast.23), calls=%async_computation.4 | async-start | bytes 1343488 | tf_op jit(solution)/shard_map/all_to_all | solution.py:280
  117.1 0.0 copy-start.3
  117.1 0.0 copy-start.5
  117.1 1.3 shard_map.79
  118.4 18.7 %all-to-all-done.4 = f32[32,1,5248]{2,1,0:T(1,128)S(1)} async-done(((f32[32,1,5248]{2,1,0:T(1,128)}), f32[32,1,5248]{2,1,0:T(1,128)S(1)}, u32[]{:S(2)}, u32[]{:S(2)}) %all-to-all-start.4) | async-done | bytes 671776 | tf_op jit(solution)/shard_map/all_to_all | solution.py:280
  137.1 0.0 copy-done.3
  137.1 0.0 copy-done.5
  137.1 1.6 %shard_map.81 = (bf16[1120,128]{1,0:T(8,128)(2,1)}, bf16[1120,128]{1,0:T(8,128)(2,1)}) custom-call(f32[1312,128]{1,0:T(8,128)S(1)} %bitcast.37, bf16[1120,128]{1,0:T(8,128)(2,1)S(1)} %bitcast.49, bf16[1120,128]{1,0:T(8,128)(2,1)S(1)} %bitcast.51), custom_call_target="tpu_custom_call" | custom-call | flops 10000000 | bytes 1000000 | tf_op jit(solution)/shard_map/pallas_call | solution.py:321
Async XLA Ops:
  0.6 1.0 copy-start.2
  1.6 1.0 copy-start.4
  30.8 28.6 %copy-start = (bf16[1,128,1120]{1,2,0:T(8,128)(2,1)S(1)}, bf16[1,128,1120]{1,2,0:T(8,128)(2,1)}, u32[]{:S(2)}) copy-start(bf16[1,128,1120]{1,2,0:T(8,128)(2,1)} %param.4) | copy-start | bytes 860164
  30.8 28.6 %copy-start.1 = (bf16[1,128,1120]{1,2,0:T(8,128)(2,1)S(1)}, bf16[1,128,1120]{1,2,0:T(8,128)(2,1)}, u32[]{:S(2)}) copy-start(bf16[1,128,1120]{1,2,0:T(8,128)(2,1)} %param.7) | copy-start | bytes 860164
  30.8 28.6 %all-to-all-start.1 = ((f32[16,1,5248]{2,1,0:T(1,128)}), f32[16,1,5248]{2,1,0:T(1,128)S(1)}, u32[]{:S(2)}, u32[]{:S(2)}) async-start(f32[16,1,5248]{2,1,0:T(1,128)} %bitcast.7), calls=%async_computation.1 | async-start | bytes 671744 | tf_op jit(solution)/shard_map/all_to_all | solution.py:280
  111.9 25.2 %all-to-all-start.4 = ((f32[32,1,5248]{2,1,0:T(1,128)}), f32[32,1,5248]{2,1,0:T(1,128)S(1)}, u32[]{:S(2)}, u32[]{:S(2)}) async-start(f32[32,1,5248]{2,1,0:T(1,128)} %bitcast.23), calls=%async_computation.4 | async-start | bytes 1343488 | tf_op jit(solution)/shard_map/all_to_all | solution.py:280
  117.1 20.0 %copy-start.3 = (bf16[1,128,1120]{1,2,0:T(8,128)(2,1)S(1)}, bf16[1,128,1120]{1,2,0:T(8,128)(2,1)}, u32[]{:S(2)}) copy-start(bf16[1,128,1120]{1,2,0:T(8,128)(2,1)} %param.5) | copy-start | bytes 860164
  117.1 20.0 %copy-start.5 = (bf16[1,128,1120]{1,2,0:T(8,128)(2,1)S(1)}, bf16[1,128,1120]{1,2,0:T(8,128)(2,1)}, u32[]{:S(2)}) copy-start(bf16[1,128,1120]{1,2,0:T(8,128)(2,1)} %param.6) | copy-start | bytes 860164

commit v3 on v2

--- a/solution.py
+++ b/solution.py
@@ -5,6 +5,7 @@
 from jax import lax
 from jax.experimental import pallas as pl
 from jax.experimental.pallas import tpu as pltpu
+from jax.sharding import Mesh
 from jax.sharding import PartitionSpec as P
 
 HEAD_DIM = 112
@@ -133,27 +134,73 @@
         out_ref[at : at + len(total), :] = total
 
 
-def sum_kernel(sources, targets, pitch, in_ref, out_ref):
-    own = in_ref[0:pitch, :]
-    for s in range(1, sources):
-        own = own + in_ref[pitch * s : pitch * (s + 1), :]
-    for s in range(targets):
+def total_of(parts):
+    parts = list(parts)
+    out = parts[0]
+    for part in parts[1:]:
+        out = out + part
+    return out
+
+
+def cut_rows(ref, pitch, piece, start, size):
+    at = pitch * piece + start
+    return ref[at : at + size, :]
+
+
+def to_rows_kernel(sizes, in_ref, out_ref):
+    chips, rows, base, pitch = sizes
+    height = in_ref.shape[0] // (2 * chips)
+    sums = [
+        total_of(cut_rows(in_ref, height, chips * c + x, 0, height) for x in range(chips))
+        for c in range(2)
+    ]
+    totals = jnp.concatenate([s[rows * base :] for s in sums], axis=0)
+    for y in range(rows):
+        for c in range(2):
+            at = pitch * y + base * c
+            out_ref[at : at + base, :] = sums[c][base * y : base * (y + 1)]
+        out_ref[pitch * y + 2 * base : pitch * (y + 1), :] = totals
+
+
+def to_planes_kernel(pieces, pitch, in_ref, out_ref):
+    own = total_of(cut_rows(in_ref, pitch, s, 0, pitch) for s in range(pieces))
+    for s in range(pieces):
         out_ref[pitch * s : pitch * (s + 1), :] = own
 
 
-def kept(in_ref, groups, pitch, keep):
-    total = None
-    for g in range(groups):
-        part = jnp.where(keep(g), in_ref[pitch * g : pitch * (g + 1), :], 0.0)
-        total = part if total is None else total + part
-    return total
-
-
-def suffix_kernel(groups, targets, pitch, mine_ref, in_ref, out_ref):
-    mine = mine_ref[0]
-    own = kept(in_ref, groups, pitch, lambda g: g >= mine)
-    for s in range(targets):
-        out_ref[pitch * s : pitch * (s + 1), :] = own
+def suffix_kernel(sizes, mine_ref, in_ref, out_ref):
+    planes, rows, base, height, pitch = sizes
+    z, core = mine_ref[0], mine_ref[1]
+    size = height - 2 * base
+    early, late, shared, own = [], [], [], []
+    for p in range(planes):
+        first, second = (cut_rows(in_ref, height, p, base * c, base) for c in range(2))
+        part = cut_rows(in_ref, height, p, 2 * base, size)
+        both = jnp.where(p > z, first + second, 0.0)
+        early.append(both + jnp.where(p == z, first + second, 0.0))
+        late.append(both + jnp.where(p == z, second, 0.0))
+        shared.append(jnp.where(p >= z, part, 0.0))
+        own.append(jnp.where(p + core > z, part, 0.0))
+    message = jnp.concatenate(
+        [total_of(early), total_of(late), total_of(shared), total_of(own)], axis=0
+    )
+    for s in range(rows):
+        out_ref[pitch * s : pitch * (s + 1), :] = message
+
+
+def to_columns_kernel(sizes, in_ref, out_ref):
+    chips, rows, base, pitch = sizes
+    size = (pitch - 2 * base) // 2
+    height = rows * base + size
+    for c in range(2):
+        parts = [cut_rows(in_ref, pitch, y, base * c, base) for y in range(rows)]
+        parts.append(
+            total_of(cut_rows(in_ref, pitch, y, 2 * base + size * c, size) for y in range(rows))
+        )
+        message = jnp.concatenate(parts, axis=0)
+        for x in range(chips):
+            at = height * (chips * c + x)
+            out_ref[at : at + height, :] = message
 
 
 def denominators(q_ref, total, padded):
@@ -176,17 +223,31 @@
         slabs.put(out_ref, t, heads_apart(t, both))
 
 
-def denominator_kernel(groups, spaces, pitch, slabs, mine_ref, in_ref, q_ref, g_ref, out_ref, rec_ref, total_ref, hi_ref, lo_ref):
-    mine = mine_ref[0]
+def prefix(planes, pitch, base, mine_ref, in_ref):
+    z, core = mine_ref[0], mine_ref[1]
+    size = (pitch - 2 * base) // 2
+    early, late, own = [], [], []
+    for p in range(planes):
+        first, second = (cut_rows(in_ref, pitch, p, base * c, base) for c in range(2))
+        low, high = (cut_rows(in_ref, pitch, p, 2 * base + size * c, size) for c in range(2))
+        both = jnp.where(p < z, first + second, 0.0)
+        early.append(both + jnp.where(p == z, first, 0.0))
+        late.append(both + jnp.where(p == z, first + second, 0.0))
+        own.append(jnp.where(p <= z, low, 0.0) + jnp.where(p < z + core, high, 0.0))
+    return total_of(early), total_of(late), total_of(own)
+
+
+def denominator_kernel(planes, pitch, slabs, mine_ref, in_ref, q_ref, g_ref, out_ref, rec_ref, total_ref, hi_ref, lo_ref):
     out_ref[...] = jnp.zeros_like(out_ref)
-    own = kept(in_ref, groups, pitch, lambda g: g <= mine)
-    share, total = own[: slabs.base], own[slabs.base :]
+    early, late, total = prefix(planes, pitch, slabs.base, mine_ref, in_ref)
     total_ref[...] = total
     rec = 1.0 / denominators(q_ref, total, rec_ref.shape[0])
     rec_ref[...] = rec
     gradient_states(slabs, q_ref, g_ref, rec, out_ref, hi_ref, lo_ref)
-    for s in range(spaces):
-        out_ref[slabs.pitch * s : slabs.pitch * s + slabs.base, :] = share
+    pieces = out_ref.shape[0] // slabs.pitch
+    for s in range(pieces):
+        at = slabs.pitch * s
+        out_ref[at : at + slabs.base, :] = early if 2 * s < pieces else late
 
 
 def attention(slabs, in_ref, q_ref, g_ref, rec, mixed_ref, sums_ref, gt_ref, flat_ref):
@@ -207,16 +268,18 @@
         gt_ref[t.j : t.j + 1, : t.width] = jnp.sum(term, axis=0, keepdims=True)
 
 
-def attention_kernel(spaces, groups, pitch, slabs, in_ref, q_ref, g_ref, rec_ref, out_ref, mixed_ref, sums_ref, flat_ref, gt_ref):
+def attention_kernel(planes, slabs, in_ref, q_ref, g_ref, rec_ref, out_ref, mixed_ref, sums_ref, flat_ref, gt_ref):
     attention(slabs, in_ref, q_ref, g_ref, rec_ref[...], mixed_ref, sums_ref, gt_ref, flat_ref)
     size = SLAB * slabs.each
-    share = in_ref[size : 2 * size, :]
-    for s in range(1, spaces):
-        at = slabs.pitch * s + size
-        share = share + in_ref[at : at + size, :]
-    own = jnp.concatenate([share, gt_ref[...]], axis=0)
-    for g in range(groups):
-        out_ref[pitch * g : pitch * (g + 1), :] = own
+    half = in_ref.shape[0] // slabs.pitch // 2
+    sums = [
+        total_of(cut_rows(in_ref, slabs.pitch, half * c + s, size, size) for s in range(half))
+        for c in range(2)
+    ]
+    message = jnp.concatenate([*sums, gt_ref[...]], axis=0)
+    height = len(message)
+    for p in range(planes):
+        out_ref[height * p : height * (p + 1), :] = message
 
 
 def queries_kernel(slabs, in_ref, q_ref, g_ref, rec_ref, sums_ref, total_ref, out_ref, hi_ref, lo_ref):
@@ -253,11 +316,10 @@
         gk_ref[of_head(h), :] = jnp.where(k > 0, grad, 0.0).astype(BF16)
 
 
-def keys_kernel(spaces, slabs, in_ref, k_ref, v_ref, gk_ref, gv_ref, flat_ref, hi_ref, lo_ref):
+def keys_kernel(slabs, in_ref, k_ref, v_ref, gk_ref, gv_ref, flat_ref, hi_ref, lo_ref):
     base = SLAB * slabs.each
-    total = in_ref[base : slabs.pitch, :]
-    for s in range(1, spaces):
-        total = total + in_ref[slabs.pitch * s + base : slabs.pitch * (s + 1), :]
+    pieces = in_ref.shape[0] // slabs.pitch
+    total = total_of(cut_rows(in_ref, slabs.pitch, s, base, slabs.pitch - base) for s in range(pieces))
     keys(slabs, in_ref, total, k_ref, v_ref, gk_ref, gv_ref, flat_ref, hi_ref, lo_ref)
 
 
@@ -280,52 +342,66 @@
     return lax.all_to_all(pieces, axis, 0, 0, tiled=True).reshape(message.shape)
 
 
+CHIP, PLANE = ("core", "x"), ("core", "x", "y")
+
+
 def body(queries, keys_in, values_in, grad_attn):
     q, k, v, g = (a[0].T for a in (queries, keys_in, values_in, grad_attn))
     channels, rows = q.shape
-    spaces, groups = lax.axis_size("space"), lax.axis_size("tm")
-    mine = lax.axis_index("tm").astype(jnp.int32).reshape(1)
+    nx, ny, nz = (lax.axis_size(a) for a in ("x", "y", "z"))
+    mine = jnp.stack([lax.axis_index("z"), lax.axis_index("core")]).astype(jnp.int32)
     count = len(tiles(channels))
-    each = -(-count * (HEAD_DIM // SLAB) // spaces)
+    each = -(-count * (HEAD_DIM // SLAB) // (2 * nx * ny))
     base = SLAB * each
-    pitch = base + count
-    first, second = Slabs(pitch, each), Slabs(2 * base, each, base)
+    tall, pitch, short = ny * base + count, 2 * (base + count), 2 * base + count
+    outer, middle = Slabs(tall, ny * each), Slabs(2 * base, each, base)
+    got = Slabs(2 * base, each)
     flat, line = ((HEAD_DIM, channels), F32), ((count, LANES), F32)
     whole, small = ((channels, rows), BF16), ((16, rows), F32)
 
+    def message(pieces, height):
+        return ((pieces * height, LANES), F32)
+
     sent = call(
-        functools.partial(states_kernel, first, spaces),
-        [((spaces * pitch, LANES), F32)], [VMEM] * 2, [line],
+        functools.partial(states_kernel, outer, 2 * nx), [message(2 * nx, tall)], [VMEM] * 2, [line]
     )(k, v)
     sent = call(
-        functools.partial(sum_kernel, spaces, groups, pitch),
-        [((groups * pitch, LANES), F32)], [VMEM],
-    )(exchanged(sent, "space"))
+        functools.partial(to_rows_kernel, (nx, ny, base, pitch)), [message(ny, pitch)], [VMEM]
+    )(exchanged(sent, CHIP))
+    sent = call(
+        functools.partial(to_planes_kernel, nz, pitch), [message(nz, pitch)], [VMEM]
+    )(exchanged(sent, "y"))
     sent, rec, total = call(
-        functools.partial(denominator_kernel, groups, spaces, pitch, second),
-        [((spaces * 2 * base, LANES), F32), small, line], [SMEM] + [VMEM] * 3, [whole, whole],
-    )(mine, exchanged(sent, "tm"), q, g)
-    states = exchanged(sent, "space")
-    got = Slabs(2 * base, each)
+        functools.partial(denominator_kernel, nz, pitch, middle),
+        [message(2 * nx * ny, 2 * base), small, line], [SMEM] + [VMEM] * 3, [whole, whole],
+    )(mine, exchanged(sent, "z"), q, g)
+    states = exchanged(sent, PLANE)
     sent, mixed, sums = call(
-        functools.partial(attention_kernel, spaces, groups, pitch, got),
-        [((groups * pitch, LANES), F32), whole, small], [VMEM] * 4, [flat, line],
+        functools.partial(attention_kernel, nz, got),
+        [message(nz, short), whole, small], [VMEM] * 4, [flat, line],
     )(states, q, g, rec)
     sent = call(
-        functools.partial(suffix_kernel, groups, spaces, pitch),
-        [((spaces * pitch, LANES), F32)], [SMEM, VMEM],
-    )(mine, exchanged(sent, "tm"))
+        functools.partial(suffix_kernel, (nz, ny, base, short, pitch)),
+        [message(ny, pitch)], [SMEM, VMEM],
+    )(mine, exchanged(sent, "z"))
+    sent = call(
+        functools.partial(to_columns_kernel, (nx, ny, base, pitch)), [message(2 * nx, tall)], [VMEM]
+    )(exchanged(sent, "y"))
     grad_queries = call(
-        functools.partial(queries_kernel, got), [whole], [VMEM] * 6, [whole, whole],
+        functools.partial(queries_kernel, got), [whole], [VMEM] * 6, [whole, whole]
     )(states, q, g, rec, sums, total)
     grad_keys, values_gradient = call(
-        functools.partial(keys_kernel, spaces, first), [whole] * 2, [VMEM] * 3, [flat, whole, whole],
-    )(exchanged(sent, "space"), k, v)
+        functools.partial(keys_kernel, outer), [whole] * 2, [VMEM] * 3, [flat, whole, whole]
+    )(exchanged(sent, CHIP), k, v)
     return tuple(a.T[None] for a in (mixed, grad_queries, grad_keys, values_gradient))
 
 
 def solution(mesh):
-    placed = P("tm", "space", None)
+    groups, spaces = mesh.devices.shape
+    split = Mesh(
+        mesh.devices.reshape(groups // 2, 2, spaces // 8, 8), ("z", "core", "x", "y")
+    )
+    placed = P(("z", "core"), ("x", "y"), None)
     return jax.shard_map(
-        body, mesh=mesh, in_specs=(placed,) * 4, out_specs=(placed,) * 4, check_vma=False
+        body, mesh=split, in_specs=(placed,) * 4, out_specs=(placed,) * 4, check_vma=False
     )

time: 139 us -> 138 us (level)
  blocking collectives: 76.6 us -> 93.4 us
  waiting for transfers between devices: 32 us -> 17.3 us
  starting transfers between devices: 20.5 us -> 15.8 us
    all_to_all x3 -> x5, blocking collectives: 76.6 us -> 93.4 us  [exchanged(): return lax.all_to_all(pieces, axis, 0, 0, tiled=True).reshape(message.shape)]
    all_to_all x2, waiting for transfers between devices: 32 us -> 17.3 us  [exchanged(): return lax.all_to_all(pieces, axis, 0, 0, tiled=True).reshape(message.shape)]
    all_to_all x2, starting transfers between devices: 20.5 us -> 15.8 us  [exchanged(): return lax.all_to_all(pieces, axis, 0, 0, tiled=True).reshape(message.shape)]
    pallas_call x6 -> x8, Pallas kernels: 5.76 us -> 6.74 us  [the longest x1 1.64 us: body(): call(functools.partial(keys_kernel, outer), [whole] * 2, [VMEM] * 3, [fla...]
where the time goes in v3:
time: 138 us; the launch traced here: 137 us
  blocking collectives  93.4 us (68%)
  waiting for transfers between devices  17.3 us (13%)
  starting transfers between devices  15.8 us (11%)
  Pallas kernels  8.01 us (6%)
  local copies, waits for them, and re-layouts  1.93 us (1%)
    all_to_all x5, blocking collectives, exchanged(): return lax.all_to_all(pieces, axis, 0, 0, tiled=True).reshape(message.shape)  93.4 us
    all_to_all x2, waiting for transfers between devices, exchanged(): return lax.all_to_all(pieces, axis, 0, 0, tiled=True).reshape(message.shape)  17.3 us
    all_to_all x2, starting transfers between devices, exchanged(): return lax.all_to_all(pieces, axis, 0, 0, tiled=True).reshape(message.shape)  15.8 us
  transfers between devices with their start and end apart: 2, of which 2 were waited for; matrix products, arithmetic and copies ran while one was open for 0% of the time, Pallas kernels for 1%

profile of v3, /device:TPU:1, one launch (start us, length us, event | category | flops | bytes accessed | tf_op | source)
XLA Modules:
  0.0 137.2 jit_solution(18273804723636165979)
XLA Ops:
  0.6 0.0 copy-start.2
  0.6 0.9 copy-done.2
  1.6 0.0 copy-start.4
  1.6 1.0 copy-done.4
  2.6 0.4 shard_map.75
  3.0 19.5 %all_to_all.63 = f32[8,1,17536]{2,1,0:T(1,128)S(1)} all-to-all(f32[8,1,17536]{2,1,0:T(1,128)S(1)} %bitcast.50), channel_id=1, replica_groups=mesh['z'=8,'core'=2,'x'=4,'y'=8] {'core','x'}, dimensions={0} | all-to-all | bytes 1122304 | tf_op jit(solution)/shard_map/all_to_all | solution.py:342
  22.5 12.5 %all_to_all.64 = f32[8,1,6400]{2,1,0:T(1,128)S(1)} all-to-all(f32[8,1,6400]{2,1,0:T(1,128)S(1)} %bitcast.58), channel_id=1, replica_groups=mesh['z'=8,'core'=2,'x'=4,'y'=8] {'y'}, dimensions={0} | all-to-all | bytes 409600 | tf_op jit(solution)/shard_map/all_to_all | solution.py:342
  35.0 0.0 copy-start.1
  35.0 0.7 shard_map.77
  35.7 0.0 copy-start
  35.7 10.2 %all-to-all-start.2 = ((f32[8,1,6400]{2,1,0:T(1,128)}), f32[8,1,6400]{2,1,0:T(1,128)S(1)}, u32[]{:S(2)}, u32[]{:S(2)}) async-start(f32[8,1,6400]{2,1,0:T(1,128)} %bitcast.10), calls=%async_computation.2 | async-start | bytes 409600 | tf_op jit(solution)/shard_map/all_to_all | solution.py:342
  45.9 0.1 pad_add_fusion.mine_ref
  46.0 8.8 %all-to-all-done.2 = f32[8,1,6400]{2,1,0:T(1,128)S(1)} async-done(((f32[8,1,6400]{2,1,0:T(1,128)}), f32[8,1,6400]{2,1,0:T(1,128)S(1)}, u32[]{:S(2)}, u32[]{:S(2)}) %all-to-all-start.2) | async-done | bytes 204832 | tf_op jit(solution)/shard_map/all_to_all | solution.py:342
  54.8 0.0 copy-done.1
  54.8 0.0 copy-done
  54.8 1.3 shard_map.78
  56.1 36.6 %all_to_all.65 = f32[64,1,4096]{2,1,0:T(1,128)S(1)} all-to-all(f32[64,1,4096]{2,1,0:T(1,128)S(1)} %bitcast.55), channel_id=1, replica_groups=mesh['z'=8,'core'=2,'x'=4,'y'=8] {'core','x','y'}, dimensions={0} | all-to-all | bytes 2097152 | tf_op jit(solution)/shard_map/all_to_all | solution.py:342
  92.7 1.2 shard_map.79
  93.9 10.5 %all_to_all.66 = f32[8,1,5248]{2,1,0:T(1,128)S(1)} all-to-all(f32[8,1,5248]{2,1,0:T(1,128)S(1)} %bitcast.62), channel_id=1, replica_groups=mesh['z'=8,'core'=2,'x'=4,'y'=8] {'z'}, dimensions={0} | all-to-all | bytes 335872 | tf_op jit(solution)/shard_map/all_to_all | solution.py:342
  104.4 0.6 shard_map.81
  105.0 14.3 %all_to_all.67 = f32[8,1,6400]{2,1,0:T(1,128)S(1)} all-to-all(f32[8,1,6400]{2,1,0:T(1,128)S(1)} %bitcast.57), channel_id=1, replica_groups=mesh['z'=8,'core'=2,'x'=4,'y'=8] {'y'}, dimensions={0} | all-to-all | bytes 409600 | tf_op jit(solution)/shard_map/all_to_all | solution.py:342
  119.3 0.8 shard_map.82
  120.2 5.6 %all-to-all-start.6 = ((f32[8,1,17536]{2,1,0:T(1,128)}), f32[8,1,17536]{2,1,0:T(1,128)S(1)}, u32[]{:S(2)}, u32[]{:S(2)}) async-start(f32[8,1,17536]{2,1,0:T(1,128)} %bitcast.28), calls=%async_computation.6 | async-start | bytes 1122304 | tf_op jit(solution)/shard_map/all_to_all | solution.py:342
  125.8 0.0 copy-start.3
  125.8 0.0 copy-start.5
  125.8 1.3 shard_map.80
  127.1 8.5 %all-to-all-done.6 = f32[8,1,17536]{2,1,0:T(1,128)S(1)} async-done(((f32[8,1,17536]{2,1,0:T(1,128)}), f32[8,1,17536]{2,1,0:T(1,128)S(1)}, u32[]{:S(2)}, u32[]{:S(2)}) %all-to-all-start.6) | async-done | bytes 561184 | tf_op jit(solution)/shard_map/all_to_all | solution.py:342
  135.6 0.0 copy-done.3
  135.6 0.0 copy-done.5
  135.6 1.6 %shard_map.83 = (bf16[1120,128]{1,0:T(8,128)(2,1)}, bf16[1120,128]{1,0:T(8,128)(2,1)}) custom-call(f32[1096,128]{1,0:T(8,128)S(1)} %bitcast.48, bf16[1120,128]{1,0:T(8,128)(2,1)S(1)} %bitcast.52, bf16[1120,128]{1,0:T(8,128)(2,1)S(1)} %bitcast.54), custom_call_target="tpu_custom_call" | custom-call | flops 10000000 | bytes 1000000 | tf_op jit(solution)/shard_map/pallas_call | solution.py:393
  (1 shorter events, 0.0 us)
Async XLA Ops:
  0.6 1.0 copy-start.2
  1.6 1.0 copy-start.4
  35.0 19.7 %copy-start.1 = (bf16[1,128,1120]{1,2,0:T(8,128)(2,1)S(1)}, bf16[1,128,1120]{1,2,0:T(8,128)(2,1)}, u32[]{:S(2)}) copy-start(bf16[1,128,1120]{1,2,0:T(8,128)(2,1)} %param.7) | copy-start | bytes 860164
  35.7 19.0 %copy-start = (bf16[1,128,1120]{1,2,0:T(8,128)(2,1)S(1)}, bf16[1,128,1120]{1,2,0:T(8,128)(2,1)}, u32[]{:S(2)}) copy-start(bf16[1,128,1120]{1,2,0:T(8,128)(2,1)} %param.4) | copy-start | bytes 860164
  35.7 19.0 %all-to-all-start.2 = ((f32[8,1,6400]{2,1,0:T(1,128)}), f32[8,1,6400]{2,1,0:T(1,128)S(1)}, u32[]{:S(2)}, u32[]{:S(2)}) async-start(f32[8,1,6400]{2,1,0:T(1,128)} %bitcast.10), calls=%async_computation.2 | async-start | bytes 409600 | tf_op jit(solution)/shard_map/all_to_all | solution.py:342
  120.2 15.4 %all-to-all-start.6 = ((f32[8,1,17536]{2,1,0:T(1,128)}), f32[8,1,17536]{2,1,0:T(1,128)S(1)}, u32[]{:S(2)}, u32[]{:S(2)}) async-start(f32[8,1,17536]{2,1,0:T(1,128)} %bitcast.28), calls=%async_computation.6 | async-start | bytes 1122304 | tf_op jit(solution)/shard_map/all_to_all | solution.py:342
  125.8 9.8 %copy-start.3 = (bf16[1,128,1120]{1,2,0:T(8,128)(2,1)S(1)}, bf16[1,128,1120]{1,2,0:T(8,128)(2,1)}, u32[]{:S(2)}) copy-start(bf16[1,128,1120]{1,2,0:T(8,128)(2,1)} %param.5) | copy-start | bytes 860164
  125.8 9.8 %copy-start.5 = (bf16[1,128,1120]{1,2,0:T(8,128)(2,1)S(1)}, bf16[1,128,1120]{1,2,0:T(8,128)(2,1)}, u32[]{:S(2)}) copy-start(bf16[1,128,1120]{1,2,0:T(8,128)(2,1)} %param.6) | copy-start | bytes 860164

commit v4 on v3

--- a/solution.py
+++ b/solution.py
@@ -14,6 +14,7 @@
 F32, BF16 = jnp.float32, jnp.bfloat16
 VMEM = pl.BlockSpec(memory_space=pltpu.VMEM)
 SMEM = pl.BlockSpec(memory_space=pltpu.SMEM)
+HBM = pl.BlockSpec(memory_space=pltpu.HBM)
 NT = (((1,), (1,)), ((), ()))
 
 
@@ -119,19 +120,30 @@
     return jnp.concatenate([x, rest.astype(BF16)], axis=0)
 
 
-def states_kernel(slabs, pieces, k_ref, v_ref, out_ref, total_ref):
+def states_kernel(slabs, pieces, *refs):
+    loaded, (out_ref, *held, total_ref, sems) = refs[:4], refs[4:]
+    copies = [pltpu.make_async_copy(a, b, sems.at[i]) for i, (a, b) in enumerate(zip(loaded, held))]
+    for copy in copies:
+        copy.start()
+    k_ref, v_ref = held[:2]
     channels, rows = k_ref.shape
-    out_ref[...] = jnp.zeros_like(out_ref)
     total_ref[...] = jnp.zeros_like(total_ref)
+    last = out_ref.shape[0] - slabs.pitch
+    out_ref[last:, :] = jnp.zeros((slabs.pitch, LANES), F32)
     ones = jnp.ones((16, rows), BF16)
-    for t in tiles(channels):
-        keys = relu(k_ref[t.here, :])
-        slabs.put(out_ref, t, heads_apart(t, dot_rows(v_ref[t.pair, :], keys)))
-        total_ref[t.j : t.j + 1, : t.width] = dot_rows(ones, keys)[:1]
+    copies[0].wait()
+    for t in tiles(channels):
+        total_ref[t.j : t.j + 1, : t.width] = dot_rows(ones, relu(k_ref[t.here, :]))[:1]
     total = total_ref[...]
     for s in range(pieces):
         at = slabs.pitch * s + SLAB * slabs.each
         out_ref[at : at + len(total), :] = total
+    copies[1].wait()
+    for t in tiles(channels):
+        both = dot_rows(v_ref[t.pair, :], relu(k_ref[t.here, :]))
+        slabs.put(out_ref, t, heads_apart(t, both))
+    copies[2].wait()
+    copies[3].wait()
 
 
 def total_of(parts):
@@ -162,30 +174,33 @@
         out_ref[pitch * y + 2 * base : pitch * (y + 1), :] = totals
 
 
-def to_planes_kernel(pieces, pitch, in_ref, out_ref):
-    own = total_of(cut_rows(in_ref, pitch, s, 0, pitch) for s in range(pieces))
-    for s in range(pieces):
-        out_ref[pitch * s : pitch * (s + 1), :] = own
-
-
-def suffix_kernel(sizes, mine_ref, in_ref, out_ref):
-    planes, rows, base, height, pitch = sizes
+def to_planes_kernel(sizes, in_ref, out_ref, own_ref):
+    planes, base, pitch = sizes
+    size = (pitch - 2 * base) // 2
+    own = total_of(cut_rows(in_ref, pitch, s, 0, pitch) for s in range(in_ref.shape[0] // pitch))
+    own_ref[...] = own
+    first, second, low, high = own[:base], own[base : 2 * base], own[2 * base : -size], own[-size:]
+    message = jnp.concatenate([first + second, low + high], axis=0)
+    for p in range(planes):
+        out_ref[len(message) * p : len(message) * (p + 1), :] = message
+
+
+def suffix_kernel(sizes, mine_ref, in_ref, own_ref, out_ref):
+    planes, rows, base = sizes
     z, core = mine_ref[0], mine_ref[1]
-    size = height - 2 * base
-    early, late, shared, own = [], [], [], []
-    for p in range(planes):
-        first, second = (cut_rows(in_ref, height, p, base * c, base) for c in range(2))
-        part = cut_rows(in_ref, height, p, 2 * base, size)
-        both = jnp.where(p > z, first + second, 0.0)
-        early.append(both + jnp.where(p == z, first + second, 0.0))
-        late.append(both + jnp.where(p == z, second, 0.0))
-        shared.append(jnp.where(p >= z, part, 0.0))
-        own.append(jnp.where(p + core > z, part, 0.0))
+    height = in_ref.shape[0] // planes
+    after = total_of(
+        jnp.where(p > z, cut_rows(in_ref, height, p, 0, height), 0.0) for p in range(planes)
+    )
+    own = own_ref[...]
+    first, second, part = own[:base], own[base : 2 * base], own[2 * base :]
+    late = after[:base] + second
+    beyond = after[base:]
     message = jnp.concatenate(
-        [total_of(early), total_of(late), total_of(shared), total_of(own)], axis=0
+        [late + first, late, beyond + part, beyond + jnp.where(core > 0, part, 0.0)], axis=0
     )
     for s in range(rows):
-        out_ref[pitch * s : pitch * (s + 1), :] = message
+        out_ref[len(message) * s : len(message) * (s + 1), :] = message
 
 
 def to_columns_kernel(sizes, in_ref, out_ref):
@@ -223,28 +238,26 @@
         slabs.put(out_ref, t, heads_apart(t, both))
 
 
-def prefix(planes, pitch, base, mine_ref, in_ref):
+def prefix(planes, base, mine_ref, in_ref, own_ref):
     z, core = mine_ref[0], mine_ref[1]
-    size = (pitch - 2 * base) // 2
-    early, late, own = [], [], []
-    for p in range(planes):
-        first, second = (cut_rows(in_ref, pitch, p, base * c, base) for c in range(2))
-        low, high = (cut_rows(in_ref, pitch, p, 2 * base + size * c, size) for c in range(2))
-        both = jnp.where(p < z, first + second, 0.0)
-        early.append(both + jnp.where(p == z, first, 0.0))
-        late.append(both + jnp.where(p == z, first + second, 0.0))
-        own.append(jnp.where(p <= z, low, 0.0) + jnp.where(p < z + core, high, 0.0))
-    return total_of(early), total_of(late), total_of(own)
-
-
-def denominator_kernel(planes, pitch, slabs, mine_ref, in_ref, q_ref, g_ref, out_ref, rec_ref, total_ref, hi_ref, lo_ref):
-    out_ref[...] = jnp.zeros_like(out_ref)
-    early, late, total = prefix(planes, pitch, slabs.base, mine_ref, in_ref)
+    height = in_ref.shape[0] // planes
+    before = total_of(
+        jnp.where(p < z, cut_rows(in_ref, height, p, 0, height), 0.0) for p in range(planes)
+    )
+    own, size = own_ref[...], height - base
+    early = before[:base] + own[:base]
+    total = before[base:] + own[2 * base : -size] + jnp.where(core > 0, own[-size:], 0.0)
+    return early, early + own[base : 2 * base], total
+
+
+def denominator_kernel(planes, slabs, mine_ref, in_ref, own_ref, q_ref, g_ref, out_ref, rec_ref, total_ref, hi_ref, lo_ref):
+    early, late, total = prefix(planes, slabs.base, mine_ref, in_ref, own_ref)
     total_ref[...] = total
     rec = 1.0 / denominators(q_ref, total, rec_ref.shape[0])
     rec_ref[...] = rec
+    pieces = out_ref.shape[0] // slabs.pitch
+    out_ref[slabs.pitch * (pieces - 1) :, :] = jnp.zeros((slabs.pitch, LANES), F32)
     gradient_states(slabs, q_ref, g_ref, rec, out_ref, hi_ref, lo_ref)
-    pieces = out_ref.shape[0] // slabs.pitch
     for s in range(pieces):
         at = slabs.pitch * s
         out_ref[at : at + slabs.base, :] = early if 2 * s < pieces else late
@@ -268,7 +281,7 @@
         gt_ref[t.j : t.j + 1, : t.width] = jnp.sum(term, axis=0, keepdims=True)
 
 
-def attention_kernel(planes, slabs, in_ref, q_ref, g_ref, rec_ref, out_ref, mixed_ref, sums_ref, flat_ref, gt_ref):
+def attention_kernel(planes, slabs, in_ref, q_ref, g_ref, rec_ref, out_ref, own_ref, mixed_ref, sums_ref, flat_ref, gt_ref):
     attention(slabs, in_ref, q_ref, g_ref, rec_ref[...], mixed_ref, sums_ref, gt_ref, flat_ref)
     size = SLAB * slabs.each
     half = in_ref.shape[0] // slabs.pitch // 2
@@ -276,14 +289,16 @@
         total_of(cut_rows(in_ref, slabs.pitch, half * c + s, size, size) for s in range(half))
         for c in range(2)
     ]
-    message = jnp.concatenate([*sums, gt_ref[...]], axis=0)
-    height = len(message)
+    part = gt_ref[...]
+    own_ref[...] = jnp.concatenate([*sums, part], axis=0)
+    message = jnp.concatenate([sums[0] + sums[1], part], axis=0)
     for p in range(planes):
-        out_ref[height * p : height * (p + 1), :] = message
-
-
-def queries_kernel(slabs, in_ref, q_ref, g_ref, rec_ref, sums_ref, total_ref, out_ref, hi_ref, lo_ref):
+        out_ref[len(message) * p : len(message) * (p + 1), :] = message
+
+
+def queries_kernel(slabs, in_ref, q_ref, g_ref, rec_ref, sums_ref, total_ref, attn_ref, out_ref, mixed_ref, hi_ref, lo_ref):
     channels, rows = q_ref.shape
+    mixed_ref[...] = attn_ref[...]
     for t in tiles(channels):
         shape = (LANES - HEAD_DIM, t.width)
         extra = jnp.where(row(shape) < 2, jnp.broadcast_to(total_ref[t.j : t.j + 1, : t.width], shape), 0.0)
@@ -323,7 +338,7 @@
     keys(slabs, in_ref, total, k_ref, v_ref, gk_ref, gv_ref, flat_ref, hi_ref, lo_ref)
 
 
-def call(kernel, out, in_specs, scratch=(), flops=10**7, moved=10**6):
+def call(kernel, out, in_specs, scratch=(), more=(), flops=10**7, moved=10**6):
     shapes = [jax.ShapeDtypeStruct(s, d) for s, d in out]
     several = len(shapes) > 1
     return pl.pallas_call(
@@ -331,7 +346,7 @@
         out_shape=shapes if several else shapes[0],
         in_specs=in_specs,
         out_specs=[VMEM] * len(shapes) if several else VMEM,
-        scratch_shapes=[pltpu.VMEM(s, d) for s, d in scratch],
+        scratch_shapes=[pltpu.VMEM(s, d) for s, d in scratch] + list(more),
         cost_estimate=pl.CostEstimate(flops=flops, bytes_accessed=moved, transcendentals=0),
         compiler_params=pltpu.CompilerParams(vmem_limit_bytes=24 * 2**20),
     )
@@ -353,7 +368,7 @@
     count = len(tiles(channels))
     each = -(-count * (HEAD_DIM // SLAB) // (2 * nx * ny))
     base = SLAB * each
-    tall, pitch, short = ny * base + count, 2 * (base + count), 2 * base + count
+    tall, pitch, short = ny * base + count, 2 * (base + count), base + count
     outer, middle = Slabs(tall, ny * each), Slabs(2 * base, each, base)
     got = Slabs(2 * base, each)
     flat, line = ((HEAD_DIM, channels), F32), ((count, LANES), F32)
@@ -362,34 +377,36 @@
     def message(pieces, height):
         return ((pieces * height, LANES), F32)
 
-    sent = call(
-        functools.partial(states_kernel, outer, 2 * nx), [message(2 * nx, tall)], [VMEM] * 2, [line]
-    )(k, v)
+    sent, k, v, q, g = call(
+        functools.partial(states_kernel, outer, 2 * nx),
+        [message(2 * nx, tall)] + [whole] * 4, [HBM] * 4, [line], [pltpu.SemaphoreType.DMA((4,))],
+    )(*(pltpu.with_memory_space_constraint(a, pltpu.HBM) for a in (k, v, q, g)))
     sent = call(
         functools.partial(to_rows_kernel, (nx, ny, base, pitch)), [message(ny, pitch)], [VMEM]
     )(exchanged(sent, CHIP))
-    sent = call(
-        functools.partial(to_planes_kernel, nz, pitch), [message(nz, pitch)], [VMEM]
+    sent, own = call(
+        functools.partial(to_planes_kernel, (nz, base, pitch)),
+        [message(nz, short), message(1, pitch)], [VMEM],
     )(exchanged(sent, "y"))
     sent, rec, total = call(
-        functools.partial(denominator_kernel, nz, pitch, middle),
-        [message(2 * nx * ny, 2 * base), small, line], [SMEM] + [VMEM] * 3, [whole, whole],
-    )(mine, exchanged(sent, "z"), q, g)
+        functools.partial(denominator_kernel, nz, middle),
+        [message(2 * nx * ny, 2 * base), small, line], [SMEM] + [VMEM] * 4, [whole, whole],
+    )(mine, exchanged(sent, "z"), own, q, g)
     states = exchanged(sent, PLANE)
-    sent, mixed, sums = call(
+    sent, own, attn, sums = call(
         functools.partial(attention_kernel, nz, got),
-        [message(nz, short), whole, small], [VMEM] * 4, [flat, line],
+        [message(nz, short), message(1, base + short), whole, small], [VMEM] * 4, [flat, line],
     )(states, q, g, rec)
+    grad_queries, mixed = call(
+        functools.partial(queries_kernel, got), [whole] * 2, [VMEM] * 7, [whole, whole]
+    )(states, q, g, rec, sums, total, attn)
+    sent, grad_queries = lax.optimization_barrier((exchanged(sent, "z"), grad_queries))
     sent = call(
-        functools.partial(suffix_kernel, (nz, ny, base, short, pitch)),
-        [message(ny, pitch)], [SMEM, VMEM],
-    )(mine, exchanged(sent, "z"))
+        functools.partial(suffix_kernel, (nz, ny, base)), [message(ny, pitch)], [SMEM, VMEM, VMEM]
+    )(mine, sent, own)
     sent = call(
         functools.partial(to_columns_kernel, (nx, ny, base, pitch)), [message(2 * nx, tall)], [VMEM]
     )(exchanged(sent, "y"))
-    grad_queries = call(
-        functools.partial(queries_kernel, got), [whole], [VMEM] * 6, [whole, whole]
-    )(states, q, g, rec, sums, total)
     grad_keys, values_gradient = call(
         functools.partial(keys_kernel, outer), [whole] * 2, [VMEM] * 3, [flat, whole, whole]
     )(exchanged(sent, CHIP), k, v)

time: 138 us -> 134 us (0.971)
  waiting for transfers between devices: 17.3 us -> 13.9 us
  blocking collectives: 93.4 us -> 96.6 us
  starting transfers between devices: 15.8 us -> 13.4 us
  local copies, waits for them, and re-layouts: 1.93 us -> 0 us
    all_to_all x2, waiting for transfers between devices: 17.3 us -> 13.9 us  [exchanged(): return lax.all_to_all(pieces, axis, 0, 0, tiled=True).reshape(message.shape)]
    all_to_all x5, blocking collectives: 93.4 us -> 96.6 us  [exchanged(): return lax.all_to_all(pieces, axis, 0, 0, tiled=True).reshape(message.shape)]
    all_to_all x2, starting transfers between devices: 15.8 us -> 13.4 us  [exchanged(): return lax.all_to_all(pieces, axis, 0, 0, tiled=True).reshape(message.shape)]
    unnamed x12 -> x0, local copies, waits for them, and re-layouts: 1.93 us -> none
where the time goes in v4:
time: 134 us; the launch traced here: 133 us
  blocking collectives  96.6 us (72%)
  waiting for transfers between devices  13.9 us (10%)
  starting transfers between devices  13.4 us (10%)
  Pallas kernels  8.54 us (6%)
    all_to_all x5, blocking collectives, exchanged(): return lax.all_to_all(pieces, axis, 0, 0, tiled=True).reshape(message.shape)  96.6 us
    all_to_all x2, waiting for transfers between devices, exchanged(): return lax.all_to_all(pieces, axis, 0, 0, tiled=True).reshape(message.shape)  13.9 us
    all_to_all x2, starting transfers between devices, exchanged(): return lax.all_to_all(pieces, axis, 0, 0, tiled=True).reshape(message.shape)  13.4 us
  transfers between devices with their start and end apart: 2, of which 2 were waited for; matrix products, arithmetic and copies ran while one was open for 0% of the time, Pallas kernels for 1%

profile of v4, /device:TPU:1, one launch (start us, length us, event | category | flops | bytes accessed | tf_op | source)
XLA Modules:
  0.0 133.2 jit_solution(1358157261063776900)
XLA Ops:
  0.6 1.6 %shard_map.75 = (f32[1096,128]{1,0:T(8,128)S(1)}, bf16[1120,128]{1,0:T(8,128)(2,1)S(1)}, bf16[1120,128]{1,0:T(8,128)(2,1)S(1)}, bf16[1120,128]{1,0:T(8,128)(2,1)S(1)}, bf16[1120,128]{1,0:T(8,128)(2,1)S(1)}) custom-call(bf16[1120,128]{1,0:T(8,128)(2,1)} %bitcast.53, bf16[1120,128]{1,0:T(8,128)(2,1)} %bitcast.54, bf16[1120,128]{1,0:T(8,128)(2,1)} %bitcast.55, ...), custom_call_target="tpu_custom_call" | custom-call | flops 10000000 | bytes 1000000 | tf_op jit(solution)/shard_map/pallas_call | solution.py:380
  2.3 19.5 %all_to_all.63 = f32[8,1,17536]{2,1,0:T(1,128)S(1)} all-to-all(f32[8,1,17536]{2,1,0:T(1,128)S(1)} %bitcast.50), channel_id=1, replica_groups=mesh['z'=8,'core'=2,'x'=4,'y'=8] {'core','x'}, dimensions={0} | all-to-all | bytes 1122304 | tf_op jit(solution)/shard_map/all_to_all | solution.py:357
  21.7 12.5 %all_to_all.64 = f32[8,1,6400]{2,1,0:T(1,128)S(1)} all-to-all(f32[8,1,6400]{2,1,0:T(1,128)S(1)} %bitcast.47), channel_id=1, replica_groups=mesh['z'=8,'core'=2,'x'=4,'y'=8] {'y'}, dimensions={0} | all-to-all | bytes 409600 | tf_op jit(solution)/shard_map/all_to_all | solution.py:357
  34.3 0.7 shard_map.77
  34.9 10.0 %all-to-all-start.2 = ((f32[8,1,3200]{2,1,0:T(1,128)}), f32[8,1,3200]{2,1,0:T(1,128)S(1)}, u32[]{:S(2)}, u32[]{:S(2)}) async-start(f32[8,1,3200]{2,1,0:T(1,128)} %bitcast.14), calls=%async_computation.2 | async-start | bytes 204800 | tf_op jit(solution)/shard_map/all_to_all | solution.py:357
  45.0 0.1 pad_add_fusion.mine_ref
  45.1 7.6 %all-to-all-done.2 = f32[8,1,3200]{2,1,0:T(1,128)S(1)} async-done(((f32[8,1,3200]{2,1,0:T(1,128)}), f32[8,1,3200]{2,1,0:T(1,128)S(1)}, u32[]{:S(2)}, u32[]{:S(2)}) %all-to-all-start.2) | async-done | bytes 102432 | tf_op jit(solution)/shard_map/all_to_all | solution.py:357
  52.6 1.3 shard_map.78
  53.9 36.5 %all_to_all.65 = f32[64,1,4096]{2,1,0:T(1,128)S(1)} all-to-all(f32[64,1,4096]{2,1,0:T(1,128)S(1)} %bitcast.45), channel_id=1, replica_groups=mesh['z'=8,'core'=2,'x'=4,'y'=8] {'core','x','y'}, dimensions={0} | all-to-all | bytes 2097152 | tf_op jit(solution)/shard_map/all_to_all | solution.py:357
  90.4 1.4 %shard_map.79 = (f32[200,128]{1,0:T(8,128)}, f32[41,128]{1,0:T(8,128)S(1)}, bf16[1120,128]{1,0:T(8,128)(2,1)S(1)}, f32[16,128]{1,0:T(8,128)S(1)}) custom-call(f32[2048,128]{1,0:T(8,128)S(1)} %bitcast.40, bf16[1120,128]{1,0:T(8,128)(2,1)S(1)} %get-tuple-element.27.q_ref, bf16[1120,128]{1,0:T(8,128)(2,1)S(1)} %get-tuple-element.28.g_ref, ...), custom_call_target="tpu_custom_call" | custom-call | flops 10000000 | bytes 1000000 | tf_op jit(solution)/shard_map/pallas_call | solution.py:396
  91.8 3.4 %all-to-all-start.4 = ((f32[8,1,3200]{2,1,0:T(1,128)}), f32[8,1,3200]{2,1,0:T(1,128)S(1)}, u32[]{:S(2)}, u32[]{:S(2)}) async-start(f32[8,1,3200]{2,1,0:T(1,128)} %bitcast.20), calls=%async_computation.4 | async-start | bytes 204800 | tf_op jit(solution)/shard_map/all_to_all | solution.py:357
  95.2 1.3 shard_map.80
  96.5 6.3 %all-to-all-done.4 = f32[8,1,3200]{2,1,0:T(1,128)S(1)} async-done(((f32[8,1,3200]{2,1,0:T(1,128)}), f32[8,1,3200]{2,1,0:T(1,128)S(1)}, u32[]{:S(2)}, u32[]{:S(2)}) %all-to-all-start.4) | async-done | bytes 102432 | tf_op jit(solution)/shard_map/all_to_all | solution.py:357
  102.8 0.6 shard_map.81
  103.4 12.8 %all_to_all.66 = f32[8,1,6400]{2,1,0:T(1,128)S(1)} all-to-all(f32[8,1,6400]{2,1,0:T(1,128)S(1)} %bitcast.49), channel_id=1, replica_groups=mesh['z'=8,'core'=2,'x'=4,'y'=8] {'y'}, dimensions={0} | all-to-all | bytes 409600 | tf_op jit(solution)/shard_map/all_to_all | solution.py:357
  116.3 15.2 %all_to_all.67 = f32[8,1,17536]{2,1,0:T(1,128)S(1)} all-to-all(f32[8,1,17536]{2,1,0:T(1,128)S(1)} %bitcast.44), channel_id=1, replica_groups=mesh['z'=8,'core'=2,'x'=4,'y'=8] {'core','x'}, dimensions={0} | all-to-all | bytes 1122304 | tf_op jit(solution)/shard_map/all_to_all | solution.py:357
  131.5 1.6 %shard_map.83 = (bf16[1120,128]{1,0:T(8,128)(2,1)}, bf16[1120,128]{1,0:T(8,128)(2,1)}) custom-call(f32[1096,128]{1,0:T(8,128)S(1)} %bitcast.42, bf16[1120,128]{1,0:T(8,128)(2,1)S(1)} %get-tuple-element.40.k_ref, bf16[1120,128]{1,0:T(8,128)(2,1)S(1)} %get-tuple-element.41.v_ref), custom_call_target="tpu_custom_call" | custom-call | flops 10000000 | bytes 1000000 | tf_op jit(solution)/shard_map/pallas_call | solution.py:410
  (2 shorter events, 0.1 us)
Async XLA Ops:
  34.9 17.7 %all-to-all-start.2 = ((f32[8,1,3200]{2,1,0:T(1,128)}), f32[8,1,3200]{2,1,0:T(1,128)S(1)}, u32[]{:S(2)}, u32[]{:S(2)}) async-start(f32[8,1,3200]{2,1,0:T(1,128)} %bitcast.14), calls=%async_computation.2 | async-start | bytes 204800 | tf_op jit(solution)/shard_map/all_to_all | solution.py:357
  91.8 11.0 %all-to-all-start.4 = ((f32[8,1,3200]{2,1,0:T(1,128)}), f32[8,1,3200]{2,1,0:T(1,128)S(1)}, u32[]{:S(2)}, u32[]{:S(2)}) async-start(f32[8,1,3200]{2,1,0:T(1,128)} %bitcast.20), calls=%async_computation.4 | async-start | bytes 204800 | tf_op jit(solution)/shard_map/all_to_all | solution.py:357

commit v5 on v4

--- a/solution.py
+++ b/solution.py
@@ -2,18 +2,23 @@
 
 import jax
 import jax.numpy as jnp
+import numpy as np
 from jax import lax
 from jax.experimental import pallas as pl
 from jax.experimental.pallas import tpu as pltpu
 from jax.sharding import Mesh
 from jax.sharding import PartitionSpec as P
 
+PLANES = (0, 1, 7, 2, 6, 3, 5, 4)
+ROWS = (0, 4, 2, 6, 1, 5, 3, 7)
+CHIP = tuple((n % 2, n // 2) for n in (1, 6, 5, 4, 7, 0, 2, 3))
+PLANE = tuple((c, x, y) for c in range(2) for y in PLANES for x in (0, 1, 3, 2))
+
 HEAD_DIM = 112
 LANES = 128
 SLAB = 8
 F32, BF16 = jnp.float32, jnp.bfloat16
 VMEM = pl.BlockSpec(memory_space=pltpu.VMEM)
-SMEM = pl.BlockSpec(memory_space=pltpu.SMEM)
 HBM = pl.BlockSpec(memory_space=pltpu.HBM)
 NT = (((1,), (1,)), ((), ()))
 
@@ -41,6 +46,11 @@
     return lax.dot_general(a, b, (((1,), (1,)), ((), ())), preferred_element_type=F32)
 
 
+def both_halves(by, hi, lo, rhs):
+    out = by(jnp.concatenate([hi, lo], axis=0), rhs)
+    return out[: len(hi)] + out[len(hi) :]
+
+
 def halves(x):
     hi = x.astype(BF16)
     return hi, (x - hi.astype(F32)).astype(BF16)
@@ -82,13 +92,15 @@
 
 
 class Slabs:
-    def __init__(self, pitch, each, base=0):
-        self.pitch, self.each, self.base = pitch, each, base
+    def __init__(self, pitch, each, base=0, places=None):
+        self.pitch, self.each, self.base, self.places = pitch, each, base, places
 
     def rows(self, tile):
         for i in range(HEAD_DIM // SLAB):
             number = HEAD_DIM // SLAB * tile.j + i
-            at = self.pitch * (number // self.each) + self.base + SLAB * (number % self.each)
+            piece = number // self.each
+            piece = piece if self.places is None else self.places[piece]
+            at = self.pitch * piece + self.base + SLAB * (number % self.each)
             yield slice(SLAB * i, SLAB * (i + 1)), slice(at, at + SLAB)
 
     def put(self, ref, tile, value):
@@ -107,8 +119,7 @@
     s = flat_ref[:, start:stop]
     c = lane(s.shape) + start
     hi, lo = halves(jnp.where((c >= HEAD_DIM * h) & (c < HEAD_DIM * (h + 1)), s, 0.0))
-    rhs = relu(rows_ref[start:stop, :])
-    return dot(hi, rhs) + dot(lo, rhs)
+    return both_halves(dot, hi, lo, relu(rows_ref[start:stop, :]))
 
 
 def turn(tile, state, extra, hi_ref, lo_ref):
@@ -123,8 +134,8 @@
 def states_kernel(slabs, pieces, *refs):
     loaded, (out_ref, *held, total_ref, sems) = refs[:4], refs[4:]
     copies = [pltpu.make_async_copy(a, b, sems.at[i]) for i, (a, b) in enumerate(zip(loaded, held))]
-    for copy in copies:
-        copy.start()
+    copies[0].start()
+    copies[1].start()
     k_ref, v_ref = held[:2]
     channels, rows = k_ref.shape
     total_ref[...] = jnp.zeros_like(total_ref)
@@ -132,6 +143,8 @@
     out_ref[last:, :] = jnp.zeros((slabs.pitch, LANES), F32)
     ones = jnp.ones((16, rows), BF16)
     copies[0].wait()
+    copies[2].start()
+    copies[3].start()
     for t in tiles(channels):
         total_ref[t.j : t.j + 1, : t.width] = dot_rows(ones, relu(k_ref[t.here, :]))[:1]
     total = total_ref[...]
@@ -160,10 +173,10 @@
 
 
 def to_rows_kernel(sizes, in_ref, out_ref):
-    chips, rows, base, pitch = sizes
-    height = in_ref.shape[0] // (2 * chips)
+    rows, base, pitch = sizes
+    height = in_ref.shape[0] // len(CHIP)
     sums = [
-        total_of(cut_rows(in_ref, height, chips * c + x, 0, height) for x in range(chips))
+        total_of(cut_rows(in_ref, height, s, 0, height) for s, d in enumerate(CHIP) if d[0] == c)
         for c in range(2)
     ]
     totals = jnp.concatenate([s[rows * base :] for s in sums], axis=0)
@@ -185,12 +198,11 @@
         out_ref[len(message) * p : len(message) * (p + 1), :] = message
 
 
-def suffix_kernel(sizes, mine_ref, in_ref, own_ref, out_ref):
-    planes, rows, base = sizes
-    z, core = mine_ref[0], mine_ref[1]
-    height = in_ref.shape[0] // planes
+def suffix_kernel(rows, base, in_ref, own_ref, out_ref):
+    z, core = lax.axis_index("z"), lax.axis_index("core")
+    height = in_ref.shape[0] // len(PLANES)
     after = total_of(
-        jnp.where(p > z, cut_rows(in_ref, height, p, 0, height), 0.0) for p in range(planes)
+        jnp.where(p > z, cut_rows(in_ref, height, s, 0, height), 0.0) for s, p in enumerate(PLANES)
     )
     own = own_ref[...]
     first, second, part = own[:base], own[base : 2 * base], own[2 * base :]
@@ -204,7 +216,7 @@
 
 
 def to_columns_kernel(sizes, in_ref, out_ref):
-    chips, rows, base, pitch = sizes
+    rows, base, pitch = sizes
     size = (pitch - 2 * base) // 2
     height = rows * base + size
     for c in range(2):
@@ -213,9 +225,9 @@
             total_of(cut_rows(in_ref, pitch, y, 2 * base + size * c, size) for y in range(rows))
         )
         message = jnp.concatenate(parts, axis=0)
-        for x in range(chips):
-            at = height * (chips * c + x)
-            out_ref[at : at + height, :] = message
+        for s, d in enumerate(CHIP):
+            if d[0] == c:
+                out_ref[height * s : height * (s + 1), :] = message
 
 
 def denominators(q_ref, total, padded):
@@ -234,15 +246,15 @@
         hi_ref[of_head(h), :], lo_ref[of_head(h), :] = hi, lo
     for t in tiles(channels):
         rhs = relu(q_ref[t.here, :])
-        both = dot_rows(hi_ref[t.pair, :], rhs) + dot_rows(lo_ref[t.pair, :], rhs)
+        both = both_halves(dot_rows, hi_ref[t.pair, :], lo_ref[t.pair, :], rhs)
         slabs.put(out_ref, t, heads_apart(t, both))
 
 
-def prefix(planes, base, mine_ref, in_ref, own_ref):
-    z, core = mine_ref[0], mine_ref[1]
-    height = in_ref.shape[0] // planes
+def prefix(base, in_ref, own_ref):
+    z, core = lax.axis_index("z"), lax.axis_index("core")
+    height = in_ref.shape[0] // len(PLANES)
     before = total_of(
-        jnp.where(p < z, cut_rows(in_ref, height, p, 0, height), 0.0) for p in range(planes)
+        jnp.where(p < z, cut_rows(in_ref, height, s, 0, height), 0.0) for s, p in enumerate(PLANES)
     )
     own, size = own_ref[...], height - base
     early = before[:base] + own[:base]
@@ -250,17 +262,18 @@
     return early, early + own[base : 2 * base], total
 
 
-def denominator_kernel(planes, slabs, mine_ref, in_ref, own_ref, q_ref, g_ref, out_ref, rec_ref, total_ref, hi_ref, lo_ref):
-    early, late, total = prefix(planes, slabs.base, mine_ref, in_ref, own_ref)
+def denominator_kernel(slabs, in_ref, own_ref, q_ref, g_ref, out_ref, rec_ref, total_ref, hi_ref, lo_ref):
+    early, late, total = prefix(slabs.base, in_ref, own_ref)
     total_ref[...] = total
     rec = 1.0 / denominators(q_ref, total, rec_ref.shape[0])
     rec_ref[...] = rec
     pieces = out_ref.shape[0] // slabs.pitch
-    out_ref[slabs.pitch * (pieces - 1) :, :] = jnp.zeros((slabs.pitch, LANES), F32)
+    spare = slabs.pitch * slabs.places[pieces - 1]
+    out_ref[spare : spare + slabs.pitch, :] = jnp.zeros((slabs.pitch, LANES), F32)
     gradient_states(slabs, q_ref, g_ref, rec, out_ref, hi_ref, lo_ref)
     for s in range(pieces):
         at = slabs.pitch * s
-        out_ref[at : at + slabs.base, :] = early if 2 * s < pieces else late
+        out_ref[at : at + slabs.base, :] = late if PLANE[s][0] else early
 
 
 def attention(slabs, in_ref, q_ref, g_ref, rec, mixed_ref, sums_ref, gt_ref, flat_ref):
@@ -284,9 +297,8 @@
 def attention_kernel(planes, slabs, in_ref, q_ref, g_ref, rec_ref, out_ref, own_ref, mixed_ref, sums_ref, flat_ref, gt_ref):
     attention(slabs, in_ref, q_ref, g_ref, rec_ref[...], mixed_ref, sums_ref, gt_ref, flat_ref)
     size = SLAB * slabs.each
-    half = in_ref.shape[0] // slabs.pitch // 2
     sums = [
-        total_of(cut_rows(in_ref, slabs.pitch, half * c + s, size, size) for s in range(half))
+        total_of(cut_rows(in_ref, slabs.pitch, s, size, size) for s, d in enumerate(PLANE) if d[0] == c)
         for c in range(2)
     ]
     part = gt_ref[...]
@@ -309,7 +321,7 @@
         rest = jnp.where(row(shape) == 0, jnp.broadcast_to(hi.astype(F32), shape), 0.0)
         rest = jnp.where(row(shape) == 1, jnp.broadcast_to(lo.astype(F32), shape), rest)
         rhs = with_rows(g_ref[of_head(h), :], rest)
-        feature = (dot(hi_ref[of_head(h), :], rhs) + dot(lo_ref[of_head(h), :], rhs)) * rec_ref[h : h + 1, :]
+        feature = both_halves(dot, hi_ref[of_head(h), :], lo_ref[of_head(h), :], rhs) * rec_ref[h : h + 1, :]
         q = q_ref[of_head(h), :].astype(F32)
         out_ref[of_head(h), :] = jnp.where(q > 0, feature, 0.0).astype(BF16)
 
@@ -326,7 +338,7 @@
     for h in range(channels // HEAD_DIM):
         gv_ref[of_head(h), :] = by_state(flat_ref, k_ref, h).astype(BF16)
         rhs = with_rows(v_ref[of_head(h), :], ones)
-        grad = dot(hi_ref[of_head(h), :], rhs) + dot(lo_ref[of_head(h), :], rhs)
+        grad = both_halves(dot, hi_ref[of_head(h), :], lo_ref[of_head(h), :], rhs)
         k = k_ref[of_head(h), :].astype(F32)
         gk_ref[of_head(h), :] = jnp.where(k > 0, grad, 0.0).astype(BF16)
 
@@ -352,25 +364,37 @@
     )
 
 
-def exchanged(message, axis):
-    pieces = message.reshape(lax.axis_size(axis), -1)
-    return lax.all_to_all(pieces, axis, 0, 0, tiled=True).reshape(message.shape)
-
-
-CHIP, PLANE = ("core", "x"), ("core", "x", "y")
+def exchanged(message, axes, order):
+    sizes = [lax.axis_size(a) for a in axes]
+    order = [int(np.ravel_multi_index(d, sizes)) for d in order]
+    pieces = message.reshape(len(order), -1)
+    pieces = lax.all_to_all(pieces, axes, 0, 0, tiled=True, axis_index_groups=[order])
+    return pieces.reshape(message.shape)
+
+
+def over_chips(message):
+    return exchanged(message, ("core", "x"), CHIP)
+
+
+def over_rows(message):
+    return exchanged(message, ("y",), [(y,) for y in ROWS])
+
+
+def over_planes(message):
+    return exchanged(message, ("z",), [(z,) for z in PLANES])
 
 
 def body(queries, keys_in, values_in, grad_attn):
     q, k, v, g = (a[0].T for a in (queries, keys_in, values_in, grad_attn))
     channels, rows = q.shape
     nx, ny, nz = (lax.axis_size(a) for a in ("x", "y", "z"))
-    mine = jnp.stack([lax.axis_index("z"), lax.axis_index("core")]).astype(jnp.int32)
     count = len(tiles(channels))
     each = -(-count * (HEAD_DIM // SLAB) // (2 * nx * ny))
     base = SLAB * each
     tall, pitch, short = ny * base + count, 2 * (base + count), base + count
-    outer, middle = Slabs(tall, ny * each), Slabs(2 * base, each, base)
-    got = Slabs(2 * base, each)
+    places = [PLANE.index((*chip, y)) for chip in CHIP for y in ROWS]
+    outer, middle = Slabs(tall, ny * each), Slabs(2 * base, each, base, places)
+    got = Slabs(2 * base, each, 0, places)
     flat, line = ((HEAD_DIM, channels), F32), ((count, LANES), F32)
     whole, small = ((channels, rows), BF16), ((16, rows), F32)
 
@@ -382,17 +406,17 @@
         [message(2 * nx, tall)] + [whole] * 4, [HBM] * 4, [line], [pltpu.SemaphoreType.DMA((4,))],
     )(*(pltpu.with_memory_space_constraint(a, pltpu.HBM) for a in (k, v, q, g)))
     sent = call(
-        functools.partial(to_rows_kernel, (nx, ny, base, pitch)), [message(ny, pitch)], [VMEM]
-    )(exchanged(sent, CHIP))
+        functools.partial(to_rows_kernel, (ny, base, pitch)), [message(ny, pitch)], [VMEM]
+    )(over_chips(sent))
     sent, own = call(
         functools.partial(to_planes_kernel, (nz, base, pitch)),
         [message(nz, short), message(1, pitch)], [VMEM],
-    )(exchanged(sent, "y"))
+    )(over_rows(sent))
     sent, rec, total = call(
-        functools.partial(denominator_kernel, nz, middle),
-        [message(2 * nx * ny, 2 * base), small, line], [SMEM] + [VMEM] * 4, [whole, whole],
-    )(mine, exchanged(sent, "z"), own, q, g)
-    states = exchanged(sent, PLANE)
+        functools.partial(denominator_kernel, middle),
+        [message(2 * nx * ny, 2 * base), small, line], [VMEM] * 4, [whole, whole],
+    )(over_planes(sent), own, q, g)
+    states = exchanged(sent, ("core", "x", "y"), PLANE)
     sent, own, attn, sums = call(
         functools.partial(attention_kernel, nz, got),
         [message(nz, short), message(1, base + short), whole, small], [VMEM] * 4, [flat, line],
@@ -400,16 +424,16 @@
     grad_queries, mixed = call(
         functools.partial(queries_kernel, got), [whole] * 2, [VMEM] * 7, [whole, whole]
     )(states, q, g, rec, sums, total, attn)
-    sent, grad_queries = lax.optimization_barrier((exchanged(sent, "z"), grad_queries))
+    sent, grad_queries = lax.optimization_barrier((over_planes(sent), grad_queries))
     sent = call(
-        functools.partial(suffix_kernel, (nz, ny, base)), [message(ny, pitch)], [SMEM, VMEM, VMEM]
-    )(mine, sent, own)
+        functools.partial(suffix_kernel, ny, base), [message(ny, pitch)], [VMEM] * 2
+    )(sent, own)
     sent = call(
-        functools.partial(to_columns_kernel, (nx, ny, base, pitch)), [message(2 * nx, tall)], [VMEM]
-    )(exchanged(sent, "y"))
+        functools.partial(to_columns_kernel, (ny, base, pitch)), [message(2 * nx, tall)], [VMEM]
+    )(over_rows(sent))
     grad_keys, values_gradient = call(
         functools.partial(keys_kernel, outer), [whole] * 2, [VMEM] * 3, [flat, whole, whole]
-    )(exchanged(sent, CHIP), k, v)
+    )(over_chips(sent), k, v)
     return tuple(a.T[None] for a in (mixed, grad_queries, grad_keys, values_gradient))
 
 

time: 134 us -> 128 us (0.955)
  blocking collectives: 96.6 us -> 109 us
  starting transfers between devices: 13.4 us -> 3.36 us
  waiting for transfers between devices: 13.9 us -> 7.45 us
  Pallas kernels: 8.54 us -> 6.9 us
    all_to_all x5 -> x6, blocking collectives: 96.6 us -> 109 us  [exchanged(): lax.all_to_all(pieces, axes, 0, 0, tiled=True, axis_index_groups=[order])]
    all_to_all x2 -> x1, starting transfers between devices: 13.4 us -> 3.36 us  [exchanged(): lax.all_to_all(pieces, axes, 0, 0, tiled=True, axis_index_groups=[order])]
    all_to_all x2 -> x1, waiting for transfers between devices: 13.9 us -> 7.45 us  [exchanged(): lax.all_to_all(pieces, axes, 0, 0, tiled=True, axis_index_groups=[order])]
  transfers between devices with their start and end apart: 2 -> 1, of which waited for: 2 -> 1; matrix products, arithmetic and copies ran while one was open for 0% -> 0% of each run, Pallas kernels for 1% -> 1%
where the time goes in v5:
time: 128 us
  blocking collectives  109 us (85%)
  waiting for transfers between devices  7.45 us (6%)
  Pallas kernels  6.9 us (5%)
  starting transfers between devices  3.36 us (3%)
    all_to_all x6, blocking collectives, exchanged(): lax.all_to_all(pieces, axes, 0, 0, tiled=True, axis_index_groups=[order])  109 us
    all_to_all x1, waiting for transfers between devices, exchanged(): lax.all_to_all(pieces, axes, 0, 0, tiled=True, axis_index_groups=[order])  7.45 us
    all_to_all x1, starting transfers between devices, exchanged(): lax.all_to_all(pieces, axes, 0, 0, tiled=True, axis_index_groups=[order])  3.36 us
  transfers between devices with their start and end apart: 1, of which 1 were waited for; matrix products, arithmetic and copies ran while one was open for 0% of the time, Pallas kernels for 1%

profile of v5, /device:TPU:1, one launch (start us, length us, event | category | flops | bytes accessed | tf_op | source)
XLA Modules:
  0.0 127.6 jit_solution(6673498897283439701)
XLA Ops:
  0.6 2.1 %shard_map.75 = (f32[1096,128]{1,0:T(8,128)S(1)}, bf16[1120,128]{1,0:T(8,128)(2,1)S(1)}, bf16[1120,128]{1,0:T(8,128)(2,1)S(1)}, bf16[1120,128]{1,0:T(8,128)(2,1)S(1)}, bf16[1120,128]{1,0:T(8,128)(2,1)S(1)}) custom-call(bf16[1120,128]{1,0:T(8,128)(2,1)} %bitcast.52, bf16[1120,128]{1,0:T(8,128)(2,1)} %bitcast.53, bf16[1120,128]{1,0:T(8,128)(2,1)} %bitcast.54, ...), custom_call_target="tpu_custom_call" | custom-call | flops 10000000 | bytes 1000000 | tf_op jit(solution)/shard_map/pallas_call | solution.py:404
  2.7 18.3 %all_to_all.63 = f32[8,1,17536]{2,1,0:T(1,128)S(1)} all-to-all(f32[8,1,17536]{2,1,0:T(1,128)S(1)} %bitcast.48), channel_id=1, replica_groups={{32,24,48,16,56,0,8,40},{33,25,49,17,57,1,9,41},{34,26,50,18,58,2,10,42..., dimensions={0} | all-to-all | bytes 1122304 | tf_op jit(solution)/shard_map/all_to_all | solution.py:371
  21.0 10.7 %all_to_all.64 = f32[8,1,6400]{2,1,0:T(1,128)S(1)} all-to-all(f32[8,1,6400]{2,1,0:T(1,128)S(1)} %bitcast.45), channel_id=1, replica_groups={{0,4,2,6,1,5,3,7},{8,12,10,14,9,13,11,15},{16,20,18,22,17,21,19,23},{24..., dimensions={0} | all-to-all | bytes 409600 | tf_op jit(solution)/shard_map/all_to_all | solution.py:371
  31.8 17.5 %all_to_all.65 = f32[8,1,3200]{2,1,0:T(1,128)S(1)} all-to-all(f32[8,1,3200]{2,1,0:T(1,128)S(1)} %bitcast.51), channel_id=1, replica_groups={{0,64,448,128,384,192,320,256},{1,65,449,129,385,193,321,257},{2,66,450..., dimensions={0} | all-to-all | bytes 204800 | tf_op jit(solution)/shard_map/all_to_all | solution.py:371
  49.2 0.7 shard_map.78
  50.0 37.9 %all_to_all.66 = f32[64,1,4096]{2,1,0:T(1,128)S(1)} all-to-all(f32[64,1,4096]{2,1,0:T(1,128)S(1)} %bitcast.43), channel_id=1, replica_groups={{0,8,24,16,1,9,25,17,7,15,31,23,2,10,26,18,6,14,30,22,3,11,27,19,5,13,2..., dimensions={0} | all-to-all | bytes 2097152 | tf_op jit(solution)/shard_map/all_to_all | solution.py:371
  87.9 1.4 %shard_map.79 = (f32[200,128]{1,0:T(8,128)}, f32[41,128]{1,0:T(8,128)S(1)}, bf16[1120,128]{1,0:T(8,128)(2,1)S(1)}, f32[16,128]{1,0:T(8,128)S(1)}) custom-call(f32[2048,128]{1,0:T(8,128)S(1)} %bitcast.38, bf16[1120,128]{1,0:T(8,128)(2,1)S(1)} %get-tuple-element.27.q_ref, bf16[1120,128]{1,0:T(8,128)(2,1)S(1)} %get-tuple-element.28.g_ref, ...), custom_call_target="tpu_custom_call" | custom-call | flops 10000000 | bytes 1000000 | tf_op jit(solution)/shard_map/pallas_call | solution.py:420
  89.2 3.4 %all-to-all-start.4 = ((f32[8,1,3200]{2,1,0:T(1,128)}), f32[8,1,3200]{2,1,0:T(1,128)S(1)}, u32[]{:S(2)}, u32[]{:S(2)}) async-start(f32[8,1,3200]{2,1,0:T(1,128)} %bitcast.18), calls=%async_computation.4 | async-start | bytes 204800 | tf_op jit(solution)/shard_map/all_to_all | solution.py:371
  92.6 1.2 shard_map.80
  93.8 7.4 %all-to-all-done.4 = f32[8,1,3200]{2,1,0:T(1,128)S(1)} async-done(((f32[8,1,3200]{2,1,0:T(1,128)}), f32[8,1,3200]{2,1,0:T(1,128)S(1)}, u32[]{:S(2)}, u32[]{:S(2)}) %all-to-all-start.4) | async-done | bytes 102432 | tf_op jit(solution)/shard_map/all_to_all | solution.py:371
  101.3 9.4 %all_to_all.67 = f32[8,1,6400]{2,1,0:T(1,128)S(1)} all-to-all(f32[8,1,6400]{2,1,0:T(1,128)S(1)} %bitcast.47), channel_id=1, replica_groups={{0,4,2,6,1,5,3,7},{8,12,10,14,9,13,11,15},{16,20,18,22,17,21,19,23},{24..., dimensions={0} | all-to-all | bytes 409600 | tf_op jit(solution)/shard_map/all_to_all | solution.py:371
  110.7 15.4 %all_to_all.68 = f32[8,1,17536]{2,1,0:T(1,128)S(1)} all-to-all(f32[8,1,17536]{2,1,0:T(1,128)S(1)} %bitcast.42), channel_id=1, replica_groups={{32,24,48,16,56,0,8,40},{33,25,49,17,57,1,9,41},{34,26,50,18,58,2,10,42..., dimensions={0} | all-to-all | bytes 1122304 | tf_op jit(solution)/shard_map/all_to_all | solution.py:371
  126.2 1.4 %shard_map.83 = (bf16[1120,128]{1,0:T(8,128)(2,1)}, bf16[1120,128]{1,0:T(8,128)(2,1)}) custom-call(f32[1096,128]{1,0:T(8,128)S(1)} %bitcast.40, bf16[1120,128]{1,0:T(8,128)(2,1)S(1)} %get-tuple-element.40.k_ref, bf16[1120,128]{1,0:T(8,128)(2,1)S(1)} %get-tuple-element.41.v_ref), custom_call_target="tpu_custom_call" | custom-call | flops 10000000 | bytes 1000000 | tf_op jit(solution)/shard_map/pallas_call | solution.py:434
  (4 shorter events, 0.1 us)
Async XLA Ops:
  89.2 12.0 %all-to-all-start.4 = ((f32[8,1,3200]{2,1,0:T(1,128)}), f32[8,1,3200]{2,1,0:T(1,128)S(1)}, u32[]{:S(2)}, u32[]{:S(2)}) async-start(f32[8,1,3200]{2,1,0:T(1,128)} %bitcast.18), calls=%async_computation.4 | async-start | bytes 204800 | tf_op jit(solution)/shard_map/all_to_all | solution.py:371

commit v6 on v5

--- a/solution.py
+++ b/solution.py
@@ -112,14 +112,17 @@
         return jnp.concatenate(parts, axis=0)
 
 
-def by_state(flat_ref, rows_ref, h):
-    channels = flat_ref.shape[1]
-    start = HEAD_DIM * h // LANES * LANES
-    stop = min(channels, -(-HEAD_DIM * (h + 1) // LANES) * LANES)
-    s = flat_ref[:, start:stop]
-    c = lane(s.shape) + start
-    hi, lo = halves(jnp.where((c >= HEAD_DIM * h) & (c < HEAD_DIM * (h + 1)), s, 0.0))
-    return both_halves(dot, hi, lo, relu(rows_ref[start:stop, :]))
+def keep_halves(tile, state, hi_ref, lo_ref):
+    hi_ref[:, tile.here], lo_ref[:, tile.here] = halves(state)
+
+
+def by_state(hi_ref, lo_ref, rows_ref, h):
+    channels, low, high = hi_ref.shape[1], HEAD_DIM * h, HEAD_DIM * (h + 1)
+    start, stop = low // LANES * LANES, min(channels, -(-high // LANES) * LANES)
+    own = relu(rows_ref[low:high, :])
+    parts = [jnp.zeros((n, own.shape[1]), BF16) for n in (low - start, stop - high)]
+    rhs = jnp.concatenate([p for p in (parts[0], own, parts[1]) if len(p)], axis=0)
+    return both_halves(dot, hi_ref[:, start:stop], lo_ref[:, start:stop], rhs)
 
 
 def turn(tile, state, extra, hi_ref, lo_ref):
@@ -134,8 +137,8 @@
 def states_kernel(slabs, pieces, *refs):
     loaded, (out_ref, *held, total_ref, sems) = refs[:4], refs[4:]
     copies = [pltpu.make_async_copy(a, b, sems.at[i]) for i, (a, b) in enumerate(zip(loaded, held))]
-    copies[0].start()
-    copies[1].start()
+    for copy in copies:
+        copy.start()
     k_ref, v_ref = held[:2]
     channels, rows = k_ref.shape
     total_ref[...] = jnp.zeros_like(total_ref)
@@ -143,8 +146,6 @@
     out_ref[last:, :] = jnp.zeros((slabs.pitch, LANES), F32)
     ones = jnp.ones((16, rows), BF16)
     copies[0].wait()
-    copies[2].start()
-    copies[3].start()
     for t in tiles(channels):
         total_ref[t.j : t.j + 1, : t.width] = dot_rows(ones, relu(k_ref[t.here, :]))[:1]
     total = total_ref[...]
@@ -276,15 +277,15 @@
         out_ref[at : at + slabs.base, :] = late if PLANE[s][0] else early
 
 
-def attention(slabs, in_ref, q_ref, g_ref, rec, mixed_ref, sums_ref, gt_ref, flat_ref):
+def attention(slabs, in_ref, q_ref, g_ref, rec, mixed_ref, sums_ref, gt_ref, *flat):
     channels = q_ref.shape[0]
     padded = rec.shape[0]
     for t in tiles(channels):
-        flat_ref[:, t.here] = slabs.get(in_ref, t)
+        keep_halves(t, slabs.get(in_ref, t), *flat)
     sums_ref[...] = jnp.zeros_like(sums_ref)
     gt_ref[...] = jnp.zeros_like(gt_ref)
     for h in range(channels // HEAD_DIM):
-        attn = by_state(flat_ref, q_ref, h) * rec[h : h + 1]
+        attn = by_state(*flat, q_ref, h) * rec[h : h + 1]
         mixed_ref[of_head(h), :] = attn.astype(BF16)
         sums_ref[h : h + 1, :] = jnp.sum(g_ref[of_head(h), :].astype(F32) * attn, axis=0, keepdims=True)
     pair = jnp.concatenate(halves(-sums_ref[...] * rec), axis=0)
@@ -294,8 +295,8 @@
         gt_ref[t.j : t.j + 1, : t.width] = jnp.sum(term, axis=0, keepdims=True)
 
 
-def attention_kernel(planes, slabs, in_ref, q_ref, g_ref, rec_ref, out_ref, own_ref, mixed_ref, sums_ref, flat_ref, gt_ref):
-    attention(slabs, in_ref, q_ref, g_ref, rec_ref[...], mixed_ref, sums_ref, gt_ref, flat_ref)
+def attention_kernel(planes, slabs, in_ref, q_ref, g_ref, rec_ref, out_ref, own_ref, mixed_ref, sums_ref, flat_hi_ref, flat_lo_ref, gt_ref):
+    attention(slabs, in_ref, q_ref, g_ref, rec_ref[...], mixed_ref, sums_ref, gt_ref, flat_hi_ref, flat_lo_ref)
     size = SLAB * slabs.each
     sums = [
         total_of(cut_rows(in_ref, slabs.pitch, s, size, size) for s, d in enumerate(PLANE) if d[0] == c)
@@ -326,28 +327,29 @@
         out_ref[of_head(h), :] = jnp.where(q > 0, feature, 0.0).astype(BF16)
 
 
-def keys(slabs, in_ref, total, k_ref, v_ref, gk_ref, gv_ref, flat_ref, hi_ref, lo_ref):
+def keys(slabs, in_ref, total, k_ref, v_ref, gk_ref, gv_ref, flat, hi_ref, lo_ref):
     channels, rows = k_ref.shape
     for t in tiles(channels):
         shape = (LANES - HEAD_DIM, t.width)
         extra = jnp.where(row(shape) < 1, jnp.broadcast_to(total[t.j : t.j + 1, : t.width], shape), 0.0)
         state = slabs.get(in_ref, t)
-        flat_ref[:, t.here] = state
+        keep_halves(t, state, *flat)
         turn(t, state, extra, hi_ref, lo_ref)
     ones = jnp.ones((LANES - HEAD_DIM, rows), BF16)
     for h in range(channels // HEAD_DIM):
-        gv_ref[of_head(h), :] = by_state(flat_ref, k_ref, h).astype(BF16)
+        gv_ref[of_head(h), :] = by_state(*flat, k_ref, h).astype(BF16)
         rhs = with_rows(v_ref[of_head(h), :], ones)
         grad = both_halves(dot, hi_ref[of_head(h), :], lo_ref[of_head(h), :], rhs)
         k = k_ref[of_head(h), :].astype(F32)
         gk_ref[of_head(h), :] = jnp.where(k > 0, grad, 0.0).astype(BF16)
 
 
-def keys_kernel(slabs, in_ref, k_ref, v_ref, gk_ref, gv_ref, flat_ref, hi_ref, lo_ref):
+def keys_kernel(slabs, in_ref, k_ref, v_ref, gk_ref, gv_ref, flat_hi_ref, flat_lo_ref, hi_ref, lo_ref):
     base = SLAB * slabs.each
     pieces = in_ref.shape[0] // slabs.pitch
     total = total_of(cut_rows(in_ref, slabs.pitch, s, base, slabs.pitch - base) for s in range(pieces))
-    keys(slabs, in_ref, total, k_ref, v_ref, gk_ref, gv_ref, flat_ref, hi_ref, lo_ref)
+    flat = flat_hi_ref, flat_lo_ref
+    keys(slabs, in_ref, total, k_ref, v_ref, gk_ref, gv_ref, flat, hi_ref, lo_ref)
 
 
 def call(kernel, out, in_specs, scratch=(), more=(), flops=10**7, moved=10**6):
@@ -395,7 +397,7 @@
     places = [PLANE.index((*chip, y)) for chip in CHIP for y in ROWS]
     outer, middle = Slabs(tall, ny * each), Slabs(2 * base, each, base, places)
     got = Slabs(2 * base, each, 0, places)
-    flat, line = ((HEAD_DIM, channels), F32), ((count, LANES), F32)
+    flat, line = ((HEAD_DIM, channels), BF16), ((count, LANES), F32)
     whole, small = ((channels, rows), BF16), ((16, rows), F32)
 
     def message(pieces, height):
@@ -419,20 +421,20 @@
     states = exchanged(sent, ("core", "x", "y"), PLANE)
     sent, own, attn, sums = call(
         functools.partial(attention_kernel, nz, got),
-        [message(nz, short), message(1, base + short), whole, small], [VMEM] * 4, [flat, line],
+        [message(nz, short), message(1, base + short), whole, small], [VMEM] * 4, [flat, flat, line],
     )(states, q, g, rec)
     grad_queries, mixed = call(
         functools.partial(queries_kernel, got), [whole] * 2, [VMEM] * 7, [whole, whole]
     )(states, q, g, rec, sums, total, attn)
-    sent, grad_queries = lax.optimization_barrier((over_planes(sent), grad_queries))
+    sent, grad_queries = lax.optimization_barrier((sent, grad_queries))
     sent = call(
         functools.partial(suffix_kernel, ny, base), [message(ny, pitch)], [VMEM] * 2
-    )(sent, own)
+    )(over_planes(sent), own)
     sent = call(
         functools.partial(to_columns_kernel, (ny, base, pitch)), [message(2 * nx, tall)], [VMEM]
     )(over_rows(sent))
     grad_keys, values_gradient = call(
-        functools.partial(keys_kernel, outer), [whole] * 2, [VMEM] * 3, [flat, whole, whole]
+        functools.partial(keys_kernel, outer), [whole] * 2, [VMEM] * 3, [flat, flat, whole, whole]
     )(over_chips(sent), k, v)
     return tuple(a.T[None] for a in (mixed, grad_queries, grad_keys, values_gradient))
 

time: 128 us -> 127 us (level)
  blocking collectives: 109 us -> 120 us
  waiting for transfers between devices: 7.45 us -> 0 us
  starting transfers between devices: 3.36 us -> 0 us
    all_to_all x6 -> x7, blocking collectives: 109 us -> 120 us  [exchanged(): lax.all_to_all(pieces, axes, 0, 0, tiled=True, axis_index_groups=[order])]
    all_to_all x1 -> x0, waiting for transfers between devices: 7.45 us -> none  [exchanged(): lax.all_to_all(pieces, axes, 0, 0, tiled=True, axis_index_groups=[order])]
    all_to_all x1 -> x0, starting transfers between devices: 3.36 us -> none  [exchanged(): lax.all_to_all(pieces, axes, 0, 0, tiled=True, axis_index_groups=[order])]
  transfers between devices with their start and end apart: 1 -> 0, of which waited for: 1 -> 0; matrix products, arithmetic and copies ran while one was open for 0% -> 0% of each run, Pallas kernels for 1% -> 0%
where the time goes in v6:
time: 127 us
  blocking collectives  120 us (94%)
  Pallas kernels  5.76 us (5%)
    all_to_all x7, blocking collectives, exchanged(): lax.all_to_all(pieces, axes, 0, 0, tiled=True, axis_index_groups=[order])  120 us

profile of v6, /device:TPU:1, one launch (start us, length us, event | category | flops | bytes accessed | tf_op | source)
XLA Modules:
  0.0 126.7 jit_solution(14132316163242532737)
XLA Ops:
  0.6 1.6 %shard_map.75 = (f32[1096,128]{1,0:T(8,128)S(1)}, bf16[1120,128]{1,0:T(8,128)(2,1)S(1)}, bf16[1120,128]{1,0:T(8,128)(2,1)S(1)}, bf16[1120,128]{1,0:T(8,128)(2,1)S(1)}, bf16[1120,128]{1,0:T(8,128)(2,1)S(1)}) custom-call(bf16[1120,128]{1,0:T(8,128)(2,1)} %bitcast.53, bf16[1120,128]{1,0:T(8,128)(2,1)} %bitcast.54, bf16[1120,128]{1,0:T(8,128)(2,1)} %bitcast.55, ...), custom_call_target="tpu_custom_call" | custom-call | flops 10000000 | bytes 1000000 | tf_op jit(solution)/shard_map/pallas_call | solution.py:406
  2.3 18.3 %all_to_all.63 = f32[8,1,17536]{2,1,0:T(1,128)S(1)} all-to-all(f32[8,1,17536]{2,1,0:T(1,128)S(1)} %bitcast.48), channel_id=1, replica_groups={{32,24,48,16,56,0,8,40},{33,25,49,17,57,1,9,41},{34,26,50,18,58,2,10,42..., dimensions={0} | all-to-all | bytes 1122304 | tf_op jit(solution)/shard_map/all_to_all | solution.py:373
  20.6 10.7 %all_to_all.64 = f32[8,1,6400]{2,1,0:T(1,128)S(1)} all-to-all(f32[8,1,6400]{2,1,0:T(1,128)S(1)} %bitcast.45), channel_id=1, replica_groups={{0,4,2,6,1,5,3,7},{8,12,10,14,9,13,11,15},{16,20,18,22,17,21,19,23},{24..., dimensions={0} | all-to-all | bytes 409600 | tf_op jit(solution)/shard_map/all_to_all | solution.py:373
  31.3 17.5 %all_to_all.65 = f32[8,1,3200]{2,1,0:T(1,128)S(1)} all-to-all(f32[8,1,3200]{2,1,0:T(1,128)S(1)} %bitcast.52), channel_id=1, replica_groups={{0,64,448,128,384,192,320,256},{1,65,449,129,385,193,321,257},{2,66,450..., dimensions={0} | all-to-all | bytes 204800 | tf_op jit(solution)/shard_map/all_to_all | solution.py:373
  48.8 0.7 shard_map.78
  49.5 37.9 %all_to_all.66 = f32[64,1,4096]{2,1,0:T(1,128)S(1)} all-to-all(f32[64,1,4096]{2,1,0:T(1,128)S(1)} %bitcast.43), channel_id=1, replica_groups={{0,8,24,16,1,9,25,17,7,15,31,23,2,10,26,18,6,14,30,22,3,11,27,19,5,13,2..., dimensions={0} | all-to-all | bytes 2097152 | tf_op jit(solution)/shard_map/all_to_all | solution.py:373
  87.4 0.7 shard_map.79
  88.1 1.2 shard_map.80
  89.3 11.1 %all_to_all.67 = f32[8,1,3200]{2,1,0:T(1,128)S(1)} all-to-all(f32[8,1,3200]{2,1,0:T(1,128)S(1)} %bitcast.51), channel_id=1, replica_groups={{0,64,448,128,384,192,320,256},{1,65,449,129,385,193,321,257},{2,66,450..., dimensions={0} | all-to-all | bytes 204800 | tf_op jit(solution)/shard_map/all_to_all | solution.py:373
  100.4 9.3 %all_to_all.68 = f32[8,1,6400]{2,1,0:T(1,128)S(1)} all-to-all(f32[8,1,6400]{2,1,0:T(1,128)S(1)} %bitcast.47), channel_id=1, replica_groups={{0,4,2,6,1,5,3,7},{8,12,10,14,9,13,11,15},{16,20,18,22,17,21,19,23},{24..., dimensions={0} | all-to-all | bytes 409600 | tf_op jit(solution)/shard_map/all_to_all | solution.py:373
  109.8 15.5 %all_to_all.69 = f32[8,1,17536]{2,1,0:T(1,128)S(1)} all-to-all(f32[8,1,17536]{2,1,0:T(1,128)S(1)} %bitcast.42), channel_id=1, replica_groups={{32,24,48,16,56,0,8,40},{33,25,49,17,57,1,9,41},{34,26,50,18,58,2,10,42..., dimensions={0} | all-to-all | bytes 1122304 | tf_op jit(solution)/shard_map/all_to_all | solution.py:373
  125.3 1.4 %shard_map.83 = (bf16[1120,128]{1,0:T(8,128)(2,1)}, bf16[1120,128]{1,0:T(8,128)(2,1)}) custom-call(f32[1096,128]{1,0:T(8,128)S(1)} %bitcast.40, bf16[1120,128]{1,0:T(8,128)(2,1)S(1)} %get-tuple-element.40.k_ref, bf16[1120,128]{1,0:T(8,128)(2,1)S(1)} %get-tuple-element.41.v_ref), custom_call_target="tpu_custom_call" | custom-call | flops 10000000 | bytes 1000000 | tf_op jit(solution)/shard_map/pallas_call | solution.py:436
  (4 shorter events, 0.1 us)

commit v7 on v6

--- a/solution.py
+++ b/solution.py
@@ -11,8 +11,8 @@
 
 PLANES = (0, 1, 7, 2, 6, 3, 5, 4)
 ROWS = (0, 4, 2, 6, 1, 5, 3, 7)
-CHIP = tuple((n % 2, n // 2) for n in (1, 6, 5, 4, 7, 0, 2, 3))
-PLANE = tuple((c, x, y) for c in range(2) for y in PLANES for x in (0, 1, 3, 2))
+FULL_ROWS = (0, 4, 1, 5, 2, 6, 3, 7)
+CHIP = tuple((n % 2, n // 2) for n in (5, 0, 6, 4, 1, 7, 2, 3))
 
 HEAD_DIM = 112
 LANES = 128
@@ -92,15 +92,12 @@
 
 
 class Slabs:
-    def __init__(self, pitch, each, base=0, places=None):
-        self.pitch, self.each, self.base, self.places = pitch, each, base, places
+    def __init__(self, start):
+        self.start = start
 
     def rows(self, tile):
         for i in range(HEAD_DIM // SLAB):
-            number = HEAD_DIM // SLAB * tile.j + i
-            piece = number // self.each
-            piece = piece if self.places is None else self.places[piece]
-            at = self.pitch * piece + self.base + SLAB * (number % self.each)
+            at = self.start(HEAD_DIM // SLAB * tile.j + i)
             yield slice(SLAB * i, SLAB * (i + 1)), slice(at, at + SLAB)
 
     def put(self, ref, tile, value):
@@ -134,7 +131,7 @@
     return jnp.concatenate([x, rest.astype(BF16)], axis=0)
 
 
-def states_kernel(slabs, pieces, *refs):
+def states_kernel(slabs, height, *refs):
     loaded, (out_ref, *held, total_ref, sems) = refs[:4], refs[4:]
     copies = [pltpu.make_async_copy(a, b, sems.at[i]) for i, (a, b) in enumerate(zip(loaded, held))]
     for copy in copies:
@@ -142,16 +139,16 @@
     k_ref, v_ref = held[:2]
     channels, rows = k_ref.shape
     total_ref[...] = jnp.zeros_like(total_ref)
-    last = out_ref.shape[0] - slabs.pitch
-    out_ref[last:, :] = jnp.zeros((slabs.pitch, LANES), F32)
+    pieces = out_ref.shape[0] // height
+    out_ref[height * (pieces - 1) :, :] = jnp.zeros((height, LANES), F32)
     ones = jnp.ones((16, rows), BF16)
     copies[0].wait()
     for t in tiles(channels):
         total_ref[t.j : t.j + 1, : t.width] = dot_rows(ones, relu(k_ref[t.here, :]))[:1]
     total = total_ref[...]
     for s in range(pieces):
-        at = slabs.pitch * s + SLAB * slabs.each
-        out_ref[at : at + len(total), :] = total
+        at = height * (s + 1)
+        out_ref[at - len(total) : at, :] = total
     copies[1].wait()
     for t in tiles(channels):
         both = dot_rows(v_ref[t.pair, :], relu(k_ref[t.here, :]))
@@ -263,18 +260,34 @@
     return early, early + own[base : 2 * base], total
 
 
-def denominator_kernel(slabs, in_ref, own_ref, q_ref, g_ref, out_ref, rec_ref, total_ref, hi_ref, lo_ref):
-    early, late, total = prefix(slabs.base, in_ref, own_ref)
+def denominator_kernel(base, slabs, in_ref, own_ref, q_ref, g_ref, out_ref, rec_ref, total_ref, hi_ref, lo_ref):
+    early, late, total = prefix(base, in_ref, own_ref)
     total_ref[...] = total
     rec = 1.0 / denominators(q_ref, total, rec_ref.shape[0])
     rec_ref[...] = rec
-    pieces = out_ref.shape[0] // slabs.pitch
-    spare = slabs.pitch * slabs.places[pieces - 1]
-    out_ref[spare : spare + slabs.pitch, :] = jnp.zeros((slabs.pitch, LANES), F32)
+    pieces = len(FULL_ROWS)
+    height = out_ref.shape[0] // pieces
+    out_ref[-base:, :] = jnp.zeros((base, LANES), F32)
     gradient_states(slabs, q_ref, g_ref, rec, out_ref, hi_ref, lo_ref)
     for s in range(pieces):
-        at = slabs.pitch * s
-        out_ref[at : at + slabs.base, :] = late if PLANE[s][0] else early
+        out_ref[height * s : height * s + base, :] = early
+        out_ref[height * s + base : height * s + 2 * base, :] = late
+
+
+def cross_kernel(base, in_ref, out_ref):
+    pieces = len(FULL_ROWS)
+    height = in_ref.shape[0] // pieces
+    size = pieces * base
+    order = [FULL_ROWS.index(y) for y in ROWS]
+    states = [
+        jnp.concatenate([cut_rows(in_ref, height, s, base * c, base) for s in order], axis=0)
+        for c in range(2)
+    ]
+    share = total_of(cut_rows(in_ref, height, s, 2 * base, size) for s in range(pieces))
+    for s, d in enumerate(CHIP):
+        at = (size + base) * s
+        out_ref[at : at + size, :] = states[d[0]]
+        out_ref[at + size : at + size + base, :] = share[base * s : base * (s + 1)]
 
 
 def attention(slabs, in_ref, q_ref, g_ref, rec, mixed_ref, sums_ref, gt_ref, *flat):
@@ -295,11 +308,11 @@
         gt_ref[t.j : t.j + 1, : t.width] = jnp.sum(term, axis=0, keepdims=True)
 
 
-def attention_kernel(planes, slabs, in_ref, q_ref, g_ref, rec_ref, out_ref, own_ref, mixed_ref, sums_ref, flat_hi_ref, flat_lo_ref, gt_ref):
+def attention_kernel(planes, base, slabs, in_ref, q_ref, g_ref, rec_ref, out_ref, own_ref, mixed_ref, sums_ref, flat_hi_ref, flat_lo_ref, gt_ref):
     attention(slabs, in_ref, q_ref, g_ref, rec_ref[...], mixed_ref, sums_ref, gt_ref, flat_hi_ref, flat_lo_ref)
-    size = SLAB * slabs.each
+    height = in_ref.shape[0] // len(CHIP)
     sums = [
-        total_of(cut_rows(in_ref, slabs.pitch, s, size, size) for s, d in enumerate(PLANE) if d[0] == c)
+        total_of(cut_rows(in_ref, height, s, height - base, base) for s, d in enumerate(CHIP) if d[0] == c)
         for c in range(2)
     ]
     part = gt_ref[...]
@@ -345,9 +358,9 @@
 
 
 def keys_kernel(slabs, in_ref, k_ref, v_ref, gk_ref, gv_ref, flat_hi_ref, flat_lo_ref, hi_ref, lo_ref):
-    base = SLAB * slabs.each
-    pieces = in_ref.shape[0] // slabs.pitch
-    total = total_of(cut_rows(in_ref, slabs.pitch, s, base, slabs.pitch - base) for s in range(pieces))
+    pieces = len(CHIP)
+    height, count = in_ref.shape[0] // pieces, len(tiles(k_ref.shape[0]))
+    total = total_of(cut_rows(in_ref, height, s, height - count, count) for s in range(pieces))
     flat = flat_hi_ref, flat_lo_ref
     keys(slabs, in_ref, total, k_ref, v_ref, gk_ref, gv_ref, flat, hi_ref, lo_ref)
 
@@ -378,8 +391,8 @@
     return exchanged(message, ("core", "x"), CHIP)
 
 
-def over_rows(message):
-    return exchanged(message, ("y",), [(y,) for y in ROWS])
+def over_rows(message, order=ROWS):
+    return exchanged(message, ("y",), [(y,) for y in order])
 
 
 def over_planes(message):
@@ -393,10 +406,18 @@
     count = len(tiles(channels))
     each = -(-count * (HEAD_DIM // SLAB) // (2 * nx * ny))
     base = SLAB * each
-    tall, pitch, short = ny * base + count, 2 * (base + count), base + count
-    places = [PLANE.index((*chip, y)) for chip in CHIP for y in ROWS]
-    outer, middle = Slabs(tall, ny * each), Slabs(2 * base, each, base, places)
-    got = Slabs(2 * base, each, 0, places)
+    size = ny * base
+    tall, pitch, short = size + count, 2 * (base + count), base + count
+    wide, full = 2 * base + size, size + base
+
+    def in_turn(height, first=0):
+        return Slabs(lambda n: height * (n // (ny * each)) + first + SLAB * (n % (ny * each)))
+
+    def last(n):
+        row, chip = FULL_ROWS[n // (ny * each)], n % (ny * each) // each
+        return tall * chip + base * ROWS.index(row) + SLAB * (n % each)
+
+    outer, got = in_turn(tall), in_turn(full)
     flat, line = ((HEAD_DIM, channels), BF16), ((count, LANES), F32)
     whole, small = ((channels, rows), BF16), ((16, rows), F32)
 
@@ -404,7 +425,7 @@
         return ((pieces * height, LANES), F32)
 
     sent, k, v, q, g = call(
-        functools.partial(states_kernel, outer, 2 * nx),
+        functools.partial(states_kernel, outer, tall),
         [message(2 * nx, tall)] + [whole] * 4, [HBM] * 4, [line], [pltpu.SemaphoreType.DMA((4,))],
     )(*(pltpu.with_memory_space_constraint(a, pltpu.HBM) for a in (k, v, q, g)))
     sent = call(
@@ -415,12 +436,15 @@
         [message(nz, short), message(1, pitch)], [VMEM],
     )(over_rows(sent))
     sent, rec, total = call(
-        functools.partial(denominator_kernel, middle),
-        [message(2 * nx * ny, 2 * base), small, line], [VMEM] * 4, [whole, whole],
+        functools.partial(denominator_kernel, base, in_turn(wide, 2 * base)),
+        [message(ny, wide), small, line], [VMEM] * 4, [whole, whole],
     )(over_planes(sent), own, q, g)
-    states = exchanged(sent, ("core", "x", "y"), PLANE)
+    sent = call(
+        functools.partial(cross_kernel, base), [message(2 * nx, full)], [VMEM]
+    )(over_rows(sent, FULL_ROWS))
+    states = over_chips(sent)
     sent, own, attn, sums = call(
-        functools.partial(attention_kernel, nz, got),
+        functools.partial(attention_kernel, nz, base, got),
         [message(nz, short), message(1, base + short), whole, small], [VMEM] * 4, [flat, flat, line],
     )(states, q, g, rec)
     grad_queries, mixed = call(
@@ -434,7 +458,7 @@
         functools.partial(to_columns_kernel, (ny, base, pitch)), [message(2 * nx, tall)], [VMEM]
     )(over_rows(sent))
     grad_keys, values_gradient = call(
-        functools.partial(keys_kernel, outer), [whole] * 2, [VMEM] * 3, [flat, flat, whole, whole]
+        functools.partial(keys_kernel, Slabs(last)), [whole] * 2, [VMEM] * 3, [flat, flat, whole, whole]
     )(over_chips(sent), k, v)
     return tuple(a.T[None] for a in (mixed, grad_queries, grad_keys, values_gradient))
 

time: 127 us -> 123 us (0.969)
  blocking collectives: 120 us -> 117 us
    all_to_all x7 -> x8, blocking collectives: 120 us -> 117 us  [exchanged(): lax.all_to_all(pieces, axes, 0, 0, tiled=True, axis_index_groups=[order])]
    pallas_call x4 -> x5, Pallas kernels: 4.44 us -> 4.43 us  [the longest x1 1.61 us: body(): call(functools.partial(states_kernel, outer, tall), [message(2 * nx, tall...]
where the time goes in v7:
time: 123 us
  blocking collectives  117 us (95%)
  Pallas kernels  5.74 us (5%)
    all_to_all x8, blocking collectives, exchanged(): lax.all_to_all(pieces, axes, 0, 0, tiled=True, axis_index_groups=[order])  117 us

profile of v7, /device:TPU:1, one launch (start us, length us, event | category | flops | bytes accessed | tf_op | source)
XLA Modules:
  0.0 123.1 jit_solution(6690597184361275935)
XLA Ops:
  0.6 1.6 %shard_map.75 = (f32[1096,128]{1,0:T(8,128)S(1)}, bf16[1120,128]{1,0:T(8,128)(2,1)S(1)}, bf16[1120,128]{1,0:T(8,128)(2,1)S(1)}, bf16[1120,128]{1,0:T(8,128)(2,1)S(1)}, bf16[1120,128]{1,0:T(8,128)(2,1)S(1)}) custom-call(bf16[1120,128]{1,0:T(8,128)(2,1)} %bitcast.57, bf16[1120,128]{1,0:T(8,128)(2,1)} %bitcast.58, bf16[1120,128]{1,0:T(8,128)(2,1)} %bitcast.59, ...), custom_call_target="tpu_custom_call" | custom-call | flops 10000000 | bytes 1000000 | tf_op jit(solution)/shard_map/pallas_call | solution.py:427
  2.3 18.5 %all_to_all.72 = f32[8,1,17536]{2,1,0:T(1,128)S(1)} all-to-all(f32[8,1,17536]{2,1,0:T(1,128)S(1)} %bitcast.52), channel_id=1, replica_groups={{48,0,24,16,32,56,8,40},{49,1,25,17,33,57,9,41},{50,2,26,18,34,58,10,42..., dimensions={0} | all-to-all | bytes 1122304 | tf_op jit(solution)/shard_map/all_to_all | solution.py:386
  20.8 9.3 %all_to_all.73 = f32[8,1,6400]{2,1,0:T(1,128)S(1)} all-to-all(f32[8,1,6400]{2,1,0:T(1,128)S(1)} %bitcast.48), channel_id=1, replica_groups={{0,4,2,6,1,5,3,7},{8,12,10,14,9,13,11,15},{16,20,18,22,17,21,19,23},{24..., dimensions={0} | all-to-all | bytes 409600 | tf_op jit(solution)/shard_map/all_to_all | solution.py:386
  30.2 16.9 %all_to_all.74 = f32[8,1,3200]{2,1,0:T(1,128)S(1)} all-to-all(f32[8,1,3200]{2,1,0:T(1,128)S(1)} %bitcast.56), channel_id=1, replica_groups={{0,64,448,128,384,192,320,256},{1,65,449,129,385,193,321,257},{2,66,450..., dimensions={0} | all-to-all | bytes 204800 | tf_op jit(solution)/shard_map/all_to_all | solution.py:386
  47.1 0.7 shard_map.78
  47.8 19.7 %all_to_all.75 = f32[8,1,20480]{2,1,0:T(1,128)S(1)} all-to-all(f32[8,1,20480]{2,1,0:T(1,128)S(1)} %bitcast.51), channel_id=1, replica_groups={{0,4,1,5,2,6,3,7},{8,12,9,13,10,14,11,15},{16,20,17,21,18,22,19,23},{24..., dimensions={0} | all-to-all | bytes 1310720 | tf_op jit(solution)/shard_map/all_to_all | solution.py:386
  67.5 17.0 %all_to_all.76 = f32[8,1,18432]{2,1,0:T(1,128)S(1)} all-to-all(f32[8,1,18432]{2,1,0:T(1,128)S(1)} %bitcast.43), channel_id=1, replica_groups={{48,0,24,16,32,56,8,40},{49,1,25,17,33,57,9,41},{50,2,26,18,34,58,10,42..., dimensions={0} | all-to-all | bytes 1179648 | tf_op jit(solution)/shard_map/all_to_all | solution.py:386
  84.5 0.7 shard_map.80
  85.2 1.2 shard_map.81
  86.4 10.3 %all_to_all.77 = f32[8,1,3200]{2,1,0:T(1,128)S(1)} all-to-all(f32[8,1,3200]{2,1,0:T(1,128)S(1)} %bitcast.55), channel_id=1, replica_groups={{0,64,448,128,384,192,320,256},{1,65,449,129,385,193,321,257},{2,66,450..., dimensions={0} | all-to-all | bytes 204800 | tf_op jit(solution)/shard_map/all_to_all | solution.py:386
  96.7 10.3 %all_to_all.78 = f32[8,1,6400]{2,1,0:T(1,128)S(1)} all-to-all(f32[8,1,6400]{2,1,0:T(1,128)S(1)} %bitcast.50), channel_id=1, replica_groups={{0,4,2,6,1,5,3,7},{8,12,10,14,9,13,11,15},{16,20,18,22,17,21,19,23},{24..., dimensions={0} | all-to-all | bytes 409600 | tf_op jit(solution)/shard_map/all_to_all | solution.py:386
  107.1 14.6 %all_to_all.79 = f32[8,1,17536]{2,1,0:T(1,128)S(1)} all-to-all(f32[8,1,17536]{2,1,0:T(1,128)S(1)} %bitcast.46), channel_id=1, replica_groups={{48,0,24,16,32,56,8,40},{49,1,25,17,33,57,9,41},{50,2,26,18,34,58,10,42..., dimensions={0} | all-to-all | bytes 1122304 | tf_op jit(solution)/shard_map/all_to_all | solution.py:386
  121.7 1.4 %shard_map.84 = (bf16[1120,128]{1,0:T(8,128)(2,1)}, bf16[1120,128]{1,0:T(8,128)(2,1)}) custom-call(f32[1096,128]{1,0:T(8,128)S(1)} %bitcast.44, bf16[1120,128]{1,0:T(8,128)(2,1)S(1)} %get-tuple-element.40.k_ref, bf16[1120,128]{1,0:T(8,128)(2,1)S(1)} %get-tuple-element.41.v_ref), custom_call_target="tpu_custom_call" | custom-call | flops 10000000 | bytes 1000000 | tf_op jit(solution)/shard_map/pallas_call | solution.py:460
  (5 shorter events, 0.2 us)

commit v8 on v7

--- a/solution.py
+++ b/solution.py
@@ -9,10 +9,10 @@
 from jax.sharding import Mesh
 from jax.sharding import PartitionSpec as P
 
-PLANES = (0, 1, 7, 2, 6, 3, 5, 4)
-ROWS = (0, 4, 2, 6, 1, 5, 3, 7)
-FULL_ROWS = (0, 4, 1, 5, 2, 6, 3, 7)
-CHIP = tuple((n % 2, n // 2) for n in (5, 0, 6, 4, 1, 7, 2, 3))
+PLANES = (0, 4, 1, 5, 2, 6, 3, 7)
+ROWS = (0, 1, 7, 2, 6, 3, 5, 4)
+FULL_ROWS = (0, 4, 6, 2, 7, 3, 5, 1)
+CHIP = tuple((n % 2, n // 2) for n in (3, 0, 6, 7, 1, 5, 2, 4))
 
 HEAD_DIM = 112
 LANES = 128
@@ -131,30 +131,45 @@
     return jnp.concatenate([x, rest.astype(BF16)], axis=0)
 
 
+def parts_of(channels):
+    heads = channels // HEAD_DIM
+    ends = [HEAD_DIM * (-(-heads * n // 3)) for n in (1, 2, 3)]
+    done = 0
+    for begin, end in zip([0, *ends], ends):
+        ready = [t for t in tiles(channels) if max(t.pair.stop, t.here.stop) <= end]
+        yield slice(begin, end), ready[done:]
+        done = len(ready)
+
+
 def states_kernel(slabs, height, *refs):
     loaded, (out_ref, *held, total_ref, sems) = refs[:4], refs[4:]
-    copies = [pltpu.make_async_copy(a, b, sems.at[i]) for i, (a, b) in enumerate(zip(loaded, held))]
+    channels, rows = loaded[0].shape
+    steps = list(parts_of(channels))
+    spans = [(i, span) for span, _ in steps for i in range(2)] + [(i, slice(0, channels)) for i in (2, 3)]
+    copies = [
+        pltpu.make_async_copy(loaded[i].at[span, :], held[i].at[span, :], sems.at[n])
+        for n, (i, span) in enumerate(spans)
+    ]
     for copy in copies:
         copy.start()
     k_ref, v_ref = held[:2]
-    channels, rows = k_ref.shape
     total_ref[...] = jnp.zeros_like(total_ref)
     pieces = out_ref.shape[0] // height
     out_ref[height * (pieces - 1) :, :] = jnp.zeros((height, LANES), F32)
     ones = jnp.ones((16, rows), BF16)
-    copies[0].wait()
-    for t in tiles(channels):
-        total_ref[t.j : t.j + 1, : t.width] = dot_rows(ones, relu(k_ref[t.here, :]))[:1]
+    for n, (_, ready) in enumerate(steps):
+        copies[2 * n].wait()
+        copies[2 * n + 1].wait()
+        for t in ready:
+            keys = relu(k_ref[t.here, :])
+            total_ref[t.j : t.j + 1, : t.width] = dot_rows(ones, keys)[:1]
+            slabs.put(out_ref, t, heads_apart(t, dot_rows(v_ref[t.pair, :], keys)))
     total = total_ref[...]
     for s in range(pieces):
         at = height * (s + 1)
         out_ref[at - len(total) : at, :] = total
-    copies[1].wait()
-    for t in tiles(channels):
-        both = dot_rows(v_ref[t.pair, :], relu(k_ref[t.here, :]))
-        slabs.put(out_ref, t, heads_apart(t, both))
-    copies[2].wait()
-    copies[3].wait()
+    copies[-2].wait()
+    copies[-1].wait()
 
 
 def total_of(parts):
@@ -322,9 +337,8 @@
         out_ref[len(message) * p : len(message) * (p + 1), :] = message
 
 
-def queries_kernel(slabs, in_ref, q_ref, g_ref, rec_ref, sums_ref, total_ref, attn_ref, out_ref, mixed_ref, hi_ref, lo_ref):
+def queries_kernel(slabs, in_ref, q_ref, g_ref, rec_ref, sums_ref, total_ref, out_ref, hi_ref, lo_ref):
     channels, rows = q_ref.shape
-    mixed_ref[...] = attn_ref[...]
     for t in tiles(channels):
         shape = (LANES - HEAD_DIM, t.width)
         extra = jnp.where(row(shape) < 2, jnp.broadcast_to(total_ref[t.j : t.j + 1, : t.width], shape), 0.0)
@@ -340,39 +354,51 @@
         out_ref[of_head(h), :] = jnp.where(q > 0, feature, 0.0).astype(BF16)
 
 
-def keys(slabs, in_ref, total, k_ref, v_ref, gk_ref, gv_ref, flat, hi_ref, lo_ref):
+def keys_kernel(slabs, in_ref, k_ref, v_ref, attn_ref, gq_ref, mixed_out, gq_out, gk_out, gv_out, gk_ref, gv_ref, flat_hi_ref, flat_lo_ref, hi_ref, lo_ref, sems):
     channels, rows = k_ref.shape
+    heads, pieces = channels // HEAD_DIM, len(CHIP)
+    middle = HEAD_DIM * (heads // 2)
+    moves = [(attn_ref, mixed_out, 0, channels), (gq_ref, gq_out, 0, channels)]
+    for begin, end in ((0, middle), (middle, channels)):
+        moves += [(gk_ref, gk_out, begin, end), (gv_ref, gv_out, begin, end)]
+    copies = [
+        pltpu.make_async_copy(a.at[begin:end, :], b.at[begin:end, :], sems.at[n])
+        for n, (a, b, begin, end) in enumerate(moves)
+    ]
+    copies[0].start()
+    copies[1].start()
+    height, count = in_ref.shape[0] // pieces, len(tiles(channels))
+    total = total_of(cut_rows(in_ref, height, s, height - count, count) for s in range(pieces))
     for t in tiles(channels):
         shape = (LANES - HEAD_DIM, t.width)
         extra = jnp.where(row(shape) < 1, jnp.broadcast_to(total[t.j : t.j + 1, : t.width], shape), 0.0)
         state = slabs.get(in_ref, t)
-        keep_halves(t, state, *flat)
+        keep_halves(t, state, flat_hi_ref, flat_lo_ref)
         turn(t, state, extra, hi_ref, lo_ref)
     ones = jnp.ones((LANES - HEAD_DIM, rows), BF16)
-    for h in range(channels // HEAD_DIM):
-        gv_ref[of_head(h), :] = by_state(*flat, k_ref, h).astype(BF16)
+    for h in range(heads):
+        gv_ref[of_head(h), :] = by_state(flat_hi_ref, flat_lo_ref, k_ref, h).astype(BF16)
         rhs = with_rows(v_ref[of_head(h), :], ones)
         grad = both_halves(dot, hi_ref[of_head(h), :], lo_ref[of_head(h), :], rhs)
         k = k_ref[of_head(h), :].astype(F32)
         gk_ref[of_head(h), :] = jnp.where(k > 0, grad, 0.0).astype(BF16)
-
-
-def keys_kernel(slabs, in_ref, k_ref, v_ref, gk_ref, gv_ref, flat_hi_ref, flat_lo_ref, hi_ref, lo_ref):
-    pieces = len(CHIP)
-    height, count = in_ref.shape[0] // pieces, len(tiles(k_ref.shape[0]))
-    total = total_of(cut_rows(in_ref, height, s, height - count, count) for s in range(pieces))
-    flat = flat_hi_ref, flat_lo_ref
-    keys(slabs, in_ref, total, k_ref, v_ref, gk_ref, gv_ref, flat, hi_ref, lo_ref)
-
-
-def call(kernel, out, in_specs, scratch=(), more=(), flops=10**7, moved=10**6):
+        if h == heads // 2 - 1:
+            copies[2].start()
+            copies[3].start()
+    copies[4].start()
+    copies[5].start()
+    for copy in copies:
+        copy.wait()
+
+
+def call(kernel, out, in_specs, scratch=(), more=(), out_space=VMEM, flops=10**7, moved=10**6):
     shapes = [jax.ShapeDtypeStruct(s, d) for s, d in out]
     several = len(shapes) > 1
     return pl.pallas_call(
         kernel,
         out_shape=shapes if several else shapes[0],
         in_specs=in_specs,
-        out_specs=[VMEM] * len(shapes) if several else VMEM,
+        out_specs=[out_space] * len(shapes) if several else out_space,
         scratch_shapes=[pltpu.VMEM(s, d) for s, d in scratch] + list(more),
         cost_estimate=pl.CostEstimate(flops=flops, bytes_accessed=moved, transcendentals=0),
         compiler_params=pltpu.CompilerParams(vmem_limit_bytes=24 * 2**20),
@@ -426,7 +452,7 @@
 
     sent, k, v, q, g = call(
         functools.partial(states_kernel, outer, tall),
-        [message(2 * nx, tall)] + [whole] * 4, [HBM] * 4, [line], [pltpu.SemaphoreType.DMA((4,))],
+        [message(2 * nx, tall)] + [whole] * 4, [HBM] * 4, [line], [pltpu.SemaphoreType.DMA((8,))],
     )(*(pltpu.with_memory_space_constraint(a, pltpu.HBM) for a in (k, v, q, g)))
     sent = call(
         functools.partial(to_rows_kernel, (ny, base, pitch)), [message(ny, pitch)], [VMEM]
@@ -447,9 +473,9 @@
         functools.partial(attention_kernel, nz, base, got),
         [message(nz, short), message(1, base + short), whole, small], [VMEM] * 4, [flat, flat, line],
     )(states, q, g, rec)
-    grad_queries, mixed = call(
-        functools.partial(queries_kernel, got), [whole] * 2, [VMEM] * 7, [whole, whole]
-    )(states, q, g, rec, sums, total, attn)
+    grad_queries = call(
+        functools.partial(queries_kernel, got), [whole], [VMEM] * 6, [whole, whole]
+    )(states, q, g, rec, sums, total)
     sent, grad_queries = lax.optimization_barrier((sent, grad_queries))
     sent = call(
         functools.partial(suffix_kernel, ny, base), [message(ny, pitch)], [VMEM] * 2
@@ -457,10 +483,12 @@
     sent = call(
         functools.partial(to_columns_kernel, (ny, base, pitch)), [message(2 * nx, tall)], [VMEM]
     )(over_rows(sent))
-    grad_keys, values_gradient = call(
-        functools.partial(keys_kernel, Slabs(last)), [whole] * 2, [VMEM] * 3, [flat, flat, whole, whole]
-    )(over_chips(sent), k, v)
-    return tuple(a.T[None] for a in (mixed, grad_queries, grad_keys, values_gradient))
+    outs = call(
+        functools.partial(keys_kernel, Slabs(last)),
+        [whole] * 4, [VMEM] * 5, [whole, whole, flat, flat, whole, whole],
+        [pltpu.SemaphoreType.DMA((6,))], HBM,
+    )(over_chips(sent), k, v, attn, grad_queries)
+    return tuple(a.T[None] for a in outs)
 
 
 def solution(mesh):

time: 123 us -> 125 us (1.016)
    all_to_all x8, blocking collectives: 117 us -> 118 us  [exchanged(): lax.all_to_all(pieces, axes, 0, 0, tiled=True, axis_index_groups=[order])]
where the time goes in v8:
time: 125 us; the launch traced here: 124 us
  blocking collectives  118 us (94%)
  Pallas kernels  5.17 us (4%)
    all_to_all x8, blocking collectives, exchanged(): lax.all_to_all(pieces, axes, 0, 0, tiled=True, axis_index_groups=[order])  118 us

profile of v8, /device:TPU:1, one launch (start us, length us, event | category | flops | bytes accessed | tf_op | source)
XLA Modules:
  0.0 124.2 jit_solution(3616702840769815521)
XLA Ops:
  0.6 1.8 %shard_map.75 = (f32[1096,128]{1,0:T(8,128)S(1)}, bf16[1120,128]{1,0:T(8,128)(2,1)S(1)}, bf16[1120,128]{1,0:T(8,128)(2,1)S(1)}, bf16[1120,128]{1,0:T(8,128)(2,1)S(1)}, bf16[1120,128]{1,0:T(8,128)(2,1)S(1)}) custom-call(bf16[1120,128]{1,0:T(8,128)(2,1)} %bitcast.57, bf16[1120,128]{1,0:T(8,128)(2,1)} %bitcast.58, bf16[1120,128]{1,0:T(8,128)(2,1)} %bitcast.59, ...), custom_call_target="tpu_custom_call" | custom-call | flops 10000000 | bytes 1000000 | tf_op jit(solution)/shard_map/pallas_call | solution.py:453
  2.4 18.8 %all_to_all.72 = f32[8,1,17536]{2,1,0:T(1,128)S(1)} all-to-all(f32[8,1,17536]{2,1,0:T(1,128)S(1)} %bitcast.52), channel_id=1, replica_groups={{40,0,24,56,32,48,8,16},{41,1,25,57,33,49,9,17},{42,2,26,58,34,50,10,18..., dimensions={0} | all-to-all | bytes 1122304 | tf_op jit(solution)/shard_map/all_to_all | solution.py:412
  21.3 12.7 %all_to_all.73 = f32[8,1,6400]{2,1,0:T(1,128)S(1)} all-to-all(f32[8,1,6400]{2,1,0:T(1,128)S(1)} %bitcast.48), channel_id=1, replica_groups={{0,1,7,2,6,3,5,4},{8,9,15,10,14,11,13,12},{16,17,23,18,22,19,21,20},{24..., dimensions={0} | all-to-all | bytes 409600 | tf_op jit(solution)/shard_map/all_to_all | solution.py:412
  34.0 16.6 %all_to_all.74 = f32[8,1,3200]{2,1,0:T(1,128)S(1)} all-to-all(f32[8,1,3200]{2,1,0:T(1,128)S(1)} %bitcast.56), channel_id=1, replica_groups={{0,256,64,320,128,384,192,448},{1,257,65,321,129,385,193,449},{2,258,66..., dimensions={0} | all-to-all | bytes 204800 | tf_op jit(solution)/shard_map/all_to_all | solution.py:412
  50.6 0.7 shard_map.78
  51.3 17.2 %all_to_all.75 = f32[8,1,20480]{2,1,0:T(1,128)S(1)} all-to-all(f32[8,1,20480]{2,1,0:T(1,128)S(1)} %bitcast.51), channel_id=1, replica_groups={{0,4,6,2,7,3,5,1},{8,12,14,10,15,11,13,9},{16,20,22,18,23,19,21,17},{24..., dimensions={0} | all-to-all | bytes 1310720 | tf_op jit(solution)/shard_map/all_to_all | solution.py:412
  68.6 17.4 %all_to_all.76 = f32[8,1,18432]{2,1,0:T(1,128)S(1)} all-to-all(f32[8,1,18432]{2,1,0:T(1,128)S(1)} %bitcast.43), channel_id=1, replica_groups={{40,0,24,56,32,48,8,16},{41,1,25,57,33,49,9,17},{42,2,26,58,34,50,10,18..., dimensions={0} | all-to-all | bytes 1179648 | tf_op jit(solution)/shard_map/all_to_all | solution.py:412
  85.9 0.7 shard_map.80
  86.6 0.4 shard_map.81.gq_ref
  87.1 9.2 %all_to_all.77 = f32[8,1,3200]{2,1,0:T(1,128)S(1)} all-to-all(f32[8,1,3200]{2,1,0:T(1,128)S(1)} %bitcast.55), channel_id=1, replica_groups={{0,256,64,320,128,384,192,448},{1,257,65,321,129,385,193,449},{2,258,66..., dimensions={0} | all-to-all | bytes 204800 | tf_op jit(solution)/shard_map/all_to_all | solution.py:412
  96.3 11.5 %all_to_all.78 = f32[8,1,6400]{2,1,0:T(1,128)S(1)} all-to-all(f32[8,1,6400]{2,1,0:T(1,128)S(1)} %bitcast.50), channel_id=1, replica_groups={{0,1,7,2,6,3,5,4},{8,9,15,10,14,11,13,12},{16,17,23,18,22,19,21,20},{24..., dimensions={0} | all-to-all | bytes 409600 | tf_op jit(solution)/shard_map/all_to_all | solution.py:412
  107.8 15.0 %all_to_all.79 = f32[8,1,17536]{2,1,0:T(1,128)S(1)} all-to-all(f32[8,1,17536]{2,1,0:T(1,128)S(1)} %bitcast.45), channel_id=1, replica_groups={{40,0,24,56,32,48,8,16},{41,1,25,57,33,49,9,17},{42,2,26,58,34,50,10,18..., dimensions={0} | all-to-all | bytes 1122304 | tf_op jit(solution)/shard_map/all_to_all | solution.py:412
  122.8 1.4 %shard_map.84 = (bf16[1120,128]{1,0:T(8,128)(2,1)}, bf16[1120,128]{1,0:T(8,128)(2,1)}, bf16[1120,128]{1,0:T(8,128)(2,1)}, bf16[1120,128]{1,0:T(8,128)(2,1)}) custom-call(f32[1096,128]{1,0:T(8,128)S(1)} %bitcast.46, bf16[1120,128]{1,0:T(8,128)(2,1)S(1)} %get-tuple-element.36.k_ref, bf16[1120,128]{1,0:T(8,128)(2,1)S(1)} %get-tuple-element.37.v_ref, ...), custom_call_target="tpu_custom_call" | custom-call | flops 10000000 | bytes 1000000 | tf_op jit(solution)/shard_map/pallas_call | solution.py:486
  (5 shorter events, 0.2 us)

commit v9 on v8

--- a/solution.py
+++ b/solution.py
@@ -10,7 +10,7 @@
 from jax.sharding import PartitionSpec as P
 
 PLANES = (0, 4, 1, 5, 2, 6, 3, 7)
-ROWS = (0, 1, 7, 2, 6, 3, 5, 4)
+ROWS = (0, 4, 2, 6, 1, 5, 3, 7)
 FULL_ROWS = (0, 4, 6, 2, 7, 3, 5, 1)
 CHIP = tuple((n % 2, n // 2) for n in (3, 0, 6, 7, 1, 5, 2, 4))
 
@@ -131,45 +131,30 @@
     return jnp.concatenate([x, rest.astype(BF16)], axis=0)
 
 
-def parts_of(channels):
-    heads = channels // HEAD_DIM
-    ends = [HEAD_DIM * (-(-heads * n // 3)) for n in (1, 2, 3)]
-    done = 0
-    for begin, end in zip([0, *ends], ends):
-        ready = [t for t in tiles(channels) if max(t.pair.stop, t.here.stop) <= end]
-        yield slice(begin, end), ready[done:]
-        done = len(ready)
-
-
 def states_kernel(slabs, height, *refs):
     loaded, (out_ref, *held, total_ref, sems) = refs[:4], refs[4:]
-    channels, rows = loaded[0].shape
-    steps = list(parts_of(channels))
-    spans = [(i, span) for span, _ in steps for i in range(2)] + [(i, slice(0, channels)) for i in (2, 3)]
-    copies = [
-        pltpu.make_async_copy(loaded[i].at[span, :], held[i].at[span, :], sems.at[n])
-        for n, (i, span) in enumerate(spans)
-    ]
+    copies = [pltpu.make_async_copy(a, b, sems.at[i]) for i, (a, b) in enumerate(zip(loaded, held))]
     for copy in copies:
         copy.start()
     k_ref, v_ref = held[:2]
+    channels, rows = k_ref.shape
     total_ref[...] = jnp.zeros_like(total_ref)
     pieces = out_ref.shape[0] // height
     out_ref[height * (pieces - 1) :, :] = jnp.zeros((height, LANES), F32)
     ones = jnp.ones((16, rows), BF16)
-    for n, (_, ready) in enumerate(steps):
-        copies[2 * n].wait()
-        copies[2 * n + 1].wait()
-        for t in ready:
-            keys = relu(k_ref[t.here, :])
-            total_ref[t.j : t.j + 1, : t.width] = dot_rows(ones, keys)[:1]
-            slabs.put(out_ref, t, heads_apart(t, dot_rows(v_ref[t.pair, :], keys)))
+    copies[0].wait()
+    for t in tiles(channels):
+        total_ref[t.j : t.j + 1, : t.width] = dot_rows(ones, relu(k_ref[t.here, :]))[:1]
     total = total_ref[...]
     for s in range(pieces):
         at = height * (s + 1)
         out_ref[at - len(total) : at, :] = total
-    copies[-2].wait()
-    copies[-1].wait()
+    copies[1].wait()
+    for t in tiles(channels):
+        both = dot_rows(v_ref[t.pair, :], relu(k_ref[t.here, :]))
+        slabs.put(out_ref, t, heads_apart(t, both))
+    copies[2].wait()
+    copies[3].wait()
 
 
 def total_of(parts):
@@ -452,7 +437,7 @@
 
     sent, k, v, q, g = call(
         functools.partial(states_kernel, outer, tall),
-        [message(2 * nx, tall)] + [whole] * 4, [HBM] * 4, [line], [pltpu.SemaphoreType.DMA((8,))],
+        [message(2 * nx, tall)] + [whole] * 4, [HBM] * 4, [line], [pltpu.SemaphoreType.DMA((4,))],
     )(*(pltpu.with_memory_space_constraint(a, pltpu.HBM) for a in (k, v, q, g)))
     sent = call(
         functools.partial(to_rows_kernel, (ny, base, pitch)), [message(ny, pitch)], [VMEM]

time: 125 us -> 122 us (0.976)
  blocking collectives: 118 us -> 116 us
    all_to_all x8, blocking collectives: 118 us -> 116 us  [exchanged(): lax.all_to_all(pieces, axes, 0, 0, tiled=True, axis_index_groups=[order])]
where the time goes in v9:
time: 122 us
  blocking collectives  116 us (95%)
  Pallas kernels  5 us (4%)
    all_to_all x8, blocking collectives, exchanged(): lax.all_to_all(pieces, axes, 0, 0, tiled=True, axis_index_groups=[order])  116 us

profile of v9, /device:TPU:1, one launch (start us, length us, event | category | flops | bytes accessed | tf_op | source)
XLA Modules:
  0.0 122.0 jit_solution(8597338475738267107)
XLA Ops:
  0.6 1.6 %shard_map.75 = (f32[1096,128]{1,0:T(8,128)S(1)}, bf16[1120,128]{1,0:T(8,128)(2,1)S(1)}, bf16[1120,128]{1,0:T(8,128)(2,1)S(1)}, bf16[1120,128]{1,0:T(8,128)(2,1)S(1)}, bf16[1120,128]{1,0:T(8,128)(2,1)S(1)}) custom-call(bf16[1120,128]{1,0:T(8,128)(2,1)} %bitcast.57, bf16[1120,128]{1,0:T(8,128)(2,1)} %bitcast.58, bf16[1120,128]{1,0:T(8,128)(2,1)} %bitcast.59, ...), custom_call_target="tpu_custom_call" | custom-call | flops 10000000 | bytes 1000000 | tf_op jit(solution)/shard_map/pallas_call | solution.py:438
  2.3 18.8 %all_to_all.72 = f32[8,1,17536]{2,1,0:T(1,128)S(1)} all-to-all(f32[8,1,17536]{2,1,0:T(1,128)S(1)} %bitcast.52), channel_id=1, replica_groups={{40,0,24,56,32,48,8,16},{41,1,25,57,33,49,9,17},{42,2,26,58,34,50,10,18..., dimensions={0} | all-to-all | bytes 1122304 | tf_op jit(solution)/shard_map/all_to_all | solution.py:397
  21.1 9.7 %all_to_all.73 = f32[8,1,6400]{2,1,0:T(1,128)S(1)} all-to-all(f32[8,1,6400]{2,1,0:T(1,128)S(1)} %bitcast.48), channel_id=1, replica_groups={{0,4,2,6,1,5,3,7},{8,12,10,14,9,13,11,15},{16,20,18,22,17,21,19,23},{24..., dimensions={0} | all-to-all | bytes 409600 | tf_op jit(solution)/shard_map/all_to_all | solution.py:397
  30.8 16.5 %all_to_all.74 = f32[8,1,3200]{2,1,0:T(1,128)S(1)} all-to-all(f32[8,1,3200]{2,1,0:T(1,128)S(1)} %bitcast.56), channel_id=1, replica_groups={{0,256,64,320,128,384,192,448},{1,257,65,321,129,385,193,449},{2,258,66..., dimensions={0} | all-to-all | bytes 204800 | tf_op jit(solution)/shard_map/all_to_all | solution.py:397
  47.3 0.7 shard_map.78
  48.0 22.1 %all_to_all.75 = f32[8,1,20480]{2,1,0:T(1,128)S(1)} all-to-all(f32[8,1,20480]{2,1,0:T(1,128)S(1)} %bitcast.51), channel_id=1, replica_groups={{0,4,6,2,7,3,5,1},{8,12,14,10,15,11,13,9},{16,20,22,18,23,19,21,17},{24..., dimensions={0} | all-to-all | bytes 1310720 | tf_op jit(solution)/shard_map/all_to_all | solution.py:397
  70.2 15.6 %all_to_all.76 = f32[8,1,18432]{2,1,0:T(1,128)S(1)} all-to-all(f32[8,1,18432]{2,1,0:T(1,128)S(1)} %bitcast.43), channel_id=1, replica_groups={{40,0,24,56,32,48,8,16},{41,1,25,57,33,49,9,17},{42,2,26,58,34,50,10,18..., dimensions={0} | all-to-all | bytes 1179648 | tf_op jit(solution)/shard_map/all_to_all | solution.py:397
  85.7 0.7 shard_map.80
  86.4 0.4 shard_map.81.gq_ref
  86.9 9.1 %all_to_all.77 = f32[8,1,3200]{2,1,0:T(1,128)S(1)} all-to-all(f32[8,1,3200]{2,1,0:T(1,128)S(1)} %bitcast.55), channel_id=1, replica_groups={{0,256,64,320,128,384,192,448},{1,257,65,321,129,385,193,449},{2,258,66..., dimensions={0} | all-to-all | bytes 204800 | tf_op jit(solution)/shard_map/all_to_all | solution.py:397
  96.0 9.5 %all_to_all.78 = f32[8,1,6400]{2,1,0:T(1,128)S(1)} all-to-all(f32[8,1,6400]{2,1,0:T(1,128)S(1)} %bitcast.50), channel_id=1, replica_groups={{0,4,2,6,1,5,3,7},{8,12,10,14,9,13,11,15},{16,20,18,22,17,21,19,23},{24..., dimensions={0} | all-to-all | bytes 409600 | tf_op jit(solution)/shard_map/all_to_all | solution.py:397
  105.6 15.0 %all_to_all.79 = f32[8,1,17536]{2,1,0:T(1,128)S(1)} all-to-all(f32[8,1,17536]{2,1,0:T(1,128)S(1)} %bitcast.45), channel_id=1, replica_groups={{40,0,24,56,32,48,8,16},{41,1,25,57,33,49,9,17},{42,2,26,58,34,50,10,18..., dimensions={0} | all-to-all | bytes 1122304 | tf_op jit(solution)/shard_map/all_to_all | solution.py:397
  120.6 1.4 %shard_map.84 = (bf16[1120,128]{1,0:T(8,128)(2,1)}, bf16[1120,128]{1,0:T(8,128)(2,1)}, bf16[1120,128]{1,0:T(8,128)(2,1)}, bf16[1120,128]{1,0:T(8,128)(2,1)}) custom-call(f32[1096,128]{1,0:T(8,128)S(1)} %bitcast.46, bf16[1120,128]{1,0:T(8,128)(2,1)S(1)} %get-tuple-element.36.k_ref, bf16[1120,128]{1,0:T(8,128)(2,1)S(1)} %get-tuple-element.37.v_ref, ...), custom_call_target="tpu_custom_call" | custom-call | flops 10000000 | bytes 1000000 | tf_op jit(solution)/shard_map/pallas_call | solution.py:471
  (5 shorter events, 0.2 us)

commit v10 on v9

--- a/solution.py
+++ b/solution.py
@@ -11,8 +11,8 @@
 
 PLANES = (0, 4, 1, 5, 2, 6, 3, 7)
 ROWS = (0, 4, 2, 6, 1, 5, 3, 7)
-FULL_ROWS = (0, 4, 6, 2, 7, 3, 5, 1)
-CHIP = tuple((n % 2, n // 2) for n in (3, 0, 6, 7, 1, 5, 2, 4))
+FULL_ROWS = (0, 4, 1, 5, 2, 6, 3, 7)
+CHIP = tuple((n % 2, n // 2) for n in (5, 0, 6, 4, 1, 7, 2, 3))
 
 HEAD_DIM = 112
 LANES = 128
@@ -308,7 +308,7 @@
         gt_ref[t.j : t.j + 1, : t.width] = jnp.sum(term, axis=0, keepdims=True)
 
 
-def attention_kernel(planes, base, slabs, in_ref, q_ref, g_ref, rec_ref, out_ref, own_ref, mixed_ref, sums_ref, flat_hi_ref, flat_lo_ref, gt_ref):
+def attention_kernel(planes, base, slabs, in_ref, q_ref, g_ref, rec_ref, total_ref, out_ref, own_ref, mixed_ref, gq_ref, sums_ref, flat_hi_ref, flat_lo_ref, gt_ref, hi_ref, lo_ref):
     attention(slabs, in_ref, q_ref, g_ref, rec_ref[...], mixed_ref, sums_ref, gt_ref, flat_hi_ref, flat_lo_ref)
     height = in_ref.shape[0] // len(CHIP)
     sums = [
@@ -320,9 +320,10 @@
     message = jnp.concatenate([sums[0] + sums[1], part], axis=0)
     for p in range(planes):
         out_ref[len(message) * p : len(message) * (p + 1), :] = message
-
-
-def queries_kernel(slabs, in_ref, q_ref, g_ref, rec_ref, sums_ref, total_ref, out_ref, hi_ref, lo_ref):
+    queries(slabs, in_ref, q_ref, g_ref, rec_ref, sums_ref, total_ref, gq_ref, hi_ref, lo_ref)
+
+
+def queries(slabs, in_ref, q_ref, g_ref, rec_ref, sums_ref, total_ref, out_ref, hi_ref, lo_ref):
     channels, rows = q_ref.shape
     for t in tiles(channels):
         shape = (LANES - HEAD_DIM, t.width)
@@ -342,9 +343,9 @@
 def keys_kernel(slabs, in_ref, k_ref, v_ref, attn_ref, gq_ref, mixed_out, gq_out, gk_out, gv_out, gk_ref, gv_ref, flat_hi_ref, flat_lo_ref, hi_ref, lo_ref, sems):
     channels, rows = k_ref.shape
     heads, pieces = channels // HEAD_DIM, len(CHIP)
-    middle = HEAD_DIM * (heads // 2)
+    ends = [HEAD_DIM * h for h in (heads // 2, heads - heads // 5, heads)]
     moves = [(attn_ref, mixed_out, 0, channels), (gq_ref, gq_out, 0, channels)]
-    for begin, end in ((0, middle), (middle, channels)):
+    for begin, end in zip([0, *ends], ends):
         moves += [(gk_ref, gk_out, begin, end), (gv_ref, gv_out, begin, end)]
     copies = [
         pltpu.make_async_copy(a.at[begin:end, :], b.at[begin:end, :], sems.at[n])
@@ -367,11 +368,10 @@
         grad = both_halves(dot, hi_ref[of_head(h), :], lo_ref[of_head(h), :], rhs)
         k = k_ref[of_head(h), :].astype(F32)
         gk_ref[of_head(h), :] = jnp.where(k > 0, grad, 0.0).astype(BF16)
-        if h == heads // 2 - 1:
-            copies[2].start()
-            copies[3].start()
-    copies[4].start()
-    copies[5].start()
+        if HEAD_DIM * (h + 1) in ends:
+            n = 2 + 2 * ends.index(HEAD_DIM * (h + 1))
+            copies[n].start()
+            copies[n + 1].start()
     for copy in copies:
         copy.wait()
 
@@ -454,14 +454,11 @@
         functools.partial(cross_kernel, base), [message(2 * nx, full)], [VMEM]
     )(over_rows(sent, FULL_ROWS))
     states = over_chips(sent)
-    sent, own, attn, sums = call(
+    sent, own, attn, grad_queries = call(
         functools.partial(attention_kernel, nz, base, got),
-        [message(nz, short), message(1, base + short), whole, small], [VMEM] * 4, [flat, flat, line],
-    )(states, q, g, rec)
-    grad_queries = call(
-        functools.partial(queries_kernel, got), [whole], [VMEM] * 6, [whole, whole]
-    )(states, q, g, rec, sums, total)
-    sent, grad_queries = lax.optimization_barrier((sent, grad_queries))
+        [message(nz, short), message(1, base + short), whole, whole], [VMEM] * 5,
+        [small, flat, flat, line, whole, whole],
+    )(states, q, g, rec, total)
     sent = call(
         functools.partial(suffix_kernel, ny, base), [message(ny, pitch)], [VMEM] * 2
     )(over_planes(sent), own)
@@ -471,7 +468,7 @@
     outs = call(
         functools.partial(keys_kernel, Slabs(last)),
         [whole] * 4, [VMEM] * 5, [whole, whole, flat, flat, whole, whole],
-        [pltpu.SemaphoreType.DMA((6,))], HBM,
+        [pltpu.SemaphoreType.DMA((8,))], HBM,
     )(over_chips(sent), k, v, attn, grad_queries)
     return tuple(a.T[None] for a in outs)
 

time: 122 us -> 121 us (level)
    all_to_all x8, blocking collectives: 116 us -> 115 us  [exchanged(): lax.all_to_all(pieces, axes, 0, 0, tiled=True, axis_index_groups=[order])]
where the time goes in v10:
time: 121 us; the launch traced here: 120 us
  blocking collectives  115 us (95%)
  Pallas kernels  4.71 us (4%)
    all_to_all x8, blocking collectives, exchanged(): lax.all_to_all(pieces, axes, 0, 0, tiled=True, axis_index_groups=[order])  115 us

profile of v10, /device:TPU:1, one launch (start us, length us, event | category | flops | bytes accessed | tf_op | source)
XLA Modules:
  0.0 120.3 jit_solution(1798202249064170062)
XLA Ops:
  0.6 1.6 %shard_map.75 = (f32[1096,128]{1,0:T(8,128)S(1)}, bf16[1120,128]{1,0:T(8,128)(2,1)S(1)}, bf16[1120,128]{1,0:T(8,128)(2,1)S(1)}, bf16[1120,128]{1,0:T(8,128)(2,1)S(1)}, bf16[1120,128]{1,0:T(8,128)(2,1)S(1)}) custom-call(bf16[1120,128]{1,0:T(8,128)(2,1)} %bitcast.56, bf16[1120,128]{1,0:T(8,128)(2,1)} %bitcast.57, bf16[1120,128]{1,0:T(8,128)(2,1)} %bitcast.58, ...), custom_call_target="tpu_custom_call" | custom-call | flops 10000000 | bytes 1000000 | tf_op jit(solution)/shard_map/pallas_call | solution.py:438
  2.3 18.5 %all_to_all.72 = f32[8,1,17536]{2,1,0:T(1,128)S(1)} all-to-all(f32[8,1,17536]{2,1,0:T(1,128)S(1)} %bitcast.51), channel_id=1, replica_groups={{48,0,24,16,32,56,8,40},{49,1,25,17,33,57,9,41},{50,2,26,18,34,58,10,42..., dimensions={0} | all-to-all | bytes 1122304 | tf_op jit(solution)/shard_map/all_to_all | solution.py:397
  20.8 9.3 %all_to_all.73 = f32[8,1,6400]{2,1,0:T(1,128)S(1)} all-to-all(f32[8,1,6400]{2,1,0:T(1,128)S(1)} %bitcast.47), channel_id=1, replica_groups={{0,4,2,6,1,5,3,7},{8,12,10,14,9,13,11,15},{16,20,18,22,17,21,19,23},{24..., dimensions={0} | all-to-all | bytes 409600 | tf_op jit(solution)/shard_map/all_to_all | solution.py:397
  30.2 16.0 %all_to_all.74 = f32[8,1,3200]{2,1,0:T(1,128)S(1)} all-to-all(f32[8,1,3200]{2,1,0:T(1,128)S(1)} %bitcast.55), channel_id=1, replica_groups={{0,256,64,320,128,384,192,448},{1,257,65,321,129,385,193,449},{2,258,66..., dimensions={0} | all-to-all | bytes 204800 | tf_op jit(solution)/shard_map/all_to_all | solution.py:397
  46.2 0.7 shard_map.78
  46.8 19.6 %all_to_all.75 = f32[8,1,20480]{2,1,0:T(1,128)S(1)} all-to-all(f32[8,1,20480]{2,1,0:T(1,128)S(1)} %bitcast.50), channel_id=1, replica_groups={{0,4,1,5,2,6,3,7},{8,12,9,13,10,14,11,15},{16,20,17,21,18,22,19,23},{24..., dimensions={0} | all-to-all | bytes 1310720 | tf_op jit(solution)/shard_map/all_to_all | solution.py:397
  66.5 17.0 %all_to_all.76 = f32[8,1,18432]{2,1,0:T(1,128)S(1)} all-to-all(f32[8,1,18432]{2,1,0:T(1,128)S(1)} %bitcast.42), channel_id=1, replica_groups={{48,0,24,16,32,56,8,40},{49,1,25,17,33,57,9,41},{50,2,26,18,34,58,10,42..., dimensions={0} | all-to-all | bytes 1179648 | tf_op jit(solution)/shard_map/all_to_all | solution.py:397
  83.6 0.9 shard_map.80
  84.5 9.1 %all_to_all.77 = f32[8,1,3200]{2,1,0:T(1,128)S(1)} all-to-all(f32[8,1,3200]{2,1,0:T(1,128)S(1)} %bitcast.54), channel_id=1, replica_groups={{0,256,64,320,128,384,192,448},{1,257,65,321,129,385,193,449},{2,258,66..., dimensions={0} | all-to-all | bytes 204800 | tf_op jit(solution)/shard_map/all_to_all | solution.py:397
  93.6 10.2 %all_to_all.78 = f32[8,1,6400]{2,1,0:T(1,128)S(1)} all-to-all(f32[8,1,6400]{2,1,0:T(1,128)S(1)} %bitcast.49), channel_id=1, replica_groups={{0,4,2,6,1,5,3,7},{8,12,10,14,9,13,11,15},{16,20,18,22,17,21,19,23},{24..., dimensions={0} | all-to-all | bytes 409600 | tf_op jit(solution)/shard_map/all_to_all | solution.py:397
  103.9 15.1 %all_to_all.79 = f32[8,1,17536]{2,1,0:T(1,128)S(1)} all-to-all(f32[8,1,17536]{2,1,0:T(1,128)S(1)} %bitcast.44), channel_id=1, replica_groups={{48,0,24,16,32,56,8,40},{49,1,25,17,33,57,9,41},{50,2,26,18,34,58,10,42..., dimensions={0} | all-to-all | bytes 1122304 | tf_op jit(solution)/shard_map/all_to_all | solution.py:397
  118.9 1.4 %shard_map.83 = (bf16[1120,128]{1,0:T(8,128)(2,1)}, bf16[1120,128]{1,0:T(8,128)(2,1)}, bf16[1120,128]{1,0:T(8,128)(2,1)}, bf16[1120,128]{1,0:T(8,128)(2,1)}) custom-call(f32[1096,128]{1,0:T(8,128)S(1)} %bitcast.45, bf16[1120,128]{1,0:T(8,128)(2,1)S(1)} %get-tuple-element.32.k_ref, bf16[1120,128]{1,0:T(8,128)(2,1)S(1)} %get-tuple-element.33.v_ref, ...), custom_call_target="tpu_custom_call" | custom-call | flops 10000000 | bytes 1000000 | tf_op jit(solution)/shard_map/pallas_call | solution.py:468
  (5 shorter events, 0.2 us)

commit v11 on v10

--- a/solution.py
+++ b/solution.py
@@ -345,8 +345,8 @@
     heads, pieces = channels // HEAD_DIM, len(CHIP)
     ends = [HEAD_DIM * h for h in (heads // 2, heads - heads // 5, heads)]
     moves = [(attn_ref, mixed_out, 0, channels), (gq_ref, gq_out, 0, channels)]
-    for begin, end in zip([0, *ends], ends):
-        moves += [(gk_ref, gk_out, begin, end), (gv_ref, gv_out, begin, end)]
+    for a, b in ((gv_ref, gv_out), (gk_ref, gk_out)):
+        moves += [(a, b, begin, end) for begin, end in zip([0, *ends], ends)]
     copies = [
         pltpu.make_async_copy(a.at[begin:end, :], b.at[begin:end, :], sems.at[n])
         for n, (a, b, begin, end) in enumerate(moves)
@@ -356,22 +356,23 @@
     height, count = in_ref.shape[0] // pieces, len(tiles(channels))
     total = total_of(cut_rows(in_ref, height, s, height - count, count) for s in range(pieces))
     for t in tiles(channels):
+        keep_halves(t, slabs.get(in_ref, t), flat_hi_ref, flat_lo_ref)
+    for h in range(heads):
+        gv_ref[of_head(h), :] = by_state(flat_hi_ref, flat_lo_ref, k_ref, h).astype(BF16)
+        if HEAD_DIM * (h + 1) in ends:
+            copies[2 + ends.index(HEAD_DIM * (h + 1))].start()
+    for t in tiles(channels):
         shape = (LANES - HEAD_DIM, t.width)
         extra = jnp.where(row(shape) < 1, jnp.broadcast_to(total[t.j : t.j + 1, : t.width], shape), 0.0)
-        state = slabs.get(in_ref, t)
-        keep_halves(t, state, flat_hi_ref, flat_lo_ref)
-        turn(t, state, extra, hi_ref, lo_ref)
+        turn(t, slabs.get(in_ref, t), extra, hi_ref, lo_ref)
     ones = jnp.ones((LANES - HEAD_DIM, rows), BF16)
     for h in range(heads):
-        gv_ref[of_head(h), :] = by_state(flat_hi_ref, flat_lo_ref, k_ref, h).astype(BF16)
         rhs = with_rows(v_ref[of_head(h), :], ones)
         grad = both_halves(dot, hi_ref[of_head(h), :], lo_ref[of_head(h), :], rhs)
         k = k_ref[of_head(h), :].astype(F32)
         gk_ref[of_head(h), :] = jnp.where(k > 0, grad, 0.0).astype(BF16)
         if HEAD_DIM * (h + 1) in ends:
-            n = 2 + 2 * ends.index(HEAD_DIM * (h + 1))
-            copies[n].start()
-            copies[n + 1].start()
+            copies[5 + ends.index(HEAD_DIM * (h + 1))].start()
     for copy in copies:
         copy.wait()
 

time: 121 us -> 121 us (level)
  no operation moved by 1% of the time
where the time goes in v11:
time: 121 us; the launch traced here: 120 us
  blocking collectives  115 us (95%)
  Pallas kernels  4.63 us (4%)
    all_to_all x8, blocking collectives, exchanged(): lax.all_to_all(pieces, axes, 0, 0, tiled=True, axis_index_groups=[order])  115 us

profile of v11, /device:TPU:1, one launch (start us, length us, event | category | flops | bytes accessed | tf_op | source)
XLA Modules:
  0.0 120.2 jit_solution(14354157147270876846)
XLA Ops:
  0.6 1.6 %shard_map.75 = (f32[1096,128]{1,0:T(8,128)S(1)}, bf16[1120,128]{1,0:T(8,128)(2,1)S(1)}, bf16[1120,128]{1,0:T(8,128)(2,1)S(1)}, bf16[1120,128]{1,0:T(8,128)(2,1)S(1)}, bf16[1120,128]{1,0:T(8,128)(2,1)S(1)}) custom-call(bf16[1120,128]{1,0:T(8,128)(2,1)} %bitcast.56, bf16[1120,128]{1,0:T(8,128)(2,1)} %bitcast.57, bf16[1120,128]{1,0:T(8,128)(2,1)} %bitcast.58, ...), custom_call_target="tpu_custom_call" | custom-call | flops 10000000 | bytes 1000000 | tf_op jit(solution)/shard_map/pallas_call | solution.py:439
  2.3 18.5 %all_to_all.72 = f32[8,1,17536]{2,1,0:T(1,128)S(1)} all-to-all(f32[8,1,17536]{2,1,0:T(1,128)S(1)} %bitcast.51), channel_id=1, replica_groups={{48,0,24,16,32,56,8,40},{49,1,25,17,33,57,9,41},{50,2,26,18,34,58,10,42..., dimensions={0} | all-to-all | bytes 1122304 | tf_op jit(solution)/shard_map/all_to_all | solution.py:398
  20.8 9.3 %all_to_all.73 = f32[8,1,6400]{2,1,0:T(1,128)S(1)} all-to-all(f32[8,1,6400]{2,1,0:T(1,128)S(1)} %bitcast.47), channel_id=1, replica_groups={{0,4,2,6,1,5,3,7},{8,12,10,14,9,13,11,15},{16,20,18,22,17,21,19,23},{24..., dimensions={0} | all-to-all | bytes 409600 | tf_op jit(solution)/shard_map/all_to_all | solution.py:398
  30.2 16.0 %all_to_all.74 = f32[8,1,3200]{2,1,0:T(1,128)S(1)} all-to-all(f32[8,1,3200]{2,1,0:T(1,128)S(1)} %bitcast.55), channel_id=1, replica_groups={{0,256,64,320,128,384,192,448},{1,257,65,321,129,385,193,449},{2,258,66..., dimensions={0} | all-to-all | bytes 204800 | tf_op jit(solution)/shard_map/all_to_all | solution.py:398
  46.2 0.7 shard_map.78
  46.8 19.6 %all_to_all.75 = f32[8,1,20480]{2,1,0:T(1,128)S(1)} all-to-all(f32[8,1,20480]{2,1,0:T(1,128)S(1)} %bitcast.50), channel_id=1, replica_groups={{0,4,1,5,2,6,3,7},{8,12,9,13,10,14,11,15},{16,20,17,21,18,22,19,23},{24..., dimensions={0} | all-to-all | bytes 1310720 | tf_op jit(solution)/shard_map/all_to_all | solution.py:398
  66.5 17.0 %all_to_all.76 = f32[8,1,18432]{2,1,0:T(1,128)S(1)} all-to-all(f32[8,1,18432]{2,1,0:T(1,128)S(1)} %bitcast.42), channel_id=1, replica_groups={{48,0,24,16,32,56,8,40},{49,1,25,17,33,57,9,41},{50,2,26,18,34,58,10,42..., dimensions={0} | all-to-all | bytes 1179648 | tf_op jit(solution)/shard_map/all_to_all | solution.py:398
  83.6 0.9 shard_map.80
  84.5 9.1 %all_to_all.77 = f32[8,1,3200]{2,1,0:T(1,128)S(1)} all-to-all(f32[8,1,3200]{2,1,0:T(1,128)S(1)} %bitcast.54), channel_id=1, replica_groups={{0,256,64,320,128,384,192,448},{1,257,65,321,129,385,193,449},{2,258,66..., dimensions={0} | all-to-all | bytes 204800 | tf_op jit(solution)/shard_map/all_to_all | solution.py:398
  93.6 10.2 %all_to_all.78 = f32[8,1,6400]{2,1,0:T(1,128)S(1)} all-to-all(f32[8,1,6400]{2,1,0:T(1,128)S(1)} %bitcast.49), channel_id=1, replica_groups={{0,4,2,6,1,5,3,7},{8,12,10,14,9,13,11,15},{16,20,18,22,17,21,19,23},{24..., dimensions={0} | all-to-all | bytes 409600 | tf_op jit(solution)/shard_map/all_to_all | solution.py:398
  103.9 15.1 %all_to_all.79 = f32[8,1,17536]{2,1,0:T(1,128)S(1)} all-to-all(f32[8,1,17536]{2,1,0:T(1,128)S(1)} %bitcast.44), channel_id=1, replica_groups={{48,0,24,16,32,56,8,40},{49,1,25,17,33,57,9,41},{50,2,26,18,34,58,10,42..., dimensions={0} | all-to-all | bytes 1122304 | tf_op jit(solution)/shard_map/all_to_all | solution.py:398
  118.9 1.3 %shard_map.83 = (bf16[1120,128]{1,0:T(8,128)(2,1)}, bf16[1120,128]{1,0:T(8,128)(2,1)}, bf16[1120,128]{1,0:T(8,128)(2,1)}, bf16[1120,128]{1,0:T(8,128)(2,1)}) custom-call(f32[1096,128]{1,0:T(8,128)S(1)} %bitcast.45, bf16[1120,128]{1,0:T(8,128)(2,1)S(1)} %get-tuple-element.32.k_ref, bf16[1120,128]{1,0:T(8,128)(2,1)S(1)} %get-tuple-element.33.v_ref, ...), custom_call_target="tpu_custom_call" | custom-call | flops 10000000 | bytes 1000000 | tf_op jit(solution)/shard_map/pallas_call | solution.py:469
  (5 shorter events, 0.2 us)
